TPU v7x, 256 devices: a whole 4x4x8 slice. The times are simulated.
256 devices in a mesh: dp: 16 (over z, core), seq: 16 (over x, y).
Axes of the slice: x: 4, y: 4, z: 8, core: 2. Of those that a mesh axis runs over, the one named last changes fastest.
Arguments:
- queries: bfloat16 [16, 2048, 4096], P('dp', 'seq'), may hold values from -6 to 6
- keys: bfloat16 [16, 2048, 4096], P('dp', 'seq'), may hold values from -6 to 6
- values: bfloat16 [16, 2048, 4096], P('dp', 'seq'), may hold values from -6 to 6
- cotangent: bfloat16 [16, 2048, 4096], P('dp', 'seq'), may hold values from -6 to 6
- query_gain: float32 [32, 128], replicated, may hold values from 0.1 to 1.9
- key_gain: float32 [32, 128], replicated, may hold values from 0.1 to 1.9
- block_ids: int32 [32, 8], replicated, may hold values from -1 to 31, as said below
Outputs:
- out: bfloat16 [16, 2048, 4096], P('dp', 'seq')
- query_grad: bfloat16 [16, 2048, 4096], P('dp', 'seq')
- key_grad: bfloat16 [16, 2048, 4096], P('dp', 'seq')
- value_grad: bfloat16 [16, 2048, 4096], P('dp', 'seq')
- query_gain_grad: float32 [32, 128], replicated
- key_gain_grad: float32 [32, 128], replicated
Inputs may be any that keep to these rules, and one draw needn't show every extreme that they name: `block_ids`: every row block r lists block r, block 0 and block 31, two window slots for blocks r - 1 and r + 1 (set to -1 where such a block is missing or is block 0 or 31), and three further blocks; no block is listed twice in a row.
All inputs are finite; a program needn't handle non-finite values.
Results may differ from a plain program's by a relative error of at most 0.011.
Values may be sent and summed in bfloat16 or wider, within the bound.
No kernel may reach another device: no remote copies, remote signals or barrier semaphores. Data moves between devices by JAX's collectives and lax.ppermute only.
A program may use at most 128 MiB of HBM per device.

v0:
```python
import functools

import jax
import jax.numpy as jnp
from jax import lax
from jax.experimental import pallas as pl
from jax.experimental.pallas import tpu as pltpu
from jax.sharding import PartitionSpec as P

HEADS = 32
HEAD = 128
BLOCK = 64
NB = 32
SLOTS = 8
SEQ = 16
CHUNKS = 2
TOK = 128
TOKENS = 2048
EPSILON = 1e-06
SCALE = HEAD**-0.5
LOG2E = 1.4426950408889634
EXTRA = 16
ROWS_OUT = 4 * TOK + EXTRA


def head_columns(chunk, s):
    return pl.ds(pl.multiple_of((chunk * SEQ + s) * HEAD, HEAD), HEAD)


def pack_kernel(chunk, q_ref, k_ref, v_ref, g_ref, send_ref, sem):
    @pl.loop(0, SEQ)
    def _(s):
        for a, ref in enumerate((q_ref, k_ref, v_ref, g_ref)):
            pltpu.make_async_copy(
                ref.at[0, :, head_columns(chunk, s)],
                send_ref.at[s, pl.ds(a * TOK, TOK), :],
                sem,
            ).start()

    pltpu.make_async_copy(send_ref, send_ref, sem).wait()


def pack(chunk, arrays):
    return pl.pallas_call(
        functools.partial(pack_kernel, chunk),
        out_shape=jax.ShapeDtypeStruct((SEQ, 4 * TOK, HEAD), jnp.bfloat16),
        in_specs=[pl.BlockSpec(memory_space=pl.ANY)] * 4,
        out_specs=pl.BlockSpec(memory_space=pl.ANY),
        scratch_shapes=[pltpu.SemaphoreType.DMA],
        cost_estimate=pl.CostEstimate(flops=0, bytes_accessed=4 << 20, transcendentals=0),
        name=f"pack{chunk}",
    )(*arrays)


def unpack_kernel(chunk, recv_ref, *refs):
    outs, sem = refs[-5:-1], refs[-1]

    @pl.loop(0, SEQ)
    def _(s):
        for a, ref in enumerate(outs):
            pltpu.make_async_copy(
                recv_ref.at[s, pl.ds(a * TOK, TOK), :],
                ref.at[0, :, head_columns(chunk, s)],
                sem,
            ).start()

    for ref in outs:
        half = ref.at[0, :, pl.ds(chunk * SEQ * HEAD, SEQ * HEAD)]
        pltpu.make_async_copy(half, half, sem).wait()


def unpack(chunk, recv, before):
    return pl.pallas_call(
        functools.partial(unpack_kernel, chunk),
        out_shape=(jax.ShapeDtypeStruct((1, TOK, HEADS * HEAD), jnp.bfloat16),) * 4,
        in_specs=[pl.BlockSpec(memory_space=pl.ANY)] * (1 + len(before)),
        out_specs=(pl.BlockSpec(memory_space=pl.ANY),) * 4,
        input_output_aliases={i + 1: i for i in range(len(before))},
        scratch_shapes=[pltpu.SemaphoreType.DMA],
        cost_estimate=pl.CostEstimate(flops=0, bytes_accessed=4 << 20, transcendentals=0),
        name=f"unpack{chunk}",
    )(recv, *before)


def dot(a, b, ca, cb):
    return lax.dot_general(
        a, b, (((ca,), (cb,)), ((), ())), preferred_element_type=jnp.float32
    )


def inverse_norm(x):
    return lax.rsqrt(jnp.mean(x * x, axis=-1, keepdims=True) + EPSILON)


def norm_backward(x, inverse, gain, grad):
    unit = x * inverse
    pulled = grad * gain
    along = jnp.mean(pulled * unit, axis=-1, keepdims=True)
    return inverse * (pulled - unit * along), grad * unit


def attend_kernel(ids_ref, gains_ref, recv_ref, back_ref, gain_ref, kn_ref, dk_ref, dv_ref, *, group):
    query_gain = gains_ref[0:1, :]
    key_gain = gains_ref[1:2, :]

    @pl.loop(0, SEQ)
    def _(s):
        x = recv_ref[s, TOK : 2 * TOK, :].astype(jnp.float32)
        rows = pl.ds(pl.multiple_of(s * TOK, TOK), TOK)
        kn_ref[rows, :] = (x * inverse_norm(x) * key_gain).astype(jnp.bfloat16)
        dk_ref[rows, :] = jnp.zeros((TOK, HEAD), jnp.float32)
        dv_ref[rows, :] = jnp.zeros((TOK, HEAD), jnp.float32)

    slot_of = lax.broadcasted_iota(jnp.int32, (1, SLOTS * BLOCK), 1) // BLOCK

    def one_row_block(r):
        src, at = r // 2, pl.multiple_of((r % 2) * BLOCK, BLOCK)
        places, tokens, valid = [], [], jnp.int32(0)
        for j in range(SLOTS):
            block = ids_ref[r, j]
            valid = valid | jnp.where(block >= 0, 1 << j, 0)
            block = jnp.maximum(block, 0)
            places.append(pl.ds(pl.multiple_of(block * BLOCK, BLOCK), BLOCK))
            tokens.append((block // 2, pl.multiple_of((block % 2) * BLOCK, BLOCK)))
        bias = jnp.where(((valid >> slot_of) & 1) == 1, 0.0, -1e30)
        x = recv_ref[src, pl.ds(at, BLOCK), :].astype(jnp.float32)
        inverse = inverse_norm(x)
        qn = (x * inverse * query_gain).astype(jnp.bfloat16)
        grad = recv_ref[src, pl.ds(3 * TOK + at, BLOCK), :]
        keys = jnp.concatenate([kn_ref[p, :] for p in places], axis=0)
        values = jnp.concatenate(
            [recv_ref[s, pl.ds(2 * TOK + o, BLOCK), :] for s, o in tokens], axis=0
        )
        scores = dot(qn, keys, 1, 1)
        raised = jnp.exp2(scores * (SCALE * LOG2E) + bias)
        probs = raised / jnp.sum(raised, axis=-1, keepdims=True)
        weights = probs.astype(jnp.bfloat16)
        out = dot(weights, values, 1, 0).astype(jnp.bfloat16)
        delta = jnp.sum(grad.astype(jnp.float32) * out.astype(jnp.float32), axis=-1, keepdims=True)
        grad_probs = dot(grad, values, 1, 1)
        grad_scores = (probs * (grad_probs - delta) * SCALE).astype(jnp.bfloat16)
        grad_qn = dot(grad_scores, keys, 1, 0).astype(jnp.bfloat16).astype(jnp.float32)
        query_grad, gain_term = norm_backward(x, inverse, query_gain, grad_qn)
        back_ref[src, pl.ds(at, BLOCK), :] = out
        back_ref[src, pl.ds(TOK + at, BLOCK), :] = query_grad.astype(jnp.bfloat16)
        key_terms = dot(grad_scores, qn, 0, 0)
        value_terms = dot(weights, grad, 0, 0)
        return places, key_terms, value_terms, gain_term.reshape(BLOCK // 8, 8, HEAD).sum(0)

    def several(i, total):
        done = [one_row_block(i * group + n) for n in range(group)]
        for places, key_terms, value_terms, gain_term in done:
            total = total + gain_term
            for j, p in enumerate(places):
                part = slice(j * BLOCK, (j + 1) * BLOCK)
                dk_ref[p, :] += key_terms[part]
                dv_ref[p, :] += value_terms[part]
        return total

    query_total = lax.fori_loop(0, NB // group, several, jnp.zeros((8, HEAD), jnp.float32))

    def finish(s, total):
        rows = pl.ds(pl.multiple_of(s * TOK, TOK), TOK)
        x = recv_ref[s, TOK : 2 * TOK, :].astype(jnp.float32)
        grad_kn = dk_ref[rows, :].astype(jnp.bfloat16).astype(jnp.float32)
        key_grad, gain_term = norm_backward(x, inverse_norm(x), key_gain, grad_kn)
        back_ref[s, 2 * TOK : 3 * TOK, :] = key_grad.astype(jnp.bfloat16)
        back_ref[s, 3 * TOK : 4 * TOK, :] = dv_ref[rows, :].astype(jnp.bfloat16)
        return total + gain_term.reshape(TOK // 8, 8, HEAD).sum(0)

    key_total = lax.fori_loop(0, SEQ, finish, jnp.zeros((8, HEAD), jnp.float32))
    gain_ref[0:1, :] = jnp.sum(query_total, axis=0, keepdims=True)
    gain_ref[1:2, :] = jnp.sum(key_total, axis=0, keepdims=True)


def attend(chunk, ids, gains, recv, group=2):
    return pl.pallas_call(
        functools.partial(attend_kernel, group=group),
        out_shape=(
            jax.ShapeDtypeStruct((SEQ, 4 * TOK, HEAD), jnp.bfloat16),
            jax.ShapeDtypeStruct((2, HEAD), jnp.float32),
        ),
        in_specs=[
            pl.BlockSpec(memory_space=pltpu.SMEM),
            pl.BlockSpec(memory_space=pltpu.VMEM),
            pl.BlockSpec(memory_space=pltpu.VMEM),
        ],
        out_specs=(
            pl.BlockSpec(memory_space=pltpu.VMEM),
            pl.BlockSpec(memory_space=pltpu.VMEM),
        ),
        scratch_shapes=[
            pltpu.VMEM((TOKENS, HEAD), jnp.bfloat16),
            pltpu.VMEM((TOKENS, HEAD), jnp.float32),
            pltpu.VMEM((TOKENS, HEAD), jnp.float32),
        ],
        compiler_params=pltpu.CompilerParams(vmem_limit_bytes=32 << 20),
        cost_estimate=pl.CostEstimate(
            flops=12 * 2 * NB * BLOCK * SLOTS * BLOCK * HEAD,
            bytes_accessed=4 << 20,
            transcendentals=NB * BLOCK * SLOTS * BLOCK,
        ),
        name=f"attend{chunk}",
    )(ids, gains, recv)


def swap(x, axis):
    return lax.all_to_all(x, axis, split_axis=0, concat_axis=0, tiled=True)


def on_device(queries, keys, values, cotangent, query_gain, key_gain, block_ids):
    arrays = (queries, keys, values, cotangent)
    s = lax.axis_index("seq")
    both = jnp.stack([query_gain, key_gain], axis=1)
    gains = [
        lax.dynamic_index_in_dim(both, c * SEQ + s, 0, keepdims=False) for c in range(CHUNKS)
    ]
    sent0 = pack(0, arrays)
    in0 = swap(sent0, "seq")
    sent1, in0 = lax.optimization_barrier((pack(1, arrays), in0))
    in1 = swap(sent1, "seq")
    back0, gain0 = attend(0, block_ids, gains[0], in0)
    back0, in1 = lax.optimization_barrier((back0, in1))
    out0 = swap(back0, "seq")
    back1, gain1 = attend(1, block_ids, gains[1], in1)
    back1, out0 = lax.optimization_barrier((back1, out0))
    out1 = swap(back1, "seq")
    done = unpack(0, out0, ())
    done = unpack(1, out1, tuple(done))
    part = jnp.stack([gain0, gain1])
    part = jnp.sum(swap(jnp.broadcast_to(part[None], (SEQ, 2, 2, HEAD)), "dp"), axis=0)
    every = swap(jnp.broadcast_to(part[None], (SEQ, 2, 2, HEAD)), "seq")
    factor = (TOKENS * lax.axis_size("dp")) ** -0.5
    every = jnp.transpose(every, (2, 1, 0, 3)).reshape(2, HEADS, HEAD) * factor
    return (*done, every[0], every[1])


def solution(mesh):
    rows = P("dp", "seq", None)
    return jax.shard_map(
        on_device,
        mesh=mesh,
        in_specs=(rows, rows, rows, rows, P(), P(), P()),
        out_specs=(rows, rows, rows, rows, P(), P()),
        check_vma=False,
    )
```

profile of v0, /device:TPU:128, one launch (start us, length us, event | category | flops | bytes accessed | tf_op | source)
XLA Modules:
  0.0 398.1 jit_solution(4496713016774359458)
XLA Ops:
  0.6 64.6 %pack0.1 = bf16[16,512,128]{2,1,0:T(8,128)(2,1)} custom-call(bf16[1,128,4096]{2,1,0:T(8,128)(2,1)} %q_ref.3, bf16[1,128,4096]{2,1,0:T(8,128)(2,1)} %k_ref.3, bf16[1,128,4096]{2,1,0:T(8,128)(2,1)} %v_ref.3, bf16[1,128,4096]{2,1,0:T(8,128)(2,1)} %g_ref.3), custom_call_target="tpu_custom_call" | custom-call | bytes 4194304 | tf_op jit(solution)/shard_map/pack0/pallas_call | solution.py:44
  65.3 7.0 %all-to-all-start = ((bf16[16,512,128]{2,1,0:T(8,128)(2,1)}), bf16[16,512,128]{2,1,0:T(8,128)(2,1)S(1)}, u32[]{:S(2)}, u32[]{:S(2)}) async-start(bf16[16,512,128]{2,1,0:T(8,128)(2,1)} %pack0.1), calls=%async_computation | async-start | bytes 4194304 | tf_op jit(solution)/shard_map/all_to_all | solution.py:208
  72.3 64.6 %pack1.1 = bf16[16,512,128]{2,1,0:T(8,128)(2,1)} custom-call(bf16[1,128,4096]{2,1,0:T(8,128)(2,1)} %q_ref.3, bf16[1,128,4096]{2,1,0:T(8,128)(2,1)} %k_ref.3, bf16[1,128,4096]{2,1,0:T(8,128)(2,1)} %v_ref.3, bf16[1,128,4096]{2,1,0:T(8,128)(2,1)} %g_ref.3), custom_call_target="tpu_custom_call" | custom-call | bytes 4194304 | tf_op jit(solution)/shard_map/pack1/pallas_call | solution.py:44
  137.0 0.0 copy-start.4
  137.0 0.0 copy-start.2
  137.0 0.0 copy-start.3
  137.0 0.0 all-to-all-done.recv_ref
  137.0 7.3 %all-to-all-start.1 = ((bf16[16,512,128]{2,1,0:T(8,128)(2,1)}), bf16[16,512,128]{2,1,0:T(8,128)(2,1)}, u32[]{:S(2)}, u32[]{:S(2)}) async-start(bf16[16,512,128]{2,1,0:T(8,128)(2,1)} %pack1.1), calls=%async_computation.1 | async-start | bytes 4194304 | tf_op jit(solution)/shard_map/all_to_all | solution.py:208
  144.3 0.0 copy-done.4
  144.3 0.1 copy.29.ids_ref
  144.4 0.0 copy-done.2
  144.4 0.0 copy-done.3
  144.4 29.0 %attend0.1 = (bf16[16,512,128]{2,1,0:T(8,128)(2,1)}, f32[2,128]{1,0:T(2,128)S(1)}) custom-call(s32[32,8]{1,0:T(8,128)S(1)} %copy.29.ids_ref, f32[2,128]{1,0:T(2,128)S(1)} %bitcast.11, bf16[16,512,128]{2,1,0:T(8,128)(2,1)S(1)} %all-to-all-done.recv_ref), custom_call_target="tpu_custom_call" | custom-call | flops 3221225472 | bytes 4194304 | tf_op jit(solution)/shard_map/attend0/pallas_call | solution.py:177
  173.5 0.1 all-to-all-done.1.recv_ref
  173.6 29.8 %attend1.1 = (bf16[16,512,128]{2,1,0:T(8,128)(2,1)}, f32[2,128]{1,0:T(2,128)S(1)}) custom-call(s32[32,8]{1,0:T(8,128)S(1)} %copy.29.ids_ref, f32[2,128]{1,0:T(2,128)S(1)} %bitcast.10, bf16[16,512,128]{2,1,0:T(8,128)(2,1)} %all-to-all-done.1.recv_ref), custom_call_target="tpu_custom_call" | custom-call | flops 3221225472 | bytes 4194304 | tf_op jit(solution)/shard_map/attend1/pallas_call | solution.py:177
  203.4 9.6 %all_to_all.30 = f32[16,2,2,128]{3,2,1,0:T(2,128)S(1)} all-to-all(f32[16,2,2,128]{3,2,1,0:T(2,128)S(1)} %broadcast_in_dim.4), channel_id=1, replica_groups=mesh['dp'=16,'seq'=16] {'dp'}, dimensions={0} | all-to-all | bytes 65536 | tf_op jit(solution)/shard_map/all_to_all | solution.py:208
  213.1 7.0 %all-to-all-start.2 = ((bf16[16,512,128]{2,1,0:T(8,128)(2,1)}), bf16[16,512,128]{2,1,0:T(8,128)(2,1)S(1)}, u32[]{:S(2)}, u32[]{:S(2)}) async-start(bf16[16,512,128]{2,1,0:T(8,128)(2,1)} %get-tuple-element.29), calls=%async_computation.2 | async-start | bytes 4194304 | tf_op jit(solution)/shard_map/all_to_all | solution.py:208
  220.1 31.1 %all-to-all-done.2.recv_ref = bf16[16,512,128]{2,1,0:T(8,128)(2,1)S(1)} async-done(((bf16[16,512,128]{2,1,0:T(8,128)(2,1)}), bf16[16,512,128]{2,1,0:T(8,128)(2,1)S(1)}, u32[]{:S(2)}, u32[]{:S(2)}) %all-to-all-start.2) | async-done | bytes 2097184 | tf_op jit(solution)/shard_map/all_to_all | solution.py:208
  251.2 0.0 copy-start.1
  251.2 0.7 broadcast_in_dim.5
  251.9 3.6 all-to-all-start.5
  255.5 7.6 %all-to-all-done.5 = f32[16,2,2,128]{3,1,2,0:T(2,128)S(1)} async-done(((f32[16,2,2,128]{3,1,2,0:T(2,128)}), f32[16,2,2,128]{3,1,2,0:T(2,128)S(1)}, u32[]{:S(2)}, u32[]{:S(2)}) %all-to-all-start.5) | async-done | bytes 32800 | tf_op jit(solution)/shard_map/all_to_all | solution.py:208
  263.1 0.0 copy-done.1
  263.1 3.7 all-to-all-start.3
  266.8 0.6 fusion.3
  267.4 64.6 %unpack0.1 = (bf16[1,128,4096]{2,1,0:T(8,128)(2,1)}, bf16[1,128,4096]{2,1,0:T(8,128)(2,1)}, bf16[1,128,4096]{2,1,0:T(8,128)(2,1)}, bf16[1,128,4096]{2,1,0:T(8,128)(2,1)}) custom-call(bf16[16,512,128]{2,1,0:T(8,128)(2,1)} %copy-done.1), custom_call_target="tpu_custom_call" | custom-call | bytes 4194304 | tf_op jit(solution)/shard_map/unpack0/pallas_call | solution.py:73
  332.1 0.0 all-to-all-done.3.recv_ref
  332.1 0.0 copy-start
  332.1 1.3 copy-done
  333.4 64.6 %unpack1.1 = (bf16[1,128,4096]{2,1,0:T(8,128)(2,1)}, bf16[1,128,4096]{2,1,0:T(8,128)(2,1)}, bf16[1,128,4096]{2,1,0:T(8,128)(2,1)}, bf16[1,128,4096]{2,1,0:T(8,128)(2,1)}) custom-call(bf16[16,512,128]{2,1,0:T(8,128)(2,1)} %copy-done, ...), custom_call_target="tpu_custom_call", output_to_operand_aliasing={{0}: (1, {}), {1}: (2, {}), {2}: (3, {}), {3}: (4, {})} | custom-call | bytes 4194304 | tf_op jit(solution)/shard_map/unpack1/pallas_call | solution.py:73
  (6 shorter events, 0.1 us)
Async XLA Ops:
  65.3 71.7 %all-to-all-start = ((bf16[16,512,128]{2,1,0:T(8,128)(2,1)}), bf16[16,512,128]{2,1,0:T(8,128)(2,1)S(1)}, u32[]{:S(2)}, u32[]{:S(2)}) async-start(bf16[16,512,128]{2,1,0:T(8,128)(2,1)} %pack0.1), calls=%async_computation | async-start | bytes 4194304 | tf_op jit(solution)/shard_map/all_to_all | solution.py:208
  137.0 7.3 %copy-start.4 = (s32[32,8]{0,1:T(8,128)S(1)}, s32[32,8]{0,1:T(8,128)}, u32[]{:S(2)}) copy-start(s32[32,8]{0,1:T(8,128)} %param.13) | copy-start | bytes 3076
  137.0 7.4 %copy-start.2 = (f32[32,128]{1,0:T(8,128)S(1)}, f32[32,128]{1,0:T(8,128)}, u32[]{:S(2)}) copy-start(f32[32,128]{1,0:T(8,128)} %param.11) | copy-start | bytes 49156
  137.0 7.4 %copy-start.3 = (f32[32,128]{1,0:T(8,128)S(1)}, f32[32,128]{1,0:T(8,128)}, u32[]{:S(2)}) copy-start(f32[32,128]{1,0:T(8,128)} %param.12) | copy-start | bytes 49156
  137.0 36.6 %all-to-all-start.1 = ((bf16[16,512,128]{2,1,0:T(8,128)(2,1)}), bf16[16,512,128]{2,1,0:T(8,128)(2,1)}, u32[]{:S(2)}, u32[]{:S(2)}) async-start(bf16[16,512,128]{2,1,0:T(8,128)(2,1)} %pack1.1), calls=%async_computation.1 | async-start | bytes 4194304 | tf_op jit(solution)/shard_map/all_to_all | solution.py:208
  213.1 38.1 %all-to-all-start.2 = ((bf16[16,512,128]{2,1,0:T(8,128)(2,1)}), bf16[16,512,128]{2,1,0:T(8,128)(2,1)S(1)}, u32[]{:S(2)}, u32[]{:S(2)}) async-start(bf16[16,512,128]{2,1,0:T(8,128)(2,1)} %get-tuple-element.29), calls=%async_computation.2 | async-start | bytes 4194304 | tf_op jit(solution)/shard_map/all_to_all | solution.py:208
  251.2 11.9 %copy-start.1 = (bf16[16,512,128]{2,1,0:T(8,128)(2,1)}, bf16[16,512,128]{2,1,0:T(8,128)(2,1)S(1)}, u32[]{:S(2)}) copy-start(bf16[16,512,128]{2,1,0:T(8,128)(2,1)S(1)} %all-to-all-done.2.recv_ref) | copy-start | bytes 6291460
  251.9 11.2 %all-to-all-start.5 = ((f32[16,2,2,128]{3,1,2,0:T(2,128)}), f32[16,2,2,128]{3,1,2,0:T(2,128)S(1)}, u32[]{:S(2)}, u32[]{:S(2)}) async-start(f32[16,2,2,128]{3,1,2,0:T(2,128)} %broadcast_in_dim.5), calls=%async_computation.5 | async-start | bytes 65536 | tf_op jit(solution)/shard_map/all_to_all | solution.py:208
  263.1 69.0 %all-to-all-start.3 = ((bf16[16,512,128]{2,1,0:T(8,128)(2,1)}), bf16[16,512,128]{2,1,0:T(8,128)(2,1)S(1)}, u32[]{:S(2)}, u32[]{:S(2)}) async-start(bf16[16,512,128]{2,1,0:T(8,128)(2,1)} %get-tuple-element.30), calls=%async_computation.3 | async-start | bytes 4194304 | tf_op jit(solution)/shard_map/all_to_all | solution.py:208
  332.1 1.3 copy-start
where the time goes:
time: 405 us; the launch traced here: 398 us
  Pallas kernels  317 us (78%)
  waiting for transfers between devices  38.8 us (10%)
  starting transfers between devices  28.7 us (7%)
  blocking collectives  9.63 us (2%)
    pallas_call x2, Pallas kernels, pack(): pl.pallas_call(functools.partial(pack_kernel, chunk), out_shape=jax.Shape...  129 us
    pallas_call x2, Pallas kernels, unpack(): pl.pallas_call(functools.partial(unpack_kernel, chunk), out_shape=(jax.Sh...  129 us
    pallas_call x2, Pallas kernels, attend(): pl.pallas_call(functools.partial(attend_kernel, group=group), out_shape=(...  58.8 us
    all_to_all x5, waiting for transfers between devices, swap(): return lax.all_to_all(x, axis, split_axis=0, concat_axis=0, tiled=True)  38.8 us
    all_to_all x5, starting transfers between devices, swap(): return lax.all_to_all(x, axis, split_axis=0, concat_axis=0, tiled=True)  28.7 us
    all_to_all x1, blocking collectives, swap(): return lax.all_to_all(x, axis, split_axis=0, concat_axis=0, tiled=True)  9.63 us
  transfers between devices with their start and end apart: 5, of which 3 were waited for; matrix products, arithmetic and copies ran while one was open for 0% of the time, Pallas kernels for 40%

commit v1 on v0

v1 whole, which is shorter than its diff:
```python
import functools

import jax
import jax.numpy as jnp
from jax import lax
from jax.experimental import pallas as pl
from jax.experimental.pallas import tpu as pltpu
from jax.sharding import PartitionSpec as P

HEADS = 32
HEAD = 128
BLOCK = 64
NB = 32
SLOTS = 8
SEQ = 16
CHUNKS = 2
TOK = 128
TOKENS = 2048
EPSILON = 1e-06
SCALE = HEAD**-0.5
LOG2E = 1.4426950408889634
AT_ONCE = 8


def pack_kernel(q_ref, k_ref, v_ref, g_ref, send_ref):
    for a, ref in enumerate((q_ref, k_ref, v_ref, g_ref)):
        for n in range(AT_ONCE):
            send_ref[n, a * TOK : (a + 1) * TOK, :] = ref[0, :, n * HEAD : (n + 1) * HEAD]


def pack(chunk, arrays):
    steps = SEQ // AT_ONCE
    return pl.pallas_call(
        pack_kernel,
        grid=(steps,),
        out_shape=jax.ShapeDtypeStruct((SEQ, 4 * TOK, HEAD), jnp.bfloat16),
        in_specs=[pl.BlockSpec((1, TOK, AT_ONCE * HEAD), lambda i: (0, 0, chunk * steps + i))] * 4,
        out_specs=pl.BlockSpec((AT_ONCE, 4 * TOK, HEAD), lambda i: (i, 0, 0)),
        cost_estimate=pl.CostEstimate(flops=0, bytes_accessed=8 << 20, transcendentals=0),
        name=f"pack{chunk}",
    )(*arrays)


def unpack_kernel(recv_ref, *refs):
    first = pl.program_id(0) * AT_ONCE
    for a, ref in enumerate(refs[-4:]):
        for n in range(AT_ONCE):
            ref[0, :, n * HEAD : (n + 1) * HEAD] = recv_ref[first + n, a * TOK : (a + 1) * TOK, :]


def unpack(chunk, recv, before):
    steps = SEQ // AT_ONCE
    return pl.pallas_call(
        unpack_kernel,
        grid=(steps,),
        out_shape=(jax.ShapeDtypeStruct((1, TOK, HEADS * HEAD), jnp.bfloat16),) * 4,
        in_specs=[pl.BlockSpec(memory_space=pltpu.VMEM)]
        + [pl.BlockSpec(memory_space=pl.ANY)] * len(before),
        out_specs=(pl.BlockSpec((1, TOK, AT_ONCE * HEAD), lambda i: (0, 0, chunk * steps + i)),) * 4,
        input_output_aliases={i + 1: i for i in range(len(before))},
        cost_estimate=pl.CostEstimate(flops=0, bytes_accessed=8 << 20, transcendentals=0),
        name=f"unpack{chunk}",
    )(recv, *before)


def dot(a, b, ca, cb):
    return lax.dot_general(
        a, b, (((ca,), (cb,)), ((), ())), preferred_element_type=jnp.float32
    )


def inverse_norm(x):
    return lax.rsqrt(jnp.mean(x * x, axis=-1, keepdims=True) + EPSILON)


def norm_backward(x, inverse, gain, grad):
    unit = x * inverse
    pulled = grad * gain
    along = jnp.mean(pulled * unit, axis=-1, keepdims=True)
    return inverse * (pulled - unit * along), grad * unit


def attend_kernel(ids_ref, gains_ref, recv_ref, back_ref, gain_ref, kv_ref, sum_ref, *, group):
    query_gain = gains_ref[0:1, :]
    key_gain = gains_ref[1:2, :]

    @pl.loop(0, SEQ, unroll=4)
    def _(s):
        x = recv_ref[s, TOK : 2 * TOK, :].astype(jnp.float32)
        rows = pl.ds(pl.multiple_of(s * TOK, TOK), TOK)
        kv_ref[rows, :HEAD] = (x * inverse_norm(x) * key_gain).astype(jnp.bfloat16)
        kv_ref[rows, HEAD:] = recv_ref[s, 2 * TOK : 3 * TOK, :]
        sum_ref[rows, :] = jnp.zeros((TOK, 2 * HEAD), jnp.float32)

    slot_of = lax.broadcasted_iota(jnp.int32, (1, SLOTS * BLOCK), 1) // BLOCK
    zeros = jnp.zeros((BLOCK, HEAD), jnp.bfloat16)

    def one_row_block(r):
        src, at = r // 2, pl.multiple_of((r % 2) * BLOCK, BLOCK)
        places, valid = [], jnp.int32(0)
        for j in range(SLOTS):
            block = ids_ref[r, j]
            valid = valid | jnp.where(block >= 0, 1 << j, 0)
            places.append(pl.ds(pl.multiple_of(jnp.maximum(block, 0) * BLOCK, BLOCK), BLOCK))
        bias = jnp.where(((valid >> slot_of) & 1) == 1, 0.0, -1e30)
        x = recv_ref[src, pl.ds(at, BLOCK), :].astype(jnp.float32)
        inverse = inverse_norm(x)
        qn = (x * inverse * query_gain).astype(jnp.bfloat16)
        grad = recv_ref[src, pl.ds(3 * TOK + at, BLOCK), :]
        apart = jnp.concatenate(
            [jnp.concatenate([qn, zeros], axis=1), jnp.concatenate([zeros, grad], axis=1)], axis=0
        )
        near = jnp.concatenate([kv_ref[p, :] for p in places], axis=0)
        products = dot(apart, near, 1, 1)
        grad_probs = products[BLOCK:]
        raised = jnp.exp2(products[:BLOCK] * (SCALE * LOG2E) + bias)
        inverse_sum = 1.0 / jnp.sum(raised, axis=-1, keepdims=True)
        delta = jnp.sum(raised * grad_probs, axis=-1, keepdims=True) * inverse_sum
        weights = (raised * inverse_sum).astype(jnp.bfloat16)
        grad_scores = (raised * ((grad_probs - delta) * (inverse_sum * SCALE))).astype(jnp.bfloat16)
        both = jnp.concatenate([grad_scores, weights], axis=0)
        mixed = dot(both, near, 1, 0)
        grad_qn = mixed[:BLOCK, :HEAD].astype(jnp.bfloat16).astype(jnp.float32)
        query_grad, gain_term = norm_backward(x, inverse, query_gain, grad_qn)
        back_ref[src, pl.ds(at, BLOCK), :] = mixed[BLOCK:, HEAD:].astype(jnp.bfloat16)
        back_ref[src, pl.ds(TOK + at, BLOCK), :] = query_grad.astype(jnp.bfloat16)
        terms = dot(both, apart, 0, 0)
        return places, terms, gain_term.reshape(BLOCK // 8, 8, HEAD).sum(0)

    def several(i, total):
        done = [one_row_block(i * group + n) for n in range(group)]
        for places, terms, gain_term in done:
            total = total + gain_term
            for j, p in enumerate(places):
                sum_ref[p, :] += terms[j * BLOCK : (j + 1) * BLOCK]
        return total

    query_total = lax.fori_loop(0, NB // group, several, jnp.zeros((8, HEAD), jnp.float32))

    def finish(s, total):
        rows = pl.ds(pl.multiple_of(s * TOK, TOK), TOK)
        x = recv_ref[s, TOK : 2 * TOK, :].astype(jnp.float32)
        grad_kn = sum_ref[rows, :HEAD].astype(jnp.bfloat16).astype(jnp.float32)
        key_grad, gain_term = norm_backward(x, inverse_norm(x), key_gain, grad_kn)
        back_ref[s, 2 * TOK : 3 * TOK, :] = key_grad.astype(jnp.bfloat16)
        back_ref[s, 3 * TOK : 4 * TOK, :] = sum_ref[rows, HEAD:].astype(jnp.bfloat16)
        return total + gain_term.reshape(TOK // 8, 8, HEAD).sum(0)

    key_total = lax.fori_loop(0, SEQ, finish, jnp.zeros((8, HEAD), jnp.float32), unroll=4)
    gain_ref[0:1, :] = jnp.sum(query_total, axis=0, keepdims=True)
    gain_ref[1:2, :] = jnp.sum(key_total, axis=0, keepdims=True)


def attend(chunk, ids, gains, recv, group=4):
    return pl.pallas_call(
        functools.partial(attend_kernel, group=group),
        out_shape=(
            jax.ShapeDtypeStruct((SEQ, 4 * TOK, HEAD), jnp.bfloat16),
            jax.ShapeDtypeStruct((2, HEAD), jnp.float32),
        ),
        in_specs=[
            pl.BlockSpec(memory_space=pltpu.SMEM),
            pl.BlockSpec(memory_space=pltpu.VMEM),
            pl.BlockSpec(memory_space=pltpu.VMEM),
        ],
        out_specs=(
            pl.BlockSpec(memory_space=pltpu.VMEM),
            pl.BlockSpec(memory_space=pltpu.VMEM),
        ),
        scratch_shapes=[
            pltpu.VMEM((TOKENS, 2 * HEAD), jnp.bfloat16),
            pltpu.VMEM((TOKENS, 2 * HEAD), jnp.float32),
        ],
        compiler_params=pltpu.CompilerParams(vmem_limit_bytes=32 << 20),
        cost_estimate=pl.CostEstimate(
            flops=25_000_000_000,
            bytes_accessed=4 << 20,
            transcendentals=NB * BLOCK * SLOTS * BLOCK,
        ),
        name=f"attend{chunk}",
    )(ids, gains, recv)


def swap(x, axis):
    return lax.all_to_all(x, axis, split_axis=0, concat_axis=0, tiled=True)


def summed(x, axis):
    size, step = lax.axis_size(axis), 1
    while step < size:
        x = x + lax.ppermute(x, axis, [(i, i ^ step) for i in range(size)])
        step *= 2
    return x


def on_device(queries, keys, values, cotangent, query_gain, key_gain, block_ids):
    arrays = (queries, keys, values, cotangent)
    s = lax.axis_index("seq")
    both = jnp.stack([query_gain, key_gain], axis=1)
    gains = [
        lax.dynamic_index_in_dim(both, c * SEQ + s, 0, keepdims=False) for c in range(CHUNKS)
    ]
    sent0 = pack(0, arrays)
    in0 = swap(sent0, "seq")
    sent1, in0 = lax.optimization_barrier((pack(1, arrays), in0))
    in1 = swap(sent1, "seq")
    back0, gain0 = attend(0, block_ids, gains[0], in0)
    back0, in1 = lax.optimization_barrier((back0, in1))
    out0 = swap(back0, "seq")
    back1, gain1 = attend(1, block_ids, gains[1], in1)
    back1, gain1, out0 = lax.optimization_barrier((back1, gain1, out0))
    out1 = swap(back1, "seq")
    done = unpack(0, out0, ())
    done = unpack(1, out1, tuple(done))
    part = jnp.concatenate([gain0, gain1], axis=0)
    part = summed(part, "dp")
    mine = lax.broadcasted_iota(jnp.int32, (SEQ, 1, 1), 0) == s
    every = summed(jnp.where(mine, part[None], 0.0), "seq")
    factor = (TOKENS * lax.axis_size("dp")) ** -0.5
    every = jnp.transpose(every.reshape(SEQ, CHUNKS, 2, HEAD), (2, 1, 0, 3)) * factor
    every = every.reshape(2, HEADS, HEAD)
    return (*done, every[0], every[1])


def solution(mesh):
    rows = P("dp", "seq", None)
    return jax.shard_map(
        on_device,
        mesh=mesh,
        in_specs=(rows, rows, rows, rows, P(), P(), P()),
        out_specs=(rows, rows, rows, rows, P(), P()),
        check_vma=False,
    )
```

time: 405 us -> 157 us (0.39); the launches traced: 398 us -> 155 us
  Pallas kernels: 317 us -> 49.8 us
  waiting for transfers between devices: 38.8 us -> 68.4 us
  blocking collectives: 9.63 us -> 0 us
    pallas_call x4, Pallas kernels: 259 us -> 11.8 us  [the longest x2 6.34 us: unpack(): pl.pallas_call(unpack_kernel, grid=(steps,), out_shape=(jax.ShapeDtypeStr...]
    ppermute x0 -> x8, waiting for transfers between devices: none -> 24.8 us  [summed(): x = x + lax.ppermute(x, axis, [(i, i ^ step) for i in range(size)])]
    pallas_call x2, Pallas kernels: 58.8 us -> 37.9 us  [attend(): pl.pallas_call(functools.partial(attend_kernel, group=group), out_shape=(...]
    ppermute x0 -> x8, starting transfers between devices: none -> 12.2 us  [summed(): x = x + lax.ppermute(x, axis, [(i, i ^ step) for i in range(size)])]
    all_to_all x1 -> x0, blocking collectives: 9.63 us -> none  [swap(): return lax.all_to_all(x, axis, split_axis=0, concat_axis=0, tiled=True)]
    all_to_all x5 -> x4, starting transfers between devices: 28.7 us -> 20.3 us  [swap(): return lax.all_to_all(x, axis, split_axis=0, concat_axis=0, tiled=True)]
    all_to_all x5 -> x4, waiting for transfers between devices: 38.8 us -> 43.5 us  [swap(): return lax.all_to_all(x, axis, split_axis=0, concat_axis=0, tiled=True)]
  transfers between devices with their start and end apart: 5 -> 12, of which waited for: 3 -> 11; matrix products, arithmetic and copies ran while one was open for 0% -> 1% of each run, Pallas kernels for 40% -> 28%
where the time goes in v1:
time: 157 us; the launch traced here: 155 us
  waiting for transfers between devices  68.4 us (44%)
  Pallas kernels  49.8 us (32%)
  starting transfers between devices  32.5 us (21%)
  local copies, waits for them, and re-layouts  3.33 us (2%)
    all_to_all x4, waiting for transfers between devices, swap(): return lax.all_to_all(x, axis, split_axis=0, concat_axis=0, tiled=True)  43.5 us
    pallas_call x2, Pallas kernels, attend(): pl.pallas_call(functools.partial(attend_kernel, group=group), out_shape=(...  37.9 us
    ppermute x8, waiting for transfers between devices, summed(): x = x + lax.ppermute(x, axis, [(i, i ^ step) for i in range(size)])  24.8 us
    all_to_all x4, starting transfers between devices, swap(): return lax.all_to_all(x, axis, split_axis=0, concat_axis=0, tiled=True)  20.3 us
    ppermute x8, starting transfers between devices, summed(): x = x + lax.ppermute(x, axis, [(i, i ^ step) for i in range(size)])  12.2 us
    pallas_call x2, Pallas kernels, unpack(): pl.pallas_call(unpack_kernel, grid=(steps,), out_shape=(jax.ShapeDtypeStr...  6.34 us
    pallas_call x2, Pallas kernels, pack(): pl.pallas_call(pack_kernel, grid=(steps,), out_shape=jax.ShapeDtypeStruct...  5.48 us
  transfers between devices with their start and end apart: 12, of which 11 were waited for; matrix products, arithmetic and copies ran while one was open for 1% of the time, Pallas kernels for 28%

profile of v1, /device:TPU:128, one launch (start us, length us, event | category | flops | bytes accessed | tf_op | source)
XLA Modules:
  0.0 155.0 jit_solution(8158642569591732282)
XLA Ops:
  0.6 2.7 %pack0.1 = bf16[16,512,128]{2,1,0:T(8,128)(2,1)} custom-call(bf16[1,128,4096]{2,1,0:T(8,128)(2,1)} %q_ref.3, bf16[1,128,4096]{2,1,0:T(8,128)(2,1)} %k_ref.3, bf16[1,128,4096]{2,1,0:T(8,128)(2,1)} %v_ref.3, bf16[1,128,4096]{2,1,0:T(8,128)(2,1)} %g_ref.3), custom_call_target="tpu_custom_call" | custom-call | bytes 8388608 | tf_op jit(solution)/shard_map/pack0/pallas_call | solution.py:33
  3.4 7.0 %all-to-all-start = ((bf16[16,512,128]{2,1,0:T(8,128)(2,1)}), bf16[16,512,128]{2,1,0:T(8,128)(2,1)S(1)}, u32[]{:S(2)}, u32[]{:S(2)}) async-start(bf16[16,512,128]{2,1,0:T(8,128)(2,1)} %pack0.1), calls=%async_computation | async-start | bytes 4194304 | tf_op jit(solution)/shard_map/all_to_all | solution.py:185
  10.4 2.8 %pack1.1 = bf16[16,512,128]{2,1,0:T(8,128)(2,1)} custom-call(bf16[1,128,4096]{2,1,0:T(8,128)(2,1)} %q_ref.3, bf16[1,128,4096]{2,1,0:T(8,128)(2,1)} %k_ref.3, bf16[1,128,4096]{2,1,0:T(8,128)(2,1)} %v_ref.3, bf16[1,128,4096]{2,1,0:T(8,128)(2,1)} %g_ref.3), custom_call_target="tpu_custom_call" | custom-call | bytes 8388608 | tf_op jit(solution)/shard_map/pack1/pallas_call | solution.py:33
  13.3 27.5 %all-to-all-done.recv_ref = bf16[16,512,128]{2,1,0:T(8,128)(2,1)S(1)} async-done(((bf16[16,512,128]{2,1,0:T(8,128)(2,1)}), bf16[16,512,128]{2,1,0:T(8,128)(2,1)S(1)}, u32[]{:S(2)}, u32[]{:S(2)}) %all-to-all-start) | async-done | bytes 2097184 | tf_op jit(solution)/shard_map/all_to_all | solution.py:185
  40.8 4.4 %all-to-all-start.1 = ((bf16[16,512,128]{2,1,0:T(8,128)(2,1)}), bf16[16,512,128]{2,1,0:T(8,128)(2,1)}, u32[]{:S(2)}, u32[]{:S(2)}) async-start(bf16[16,512,128]{2,1,0:T(8,128)(2,1)} %pack1.1), calls=%async_computation.1 | async-start | bytes 4194304 | tf_op jit(solution)/shard_map/all_to_all | solution.py:185
  45.2 17.9 %attend0.1 = (bf16[16,512,128]{2,1,0:T(8,128)(2,1)S(1)}, f32[2,128]{1,0:T(2,128)S(1)}) custom-call(s32[32,8]{1,0:T(8,128)S(1)} %copy.20.ids_ref, f32[2,128]{1,0:T(2,128)S(1)} %bitcast.10, bf16[16,512,128]{2,1,0:T(8,128)(2,1)S(1)} %all-to-all-done.recv_ref), custom_call_target="tpu_custom_call" | custom-call | flops 24999999488 | bytes 4194304 | tf_op jit(solution)/shard_map/attend0/pallas_call | solution.py:155
  63.1 1.3 copy-done
  64.4 8.5 %all-to-all-done.1.recv_ref = bf16[16,512,128]{2,1,0:T(8,128)(2,1)} async-done(((bf16[16,512,128]{2,1,0:T(8,128)(2,1)}), bf16[16,512,128]{2,1,0:T(8,128)(2,1)}, u32[]{:S(2)}, u32[]{:S(2)}) %all-to-all-start.1) | async-done | bytes 2097184 | tf_op jit(solution)/shard_map/all_to_all | solution.py:185
  72.9 4.4 %all-to-all-start.2 = ((bf16[16,512,128]{2,1,0:T(8,128)(2,1)}), bf16[16,512,128]{2,1,0:T(8,128)(2,1)}, u32[]{:S(2)}, u32[]{:S(2)}) async-start(bf16[16,512,128]{2,1,0:T(8,128)(2,1)} %copy-done), calls=%async_computation.2 | async-start | bytes 4194304 | tf_op jit(solution)/shard_map/all_to_all | solution.py:185
  77.3 20.1 %attend1.1 = (bf16[16,512,128]{2,1,0:T(8,128)(2,1)}, f32[2,128]{1,0:T(2,128)S(1)}) custom-call(s32[32,8]{1,0:T(8,128)S(1)} %copy.20.ids_ref, f32[2,128]{1,0:T(2,128)S(1)} %bitcast.9, bf16[16,512,128]{2,1,0:T(8,128)(2,1)} %all-to-all-done.1.recv_ref), custom_call_target="tpu_custom_call" | custom-call | flops 24999999488 | bytes 4194304 | tf_op jit(solution)/shard_map/attend1/pallas_call | solution.py:155
  97.4 7.6 %all-to-all-done.2.recv_ref = bf16[16,512,128]{2,1,0:T(8,128)(2,1)} async-done(((bf16[16,512,128]{2,1,0:T(8,128)(2,1)}), bf16[16,512,128]{2,1,0:T(8,128)(2,1)}, u32[]{:S(2)}, u32[]{:S(2)}) %all-to-all-start.2) | async-done | bytes 2097184 | tf_op jit(solution)/shard_map/all_to_all | solution.py:185
  105.0 4.3 %all-to-all-start.3 = ((bf16[16,512,128]{2,1,0:T(8,128)(2,1)}), bf16[16,512,128]{2,1,0:T(8,128)(2,1)S(1)}, u32[]{:S(2)}, u32[]{:S(2)}) async-start(bf16[16,512,128]{2,1,0:T(8,128)(2,1)} %get-tuple-element.32), calls=%async_computation.3 | async-start | bytes 4194304 | tf_op jit(solution)/shard_map/all_to_all | solution.py:185
  109.3 0.1 collective-permute-start
  109.4 1.1 collective-permute-done
  110.6 1.1 collective-permute-start.1
  111.7 2.6 %collective-permute-done.1 = f32[4,128]{1,0:T(4,128)S(1)} collective-permute-done((f32[4,128]{1,0:T(4,128)S(1)}, f32[4,128]{1,0:T(4,128)S(1)}, u32[]{:S(2)}, u32[]{:S(2)}) %collective-permute-start.1) | collective-permute-done | bytes 2080 | tf_op jit(solution)/shard_map/ppermute | solution.py:191
  114.3 1.5 collective-permute-start.2
  115.7 3.0 %collective-permute-done.2 = f32[4,128]{1,0:T(4,128)S(1)} collective-permute-done((f32[4,128]{1,0:T(4,128)S(1)}, f32[4,128]{1,0:T(4,128)S(1)}, u32[]{:S(2)}, u32[]{:S(2)}) %collective-permute-start.2) | collective-permute-done | bytes 2080 | tf_op jit(solution)/shard_map/ppermute | solution.py:191
  118.8 7.5 %collective-permute-done.3 = f32[4,128]{1,0:T(4,128)S(1)} collective-permute-done((f32[4,128]{1,0:T(4,128)S(1)}, f32[4,128]{1,0:T(4,128)S(1)}, u32[]{:S(2)}, u32[]{:S(2)}) %collective-permute-start.3) | collective-permute-done | bytes 2080 | tf_op jit(solution)/shard_map/ppermute | solution.py:191
  126.3 1.9 %collective-permute-start.4 = (f32[16,4,128]{2,0,1:T(8,128)S(1)}, f32[16,4,128]{2,0,1:T(8,128)S(1)}, u32[]{:S(2)}, u32[]{:S(2)}) collective-permute-start(f32[16,4,128]{2,0,1:T(8,128)S(1)} %broadcast_select_fusion), channel_id=1, source_target_pairs={{0,1},{1,0},{2,3},{3,2},{4,5},{5,4},{6,7},{7,6},{8,9},{9,8},{10,11... | collective-permute-start | bytes 98312 | tf_op jit(solution)/shard_map/ppermute | solution.py:191
  128.3 4.1 %collective-permute-done.4 = f32[16,4,128]{2,0,1:T(8,128)S(1)} collective-permute-done((f32[16,4,128]{2,0,1:T(8,128)S(1)}, f32[16,4,128]{2,0,1:T(8,128)S(1)}, u32[]{:S(2)}, u32[]{:S(2)}) %collective-permute-start.4) | collective-permute-done | bytes 32800 | tf_op jit(solution)/shard_map/ppermute | solution.py:191
  132.4 6.1 %collective-permute-start.5 = (f32[16,4,128]{2,0,1:T(8,128)S(1)}, f32[16,4,128]{2,0,1:T(8,128)S(1)}, u32[]{:S(2)}, u32[]{:S(2)}) collective-permute-start(f32[16,4,128]{2,0,1:T(8,128)S(1)} %fusion), channel_id=1, source_target_pairs={{0,2},{1,3},{2,0},{3,1},{4,6},{5,7},{6,4},{7,5},{8,10},{9,11},{10,... | collective-permute-start | bytes 98312 | tf_op jit(solution)/shard_map/ppermute | solution.py:191
  138.5 1.9 %collective-permute-done.5 = f32[16,4,128]{2,0,1:T(8,128)S(1)} collective-permute-done((f32[16,4,128]{2,0,1:T(8,128)S(1)}, f32[16,4,128]{2,0,1:T(8,128)S(1)}, u32[]{:S(2)}, u32[]{:S(2)}) %collective-permute-start.5) | collective-permute-done | bytes 32800 | tf_op jit(solution)/shard_map/ppermute | solution.py:191
  140.4 0.1 fusion.5
  140.5 0.4 collective-permute-start.6
  140.9 3.5 %collective-permute-done.6 = f32[16,4,128]{2,0,1:T(8,128)S(1)} collective-permute-done((f32[16,4,128]{2,0,1:T(8,128)S(1)}, f32[16,4,128]{2,0,1:T(8,128)S(1)}, u32[]{:S(2)}, u32[]{:S(2)}) %collective-permute-start.6) | collective-permute-done | bytes 32800 | tf_op jit(solution)/shard_map/ppermute | solution.py:191
  144.4 1.1 collective-permute-start.7
  145.5 3.2 %unpack0.1 = (bf16[1,128,4096]{2,1,0:T(8,128)(2,1)}, bf16[1,128,4096]{2,1,0:T(8,128)(2,1)}, bf16[1,128,4096]{2,1,0:T(8,128)(2,1)}, bf16[1,128,4096]{2,1,0:T(8,128)(2,1)}) custom-call(bf16[16,512,128]{2,1,0:T(8,128)(2,1)} %all-to-all-done.2.recv_ref), custom_call_target="tpu_custom_call" | custom-call | bytes 8388608 | tf_op jit(solution)/shard_map/unpack0/pallas_call | solution.py:53
  148.7 1.1 collective-permute-done.7
  149.8 0.6 fusion.4
  150.5 1.3 copy-done.1
  151.8 3.2 %unpack1.1 = (bf16[1,128,4096]{2,1,0:T(8,128)(2,1)}, bf16[1,128,4096]{2,1,0:T(8,128)(2,1)}, bf16[1,128,4096]{2,1,0:T(8,128)(2,1)}, bf16[1,128,4096]{2,1,0:T(8,128)(2,1)}) custom-call(bf16[16,512,128]{2,1,0:T(8,128)(2,1)} %copy-done.1, ...), custom_call_target="tpu_custom_call", output_to_operand_aliasing={{0}: (1, {}), {1}: (2, {}), {2}: (3, {}), {3}: (4, {})} | custom-call | bytes 8388608 | tf_op jit(solution)/shard_map/unpack1/pallas_call | solution.py:53
  (22 shorter events, 0.3 us)
Async XLA Ops:
  3.4 37.4 %all-to-all-start = ((bf16[16,512,128]{2,1,0:T(8,128)(2,1)}), bf16[16,512,128]{2,1,0:T(8,128)(2,1)S(1)}, u32[]{:S(2)}, u32[]{:S(2)}) async-start(bf16[16,512,128]{2,1,0:T(8,128)(2,1)} %pack0.1), calls=%async_computation | async-start | bytes 4194304 | tf_op jit(solution)/shard_map/all_to_all | solution.py:185
  10.4 2.8 %copy-start.4 = (s32[32,8]{0,1:T(8,128)S(1)}, s32[32,8]{0,1:T(8,128)}, u32[]{:S(2)}) copy-start(s32[32,8]{0,1:T(8,128)} %param.13) | copy-start | bytes 3076
  10.4 2.9 %copy-start.2 = (f32[32,128]{1,0:T(8,128)S(1)}, f32[32,128]{1,0:T(8,128)}, u32[]{:S(2)}) copy-start(f32[32,128]{1,0:T(8,128)} %param.11) | copy-start | bytes 49156
  10.4 2.9 %copy-start.3 = (f32[32,128]{1,0:T(8,128)S(1)}, f32[32,128]{1,0:T(8,128)}, u32[]{:S(2)}) copy-start(f32[32,128]{1,0:T(8,128)} %param.12) | copy-start | bytes 49156
  40.8 32.1 %all-to-all-start.1 = ((bf16[16,512,128]{2,1,0:T(8,128)(2,1)}), bf16[16,512,128]{2,1,0:T(8,128)(2,1)}, u32[]{:S(2)}, u32[]{:S(2)}) async-start(bf16[16,512,128]{2,1,0:T(8,128)(2,1)} %pack1.1), calls=%async_computation.1 | async-start | bytes 4194304 | tf_op jit(solution)/shard_map/all_to_all | solution.py:185
  63.1 1.3 copy-start
  72.9 32.1 %all-to-all-start.2 = ((bf16[16,512,128]{2,1,0:T(8,128)(2,1)}), bf16[16,512,128]{2,1,0:T(8,128)(2,1)}, u32[]{:S(2)}, u32[]{:S(2)}) async-start(bf16[16,512,128]{2,1,0:T(8,128)(2,1)} %copy-done), calls=%async_computation.2 | async-start | bytes 4194304 | tf_op jit(solution)/shard_map/all_to_all | solution.py:185
  105.0 45.5 %all-to-all-start.3 = ((bf16[16,512,128]{2,1,0:T(8,128)(2,1)}), bf16[16,512,128]{2,1,0:T(8,128)(2,1)S(1)}, u32[]{:S(2)}, u32[]{:S(2)}) async-start(bf16[16,512,128]{2,1,0:T(8,128)(2,1)} %get-tuple-element.32), calls=%async_computation.3 | async-start | bytes 4194304 | tf_op jit(solution)/shard_map/all_to_all | solution.py:185
  109.3 1.2 collective-permute-start
  110.6 3.7 %collective-permute-start.1 = (f32[4,128]{1,0:T(4,128)S(1)}, f32[4,128]{1,0:T(4,128)S(1)}, u32[]{:S(2)}, u32[]{:S(2)}) collective-permute-start(f32[4,128]{1,0:T(4,128)S(1)} %fusion.3), channel_id=1, source_target_pairs={{0,32},{16,48},{32,0},{48,16},{64,96},{80,112},{96,64},{112,80},{1... | collective-permute-start | bytes 6152 | tf_op jit(solution)/shard_map/ppermute | solution.py:191
  114.3 4.5 %collective-permute-start.2 = (f32[4,128]{1,0:T(4,128)S(1)}, f32[4,128]{1,0:T(4,128)S(1)}, u32[]{:S(2)}, u32[]{:S(2)}) collective-permute-start(f32[4,128]{1,0:T(4,128)S(1)} %add.36), channel_id=1, source_target_pairs={{0,64},{16,80},{32,96},{48,112},{64,0},{80,16},{96,32},{112,48},{1... | collective-permute-start | bytes 6152 | tf_op jit(solution)/shard_map/ppermute | solution.py:191
  118.8 7.5 %collective-permute-start.3 = (f32[4,128]{1,0:T(4,128)S(1)}, f32[4,128]{1,0:T(4,128)S(1)}, u32[]{:S(2)}, u32[]{:S(2)}) collective-permute-start(f32[4,128]{1,0:T(4,128)S(1)} %add.37), channel_id=1, source_target_pairs={{0,128},{16,144},{32,160},{48,176},{64,192},{80,208},{96,224},{112... | collective-permute-start | bytes 6152 | tf_op jit(solution)/shard_map/ppermute | solution.py:191
  126.3 6.0 %collective-permute-start.4 = (f32[16,4,128]{2,0,1:T(8,128)S(1)}, f32[16,4,128]{2,0,1:T(8,128)S(1)}, u32[]{:S(2)}, u32[]{:S(2)}) collective-permute-start(f32[16,4,128]{2,0,1:T(8,128)S(1)} %broadcast_select_fusion), channel_id=1, source_target_pairs={{0,1},{1,0},{2,3},{3,2},{4,5},{5,4},{6,7},{7,6},{8,9},{9,8},{10,11... | collective-permute-start | bytes 98312 | tf_op jit(solution)/shard_map/ppermute | solution.py:191
  132.4 8.0 %collective-permute-start.5 = (f32[16,4,128]{2,0,1:T(8,128)S(1)}, f32[16,4,128]{2,0,1:T(8,128)S(1)}, u32[]{:S(2)}, u32[]{:S(2)}) collective-permute-start(f32[16,4,128]{2,0,1:T(8,128)S(1)} %fusion), channel_id=1, source_target_pairs={{0,2},{1,3},{2,0},{3,1},{4,6},{5,7},{6,4},{7,5},{8,10},{9,11},{10,... | collective-permute-start | bytes 98312 | tf_op jit(solution)/shard_map/ppermute | solution.py:191
  140.5 3.9 %collective-permute-start.6 = (f32[16,4,128]{2,0,1:T(8,128)S(1)}, f32[16,4,128]{2,0,1:T(8,128)S(1)}, u32[]{:S(2)}, u32[]{:S(2)}) collective-permute-start(f32[16,4,128]{2,0,1:T(8,128)S(1)} %fusion.5), channel_id=1, source_target_pairs={{0,4},{1,5},{2,6},{3,7},{4,0},{5,1},{6,2},{7,3},{8,12},{9,13},{10,... | collective-permute-start | bytes 98312 | tf_op jit(solution)/shard_map/ppermute | solution.py:191
  144.4 5.4 %collective-permute-start.7 = (f32[16,4,128]{2,0,1:T(8,128)S(1)}, f32[16,4,128]{2,0,1:T(8,128)S(1)}, u32[]{:S(2)}, u32[]{:S(2)}) collective-permute-start(f32[16,4,128]{2,0,1:T(8,128)S(1)} %add.41), channel_id=1, source_target_pairs={{0,8},{1,9},{2,10},{3,11},{4,12},{5,13},{6,14},{7,15},{8,0},{9,1},... | collective-permute-start | bytes 98312 | tf_op jit(solution)/shard_map/ppermute | solution.py:191
  150.5 1.3 copy-start.1

commit v2 on v1

--- a/solution.py
+++ b/solution.py
@@ -58,6 +58,7 @@
         + [pl.BlockSpec(memory_space=pl.ANY)] * len(before),
         out_specs=(pl.BlockSpec((1, TOK, AT_ONCE * HEAD), lambda i: (0, 0, chunk * steps + i)),) * 4,
         input_output_aliases={i + 1: i for i in range(len(before))},
+        compiler_params=pltpu.CompilerParams(vmem_limit_bytes=24 << 20),
         cost_estimate=pl.CostEstimate(flops=0, bytes_accessed=8 << 20, transcendentals=0),
         name=f"unpack{chunk}",
     )(recv, *before)
@@ -80,62 +81,92 @@
     return inverse * (pulled - unit * along), grad * unit
 
 
-def attend_kernel(ids_ref, gains_ref, recv_ref, back_ref, gain_ref, kv_ref, sum_ref, *, group):
+def attend_kernel(
+    ids_ref, gains_ref, recv_ref, back_ref, gain_ref, kv_ref, qg_ref, sum_ref, prod_a, prod_b, mix_a, mix_b, *, group
+):
     query_gain = gains_ref[0:1, :]
     key_gain = gains_ref[1:2, :]
+    prods, mixes = (prod_a, prod_b), (mix_a, mix_b)
+    units = NB // group
+    zeros = jnp.zeros((BLOCK, HEAD), jnp.bfloat16)
 
     @pl.loop(0, SEQ, unroll=4)
     def _(s):
+        rows = pl.ds(pl.multiple_of(s * TOK, TOK), TOK)
         x = recv_ref[s, TOK : 2 * TOK, :].astype(jnp.float32)
-        rows = pl.ds(pl.multiple_of(s * TOK, TOK), TOK)
         kv_ref[rows, :HEAD] = (x * inverse_norm(x) * key_gain).astype(jnp.bfloat16)
         kv_ref[rows, HEAD:] = recv_ref[s, 2 * TOK : 3 * TOK, :]
         sum_ref[rows, :] = jnp.zeros((TOK, 2 * HEAD), jnp.float32)
+        x = recv_ref[s, :TOK, :].astype(jnp.float32)
+        qn = (x * inverse_norm(x) * query_gain).astype(jnp.bfloat16)
+        grad = recv_ref[s, 3 * TOK : 4 * TOK, :]
+        for h in range(2):
+            part = slice(h * BLOCK, (h + 1) * BLOCK)
+            qg_ref[2 * s + h, :BLOCK, :HEAD] = qn[part]
+            qg_ref[2 * s + h, :BLOCK, HEAD:] = zeros
+            qg_ref[2 * s + h, BLOCK:, :HEAD] = zeros
+            qg_ref[2 * s + h, BLOCK:, HEAD:] = grad[part]
 
     slot_of = lax.broadcasted_iota(jnp.int32, (1, SLOTS * BLOCK), 1) // BLOCK
-    zeros = jnp.zeros((BLOCK, HEAD), jnp.bfloat16)
-
-    def one_row_block(r):
-        src, at = r // 2, pl.multiple_of((r % 2) * BLOCK, BLOCK)
-        places, valid = [], jnp.int32(0)
-        for j in range(SLOTS):
-            block = ids_ref[r, j]
-            valid = valid | jnp.where(block >= 0, 1 << j, 0)
-            places.append(pl.ds(pl.multiple_of(jnp.maximum(block, 0) * BLOCK, BLOCK), BLOCK))
-        bias = jnp.where(((valid >> slot_of) & 1) == 1, 0.0, -1e30)
-        x = recv_ref[src, pl.ds(at, BLOCK), :].astype(jnp.float32)
-        inverse = inverse_norm(x)
-        qn = (x * inverse * query_gain).astype(jnp.bfloat16)
-        grad = recv_ref[src, pl.ds(3 * TOK + at, BLOCK), :]
-        apart = jnp.concatenate(
-            [jnp.concatenate([qn, zeros], axis=1), jnp.concatenate([zeros, grad], axis=1)], axis=0
-        )
-        near = jnp.concatenate([kv_ref[p, :] for p in places], axis=0)
-        products = dot(apart, near, 1, 1)
-        grad_probs = products[BLOCK:]
-        raised = jnp.exp2(products[:BLOCK] * (SCALE * LOG2E) + bias)
-        inverse_sum = 1.0 / jnp.sum(raised, axis=-1, keepdims=True)
-        delta = jnp.sum(raised * grad_probs, axis=-1, keepdims=True) * inverse_sum
-        weights = (raised * inverse_sum).astype(jnp.bfloat16)
-        grad_scores = (raised * ((grad_probs - delta) * (inverse_sum * SCALE))).astype(jnp.bfloat16)
-        both = jnp.concatenate([grad_scores, weights], axis=0)
-        mixed = dot(both, near, 1, 0)
-        grad_qn = mixed[:BLOCK, :HEAD].astype(jnp.bfloat16).astype(jnp.float32)
-        query_grad, gain_term = norm_backward(x, inverse, query_gain, grad_qn)
-        back_ref[src, pl.ds(at, BLOCK), :] = mixed[BLOCK:, HEAD:].astype(jnp.bfloat16)
-        back_ref[src, pl.ds(TOK + at, BLOCK), :] = query_grad.astype(jnp.bfloat16)
-        terms = dot(both, apart, 0, 0)
-        return places, terms, gain_term.reshape(BLOCK // 8, 8, HEAD).sum(0)
-
-    def several(i, total):
-        done = [one_row_block(i * group + n) for n in range(group)]
-        for places, terms, gain_term in done:
-            total = total + gain_term
-            for j, p in enumerate(places):
+
+    def places_of(r):
+        blocks = [jnp.maximum(ids_ref[r, j], 0) for j in range(SLOTS)]
+        return [pl.ds(pl.multiple_of(b * BLOCK, BLOCK), BLOCK) for b in blocks]
+
+    def near_of(r):
+        return jnp.concatenate([kv_ref[p, :] for p in places_of(r)], axis=0)
+
+    def multiply(t, at):
+        for n in range(group):
+            r = t * group + n
+            prods[at][n] = dot(qg_ref[r], near_of(r), 1, 1)
+
+    def weigh(t, at):
+        for n in range(group):
+            r = t * group + n
+            valid = jnp.int32(0)
+            for j in range(SLOTS):
+                valid = valid | jnp.where(ids_ref[r, j] >= 0, 1 << j, 0)
+            bias = jnp.where(((valid >> slot_of) & 1) == 1, 0.0, -1e30)
+            grad_probs = prods[at][n, BLOCK:, :]
+            raised = jnp.exp2(prods[at][n, :BLOCK, :] * (SCALE * LOG2E) + bias)
+            inverse_sum = 1.0 / jnp.sum(raised, axis=-1, keepdims=True)
+            delta = jnp.sum(raised * grad_probs, axis=-1, keepdims=True) * inverse_sum
+            mixes[at][n, BLOCK:, :] = (raised * inverse_sum).astype(jnp.bfloat16)
+            grad_scores = raised * ((grad_probs - delta) * (inverse_sum * SCALE))
+            mixes[at][n, :BLOCK, :] = grad_scores.astype(jnp.bfloat16)
+
+    def spread(t, at, total):
+        for n in range(group):
+            r = t * group + n
+            src, first = r // 2, pl.multiple_of((r % 2) * BLOCK, BLOCK)
+            mixed = dot(mixes[at][n], near_of(r), 1, 0)
+            x = recv_ref[src, pl.ds(first, BLOCK), :].astype(jnp.float32)
+            grad_qn = mixed[:BLOCK, :HEAD].astype(jnp.bfloat16).astype(jnp.float32)
+            query_grad, gain_term = norm_backward(x, inverse_norm(x), query_gain, grad_qn)
+            back_ref[src, pl.ds(first, BLOCK), :] = mixed[BLOCK:, HEAD:].astype(jnp.bfloat16)
+            back_ref[src, pl.ds(TOK + first, BLOCK), :] = query_grad.astype(jnp.bfloat16)
+            total = total + gain_term.reshape(BLOCK // 8, 8, HEAD).sum(0)
+            terms = dot(mixes[at][n], qg_ref[r], 0, 0)
+            for j, p in enumerate(places_of(r)):
                 sum_ref[p, :] += terms[j * BLOCK : (j + 1) * BLOCK]
         return total
 
-    query_total = lax.fori_loop(0, NB // group, several, jnp.zeros((8, HEAD), jnp.float32))
+    def step(t, at, total):
+        multiply(t, at)
+        weigh(t - 1, 1 - at)
+        return spread(t - 2, at, total)
+
+    def two_steps(i, total):
+        return step(2 * i + 1, 1, step(2 * i, 0, total))
+
+    multiply(0, 0)
+    multiply(1, 1)
+    weigh(0, 0)
+    query_total = lax.fori_loop(1, units // 2, two_steps, jnp.zeros((8, HEAD), jnp.float32))
+    weigh(units - 1, 1)
+    query_total = spread(units - 2, 0, query_total)
+    query_total = spread(units - 1, 1, query_total)
 
     def finish(s, total):
         rows = pl.ds(pl.multiple_of(s * TOK, TOK), TOK)
@@ -151,7 +182,7 @@
     gain_ref[1:2, :] = jnp.sum(key_total, axis=0, keepdims=True)
 
 
-def attend(chunk, ids, gains, recv, group=4):
+def attend(chunk, ids, gains, recv, group=2):
     return pl.pallas_call(
         functools.partial(attend_kernel, group=group),
         out_shape=(
@@ -169,7 +200,12 @@
         ),
         scratch_shapes=[
             pltpu.VMEM((TOKENS, 2 * HEAD), jnp.bfloat16),
+            pltpu.VMEM((NB, 2 * BLOCK, 2 * HEAD), jnp.bfloat16),
             pltpu.VMEM((TOKENS, 2 * HEAD), jnp.float32),
+            pltpu.VMEM((group, 2 * BLOCK, SLOTS * BLOCK), jnp.float32),
+            pltpu.VMEM((group, 2 * BLOCK, SLOTS * BLOCK), jnp.float32),
+            pltpu.VMEM((group, 2 * BLOCK, SLOTS * BLOCK), jnp.bfloat16),
+            pltpu.VMEM((group, 2 * BLOCK, SLOTS * BLOCK), jnp.bfloat16),
         ],
         compiler_params=pltpu.CompilerParams(vmem_limit_bytes=32 << 20),
         cost_estimate=pl.CostEstimate(
@@ -185,11 +221,10 @@
     return lax.all_to_all(x, axis, split_axis=0, concat_axis=0, tiled=True)
 
 
-def summed(x, axis):
-    size, step = lax.axis_size(axis), 1
-    while step < size:
+def summed(x, axis, steps):
+    size = lax.axis_size(axis)
+    for step in steps:
         x = x + lax.ppermute(x, axis, [(i, i ^ step) for i in range(size)])
-        step *= 2
     return x
 
 
@@ -208,14 +243,14 @@
     back0, in1 = lax.optimization_barrier((back0, in1))
     out0 = swap(back0, "seq")
     back1, gain1 = attend(1, block_ids, gains[1], in1)
-    back1, gain1, out0 = lax.optimization_barrier((back1, gain1, out0))
+    part = summed(jnp.concatenate([gain0, gain1], axis=0), "dp", (1, 2, 4))
+    back1, part, out0 = lax.optimization_barrier((back1, part, out0))
     out1 = swap(back1, "seq")
     done = unpack(0, out0, ())
     done = unpack(1, out1, tuple(done))
-    part = jnp.concatenate([gain0, gain1], axis=0)
-    part = summed(part, "dp")
+    part = summed(part, "dp", (8,))
     mine = lax.broadcasted_iota(jnp.int32, (SEQ, 1, 1), 0) == s
-    every = summed(jnp.where(mine, part[None], 0.0), "seq")
+    every = summed(jnp.where(mine, part[None], 0.0), "seq", (1, 2, 4, 8))
     factor = (TOKENS * lax.axis_size("dp")) ** -0.5
     every = jnp.transpose(every.reshape(SEQ, CHUNKS, 2, HEAD), (2, 1, 0, 3)) * factor
     every = every.reshape(2, HEADS, HEAD)

time: 157 us -> 153 us (0.975); the launches traced: 155 us -> 153 us
  Pallas kernels: 49.8 us -> 30.7 us
  waiting for transfers between devices: 68.4 us -> 84.5 us
  local copies, waits for them, and re-layouts: 3.33 us -> 6.24 us
  starting transfers between devices: 32.5 us -> 30.3 us
    pallas_call x2, Pallas kernels: 37.9 us -> 22 us  [attend(): pl.pallas_call(functools.partial(attend_kernel, group=group), out_shape=(...]
    ppermute x8, waiting for transfers between devices: 24.8 us -> 35.7 us  [summed(): x = x + lax.ppermute(x, axis, [(i, i ^ step) for i in range(size)])]
    all_to_all x4, waiting for transfers between devices: 43.5 us -> 48.8 us  [swap(): return lax.all_to_all(x, axis, split_axis=0, concat_axis=0, tiled=True)]
    pallas_call x2, Pallas kernels: 6.34 us -> 3.19 us  [unpack(): pl.pallas_call(unpack_kernel, grid=(steps,), out_shape=(jax.ShapeDtypeStr...]
    unnamed x11 -> x15, local copies, waits for them, and re-layouts: 2.72 us -> 5.63 us
    ppermute x8, starting transfers between devices: 12.2 us -> 10.3 us  [summed(): x = x + lax.ppermute(x, axis, [(i, i ^ step) for i in range(size)])]
  transfers between devices with their start and end apart: 12 -> 12, of which waited for: 11 -> 10; matrix products, arithmetic and copies ran while one was open for 1% -> 1% of each run, Pallas kernels for 28% -> 17%
where the time goes in v2:
time: 153 us
  waiting for transfers between devices  84.5 us (55%)
  Pallas kernels  30.7 us (20%)
  starting transfers between devices  30.3 us (20%)
  local copies, waits for them, and re-layouts  6.24 us (4%)
    all_to_all x4, waiting for transfers between devices, swap(): return lax.all_to_all(x, axis, split_axis=0, concat_axis=0, tiled=True)  48.8 us
    ppermute x8, waiting for transfers between devices, summed(): x = x + lax.ppermute(x, axis, [(i, i ^ step) for i in range(size)])  35.7 us
    pallas_call x2, Pallas kernels, attend(): pl.pallas_call(functools.partial(attend_kernel, group=group), out_shape=(...  22 us
    all_to_all x4, starting transfers between devices, swap(): return lax.all_to_all(x, axis, split_axis=0, concat_axis=0, tiled=True)  20 us
    ppermute x8, starting transfers between devices, summed(): x = x + lax.ppermute(x, axis, [(i, i ^ step) for i in range(size)])  10.3 us
    unnamed x15, local copies, waits for them, and re-layouts  5.63 us
    pallas_call x2, Pallas kernels, pack(): pl.pallas_call(pack_kernel, grid=(steps,), out_shape=jax.ShapeDtypeStruct...  5.44 us
    pallas_call x2, Pallas kernels, unpack(): pl.pallas_call(unpack_kernel, grid=(steps,), out_shape=(jax.ShapeDtypeStr...  3.19 us
  transfers between devices with their start and end apart: 12, of which 10 were waited for; matrix products, arithmetic and copies ran while one was open for 1% of the time, Pallas kernels for 17%

profile of v2, /device:TPU:128, one launch (start us, length us, event | category | flops | bytes accessed | tf_op | source)
XLA Modules:
  0.0 152.8 jit_solution(4438407014815177972)
XLA Ops:
  0.6 2.7 %pack0.1 = bf16[16,512,128]{2,1,0:T(8,128)(2,1)} custom-call(bf16[1,128,4096]{2,1,0:T(8,128)(2,1)} %q_ref.3, bf16[1,128,4096]{2,1,0:T(8,128)(2,1)} %k_ref.3, bf16[1,128,4096]{2,1,0:T(8,128)(2,1)} %v_ref.3, bf16[1,128,4096]{2,1,0:T(8,128)(2,1)} %g_ref.3), custom_call_target="tpu_custom_call" | custom-call | bytes 8388608 | tf_op jit(solution)/shard_map/pack0/pallas_call | solution.py:33
  3.3 7.0 %all-to-all-start = ((bf16[16,512,128]{2,1,0:T(8,128)(2,1)}), bf16[16,512,128]{2,1,0:T(8,128)(2,1)S(1)}, u32[]{:S(2)}, u32[]{:S(2)}) async-start(bf16[16,512,128]{2,1,0:T(8,128)(2,1)} %pack0.1), calls=%async_computation | async-start | bytes 4194304 | tf_op jit(solution)/shard_map/all_to_all | solution.py:221
  10.4 2.7 %pack1.1 = bf16[16,512,128]{2,1,0:T(8,128)(2,1)} custom-call(bf16[1,128,4096]{2,1,0:T(8,128)(2,1)} %q_ref.3, bf16[1,128,4096]{2,1,0:T(8,128)(2,1)} %k_ref.3, bf16[1,128,4096]{2,1,0:T(8,128)(2,1)} %v_ref.3, bf16[1,128,4096]{2,1,0:T(8,128)(2,1)} %g_ref.3), custom_call_target="tpu_custom_call" | custom-call | bytes 8388608 | tf_op jit(solution)/shard_map/pack1/pallas_call | solution.py:33
  13.3 27.5 %all-to-all-done.recv_ref = bf16[16,512,128]{2,1,0:T(8,128)(2,1)S(1)} async-done(((bf16[16,512,128]{2,1,0:T(8,128)(2,1)}), bf16[16,512,128]{2,1,0:T(8,128)(2,1)S(1)}, u32[]{:S(2)}, u32[]{:S(2)}) %all-to-all-start) | async-done | bytes 2097184 | tf_op jit(solution)/shard_map/all_to_all | solution.py:221
  40.8 4.4 %all-to-all-start.1 = ((bf16[16,512,128]{2,1,0:T(8,128)(2,1)}), bf16[16,512,128]{2,1,0:T(8,128)(2,1)}, u32[]{:S(2)}, u32[]{:S(2)}) async-start(bf16[16,512,128]{2,1,0:T(8,128)(2,1)} %pack1.1), calls=%async_computation.1 | async-start | bytes 4194304 | tf_op jit(solution)/shard_map/all_to_all | solution.py:221
  45.2 10.6 %attend0.1 = (bf16[16,512,128]{2,1,0:T(8,128)(2,1)S(1)}, f32[2,128]{1,0:T(2,128)S(1)}) custom-call(s32[32,8]{1,0:T(8,128)S(1)} %copy.20.ids_ref, f32[2,128]{1,0:T(2,128)S(1)} %bitcast.10, bf16[16,512,128]{2,1,0:T(8,128)(2,1)S(1)} %all-to-all-done.recv_ref), custom_call_target="tpu_custom_call" | custom-call | flops 24999999488 | bytes 4194304 | tf_op jit(solution)/shard_map/attend0/pallas_call | solution.py:186
  55.8 1.3 copy-done.3
  57.1 15.7 %all-to-all-done.1.recv_ref = bf16[16,512,128]{2,1,0:T(8,128)(2,1)} async-done(((bf16[16,512,128]{2,1,0:T(8,128)(2,1)}), bf16[16,512,128]{2,1,0:T(8,128)(2,1)}, u32[]{:S(2)}, u32[]{:S(2)}) %all-to-all-start.1) | async-done | bytes 2097184 | tf_op jit(solution)/shard_map/all_to_all | solution.py:221
  72.9 4.2 %all-to-all-start.2 = ((bf16[16,512,128]{2,1,0:T(8,128)(2,1)}), bf16[16,512,128]{2,1,0:T(8,128)(2,1)S(1)}, u32[]{:S(2)}, u32[]{:S(2)}) async-start(bf16[16,512,128]{2,1,0:T(8,128)(2,1)} %copy-done.3), calls=%async_computation.2 | async-start | bytes 4194304 | tf_op jit(solution)/shard_map/all_to_all | solution.py:221
  77.1 11.4 %attend1.1 = (bf16[16,512,128]{2,1,0:T(8,128)(2,1)S(1)}, f32[2,128]{1,0:T(2,128)S(1)}) custom-call(s32[32,8]{1,0:T(8,128)S(1)} %copy.20.ids_ref, f32[2,128]{1,0:T(2,128)S(1)} %bitcast.9, bf16[16,512,128]{2,1,0:T(8,128)(2,1)} %all-to-all-done.1.recv_ref), custom_call_target="tpu_custom_call" | custom-call | flops 24999999488 | bytes 4194304 | tf_op jit(solution)/shard_map/attend1/pallas_call | solution.py:186
  88.5 1.3 copy-done.2
  89.9 1.1 collective-permute-done
  91.0 1.1 collective-permute-start.1
  92.1 2.6 %collective-permute-done.1 = f32[4,128]{1,0:T(4,128)S(1)} collective-permute-done((f32[4,128]{1,0:T(4,128)S(1)}, f32[4,128]{1,0:T(4,128)S(1)}, u32[]{:S(2)}, u32[]{:S(2)}) %collective-permute-start.1) | collective-permute-done | bytes 2080 | tf_op jit(solution)/shard_map/ppermute | solution.py:227
  94.7 1.5 collective-permute-start.2
  96.2 3.0 %collective-permute-done.2 = f32[4,128]{1,0:T(4,128)S(1)} collective-permute-done((f32[4,128]{1,0:T(4,128)S(1)}, f32[4,128]{1,0:T(4,128)S(1)}, u32[]{:S(2)}, u32[]{:S(2)}) %collective-permute-start.2) | collective-permute-done | bytes 2080 | tf_op jit(solution)/shard_map/ppermute | solution.py:227
  99.2 5.6 %all-to-all-done.2.recv_ref = bf16[16,512,128]{2,1,0:T(8,128)(2,1)S(1)} async-done(((bf16[16,512,128]{2,1,0:T(8,128)(2,1)}), bf16[16,512,128]{2,1,0:T(8,128)(2,1)S(1)}, u32[]{:S(2)}, u32[]{:S(2)}) %all-to-all-start.2) | async-done | bytes 2097184 | tf_op jit(solution)/shard_map/all_to_all | solution.py:221
  104.8 1.3 copy-done
  106.1 4.3 %all-to-all-start.3 = ((bf16[16,512,128]{2,1,0:T(8,128)(2,1)}), bf16[16,512,128]{2,1,0:T(8,128)(2,1)S(1)}, u32[]{:S(2)}, u32[]{:S(2)}) async-start(bf16[16,512,128]{2,1,0:T(8,128)(2,1)} %copy-done.2), calls=%async_computation.3 | async-start | bytes 4194304 | tf_op jit(solution)/shard_map/all_to_all | solution.py:221
  110.4 0.1 collective-permute-start.3
  110.5 7.5 %collective-permute-done.3 = f32[4,128]{1,0:T(4,128)S(1)} collective-permute-done((f32[4,128]{1,0:T(4,128)S(1)}, f32[4,128]{1,0:T(4,128)S(1)}, u32[]{:S(2)}, u32[]{:S(2)}) %collective-permute-start.3) | collective-permute-done | bytes 2080 | tf_op jit(solution)/shard_map/ppermute | solution.py:227
  118.1 1.9 %collective-permute-start.4 = (f32[16,4,128]{2,0,1:T(8,128)S(1)}, f32[16,4,128]{2,0,1:T(8,128)S(1)}, u32[]{:S(2)}, u32[]{:S(2)}) collective-permute-start(f32[16,4,128]{2,0,1:T(8,128)S(1)} %broadcast_select_fusion), channel_id=1, source_target_pairs={{0,1},{1,0},{2,3},{3,2},{4,5},{5,4},{6,7},{7,6},{8,9},{9,8},{10,11... | collective-permute-start | bytes 98312 | tf_op jit(solution)/shard_map/ppermute | solution.py:227
  119.9 13.8 %collective-permute-done.4 = f32[16,4,128]{2,0,1:T(8,128)S(1)} collective-permute-done((f32[16,4,128]{2,0,1:T(8,128)S(1)}, f32[16,4,128]{2,0,1:T(8,128)S(1)}, u32[]{:S(2)}, u32[]{:S(2)}) %collective-permute-start.4) | collective-permute-done | bytes 32800 | tf_op jit(solution)/shard_map/ppermute | solution.py:227
  133.8 5.4 %collective-permute-done.5 = f32[16,4,128]{2,0,1:T(8,128)S(1)} collective-permute-done((f32[16,4,128]{2,0,1:T(8,128)S(1)}, f32[16,4,128]{2,0,1:T(8,128)S(1)}, u32[]{:S(2)}, u32[]{:S(2)}) %collective-permute-start.5) | collective-permute-done | bytes 32800 | tf_op jit(solution)/shard_map/ppermute | solution.py:227
  139.2 0.1 fusion.5
  139.3 1.7 %collective-permute-start.6 = (f32[16,4,128]{2,0,1:T(8,128)S(1)}, f32[16,4,128]{2,0,1:T(8,128)S(1)}, u32[]{:S(2)}, u32[]{:S(2)}) collective-permute-start(f32[16,4,128]{2,0,1:T(8,128)S(1)} %fusion.5), channel_id=1, source_target_pairs={{0,4},{1,5},{2,6},{3,7},{4,0},{5,1},{6,2},{7,3},{8,12},{9,13},{10,... | collective-permute-start | bytes 98312 | tf_op jit(solution)/shard_map/ppermute | solution.py:227
  141.0 2.3 %collective-permute-done.6 = f32[16,4,128]{2,0,1:T(8,128)S(1)} collective-permute-done((f32[16,4,128]{2,0,1:T(8,128)S(1)}, f32[16,4,128]{2,0,1:T(8,128)S(1)}, u32[]{:S(2)}, u32[]{:S(2)}) %collective-permute-start.6) | collective-permute-done | bytes 32800 | tf_op jit(solution)/shard_map/ppermute | solution.py:227
  143.3 4.0 %collective-permute-start.7 = (f32[16,4,128]{2,0,1:T(8,128)S(1)}, f32[16,4,128]{2,0,1:T(8,128)S(1)}, u32[]{:S(2)}, u32[]{:S(2)}) collective-permute-start(f32[16,4,128]{2,0,1:T(8,128)S(1)} %add.41), channel_id=1, source_target_pairs={{0,8},{1,9},{2,10},{3,11},{4,12},{5,13},{6,14},{7,15},{8,0},{9,1},... | collective-permute-start | bytes 98312 | tf_op jit(solution)/shard_map/ppermute | solution.py:227
  147.3 1.6 %copy-done.1 = bf16[16,512,128]{2,1,0:T(8,128)(2,1)S(1)} copy-done((bf16[16,512,128]{2,1,0:T(8,128)(2,1)S(1)}, bf16[16,512,128]{2,1,0:T(8,128)(2,1)}, u32[]{:S(2)}) %copy-start.1) | copy-done | bytes 2097176
  148.9 1.6 %unpack0.1 = (bf16[1,128,4096]{2,1,0:T(8,128)(2,1)}, bf16[1,128,4096]{2,1,0:T(8,128)(2,1)}, bf16[1,128,4096]{2,1,0:T(8,128)(2,1)}, bf16[1,128,4096]{2,1,0:T(8,128)(2,1)}) custom-call(bf16[16,512,128]{2,1,0:T(8,128)(2,1)S(1)} %copy-done.1), custom_call_target="tpu_custom_call" | custom-call | bytes 8388608 | tf_op jit(solution)/shard_map/unpack0/pallas_call | solution.py:53
  150.5 0.6 fusion.4
  151.1 1.6 %unpack1.1 = (bf16[1,128,4096]{2,1,0:T(8,128)(2,1)}, bf16[1,128,4096]{2,1,0:T(8,128)(2,1)}, bf16[1,128,4096]{2,1,0:T(8,128)(2,1)}, bf16[1,128,4096]{2,1,0:T(8,128)(2,1)}) custom-call(bf16[16,512,128]{2,1,0:T(8,128)(2,1)S(1)} %all-to-all-done.3.recv_ref, ...), custom_call_target="tpu_custom_call", output_to_operand_aliasing={{0}: (1, {}), {1}: (2, {}), {2}: (3, {}), {3}: (4, {})} | custom-call | bytes 8388608 | tf_op jit(solution)/shard_map/unpack1/pallas_call | solution.py:53
  (26 shorter events, 0.3 us)
Async XLA Ops:
  3.3 37.4 %all-to-all-start = ((bf16[16,512,128]{2,1,0:T(8,128)(2,1)}), bf16[16,512,128]{2,1,0:T(8,128)(2,1)S(1)}, u32[]{:S(2)}, u32[]{:S(2)}) async-start(bf16[16,512,128]{2,1,0:T(8,128)(2,1)} %pack0.1), calls=%async_computation | async-start | bytes 4194304 | tf_op jit(solution)/shard_map/all_to_all | solution.py:221
  10.4 2.8 %copy-start.6 = (s32[32,8]{0,1:T(8,128)S(1)}, s32[32,8]{0,1:T(8,128)}, u32[]{:S(2)}) copy-start(s32[32,8]{0,1:T(8,128)} %param.13) | copy-start | bytes 3076
  10.4 2.8 %copy-start.4 = (f32[32,128]{1,0:T(8,128)S(1)}, f32[32,128]{1,0:T(8,128)}, u32[]{:S(2)}) copy-start(f32[32,128]{1,0:T(8,128)} %param.11) | copy-start | bytes 49156
  10.4 2.8 %copy-start.5 = (f32[32,128]{1,0:T(8,128)S(1)}, f32[32,128]{1,0:T(8,128)}, u32[]{:S(2)}) copy-start(f32[32,128]{1,0:T(8,128)} %param.12) | copy-start | bytes 49156
  40.8 32.1 %all-to-all-start.1 = ((bf16[16,512,128]{2,1,0:T(8,128)(2,1)}), bf16[16,512,128]{2,1,0:T(8,128)(2,1)}, u32[]{:S(2)}, u32[]{:S(2)}) async-start(bf16[16,512,128]{2,1,0:T(8,128)(2,1)} %pack1.1), calls=%async_computation.1 | async-start | bytes 4194304 | tf_op jit(solution)/shard_map/all_to_all | solution.py:221
  55.8 1.3 copy-start.3
  72.9 31.9 %all-to-all-start.2 = ((bf16[16,512,128]{2,1,0:T(8,128)(2,1)}), bf16[16,512,128]{2,1,0:T(8,128)(2,1)S(1)}, u32[]{:S(2)}, u32[]{:S(2)}) async-start(bf16[16,512,128]{2,1,0:T(8,128)(2,1)} %copy-done.3), calls=%async_computation.2 | async-start | bytes 4194304 | tf_op jit(solution)/shard_map/all_to_all | solution.py:221
  88.5 1.3 copy-start.2
  89.9 1.2 collective-permute-start
  91.0 3.7 %collective-permute-start.1 = (f32[4,128]{1,0:T(4,128)S(1)}, f32[4,128]{1,0:T(4,128)S(1)}, u32[]{:S(2)}, u32[]{:S(2)}) collective-permute-start(f32[4,128]{1,0:T(4,128)S(1)} %fusion.3), channel_id=1, source_target_pairs={{0,32},{16,48},{32,0},{48,16},{64,96},{80,112},{96,64},{112,80},{1... | collective-permute-start | bytes 6152 | tf_op jit(solution)/shard_map/ppermute | solution.py:227
  94.7 4.5 %collective-permute-start.2 = (f32[4,128]{1,0:T(4,128)S(1)}, f32[4,128]{1,0:T(4,128)S(1)}, u32[]{:S(2)}, u32[]{:S(2)}) collective-permute-start(f32[4,128]{1,0:T(4,128)S(1)} %add.36), channel_id=1, source_target_pairs={{0,64},{16,80},{32,96},{48,112},{64,0},{80,16},{96,32},{112,48},{1... | collective-permute-start | bytes 6152 | tf_op jit(solution)/shard_map/ppermute | solution.py:227
  104.8 1.3 copy-start
  106.1 45.0 %all-to-all-start.3 = ((bf16[16,512,128]{2,1,0:T(8,128)(2,1)}), bf16[16,512,128]{2,1,0:T(8,128)(2,1)S(1)}, u32[]{:S(2)}, u32[]{:S(2)}) async-start(bf16[16,512,128]{2,1,0:T(8,128)(2,1)} %copy-done.2), calls=%async_computation.3 | async-start | bytes 4194304 | tf_op jit(solution)/shard_map/all_to_all | solution.py:221
  110.4 7.6 %collective-permute-start.3 = (f32[4,128]{1,0:T(4,128)S(1)}, f32[4,128]{1,0:T(4,128)S(1)}, u32[]{:S(2)}, u32[]{:S(2)}) collective-permute-start(f32[4,128]{1,0:T(4,128)S(1)} %add.37), channel_id=1, source_target_pairs={{0,128},{16,144},{32,160},{48,176},{64,192},{80,208},{96,224},{112... | collective-permute-start | bytes 6152 | tf_op jit(solution)/shard_map/ppermute | solution.py:227
  118.1 15.6 %collective-permute-start.4 = (f32[16,4,128]{2,0,1:T(8,128)S(1)}, f32[16,4,128]{2,0,1:T(8,128)S(1)}, u32[]{:S(2)}, u32[]{:S(2)}) collective-permute-start(f32[16,4,128]{2,0,1:T(8,128)S(1)} %broadcast_select_fusion), channel_id=1, source_target_pairs={{0,1},{1,0},{2,3},{3,2},{4,5},{5,4},{6,7},{7,6},{8,9},{9,8},{10,11... | collective-permute-start | bytes 98312 | tf_op jit(solution)/shard_map/ppermute | solution.py:227
  133.8 5.4 %collective-permute-start.5 = (f32[16,4,128]{2,0,1:T(8,128)S(1)}, f32[16,4,128]{2,0,1:T(8,128)S(1)}, u32[]{:S(2)}, u32[]{:S(2)}) collective-permute-start(f32[16,4,128]{2,0,1:T(8,128)S(1)} %fusion), channel_id=1, source_target_pairs={{0,2},{1,3},{2,0},{3,1},{4,6},{5,7},{6,4},{7,5},{8,10},{9,11},{10,... | collective-permute-start | bytes 98312 | tf_op jit(solution)/shard_map/ppermute | solution.py:227
  139.3 4.0 %collective-permute-start.6 = (f32[16,4,128]{2,0,1:T(8,128)S(1)}, f32[16,4,128]{2,0,1:T(8,128)S(1)}, u32[]{:S(2)}, u32[]{:S(2)}) collective-permute-start(f32[16,4,128]{2,0,1:T(8,128)S(1)} %fusion.5), channel_id=1, source_target_pairs={{0,4},{1,5},{2,6},{3,7},{4,0},{5,1},{6,2},{7,3},{8,12},{9,13},{10,... | collective-permute-start | bytes 98312 | tf_op jit(solution)/shard_map/ppermute | solution.py:227
  143.3 7.2 %collective-permute-start.7 = (f32[16,4,128]{2,0,1:T(8,128)S(1)}, f32[16,4,128]{2,0,1:T(8,128)S(1)}, u32[]{:S(2)}, u32[]{:S(2)}) collective-permute-start(f32[16,4,128]{2,0,1:T(8,128)S(1)} %add.41), channel_id=1, source_target_pairs={{0,8},{1,9},{2,10},{3,11},{4,12},{5,13},{6,14},{7,15},{8,0},{9,1},... | collective-permute-start | bytes 98312 | tf_op jit(solution)/shard_map/ppermute | solution.py:227
  147.3 1.6 %copy-start.1 = (bf16[16,512,128]{2,1,0:T(8,128)(2,1)S(1)}, bf16[16,512,128]{2,1,0:T(8,128)(2,1)}, u32[]{:S(2)}) copy-start(bf16[16,512,128]{2,1,0:T(8,128)(2,1)} %copy-done) | copy-start | bytes 6291460

commit v3 on v2

--- a/solution.py
+++ b/solution.py
@@ -20,6 +20,7 @@
 SCALE = HEAD**-0.5
 LOG2E = 1.4426950408889634
 AT_ONCE = 8
+EXTRA = 16
 
 
 def pack_kernel(q_ref, k_ref, v_ref, g_ref, send_ref):
@@ -43,25 +44,83 @@
 
 def unpack_kernel(recv_ref, *refs):
     first = pl.program_id(0) * AT_ONCE
-    for a, ref in enumerate(refs[-4:]):
+    for a, ref in enumerate(refs):
         for n in range(AT_ONCE):
             ref[0, :, n * HEAD : (n + 1) * HEAD] = recv_ref[first + n, a * TOK : (a + 1) * TOK, :]
 
 
-def unpack(chunk, recv, before):
+def last_unpack_kernel(factor, recv_ref, *refs):
+    outs, query_gain_ref, key_gain_ref = refs[4:8], refs[8], refs[9]
+    first = pl.program_id(0) * AT_ONCE
+    for a, ref in enumerate(outs):
+        for n in range(AT_ONCE):
+            ref[0, :, n * HEAD : (n + 1) * HEAD] = recv_ref[first + n, a * TOK : (a + 1) * TOK, :]
+
+    @pl.when(pl.program_id(0) == 0)
+    def _():
+        terms = recv_ref[:, 4 * TOK :, :].astype(jnp.float32)
+        for c in range(CHUNKS):
+            for k, ref in enumerate((query_gain_ref, key_gain_ref)):
+                row = 2 * c + k
+                total = terms[:, row] + terms[:, 4 + row] + terms[:, 8 + row]
+                ref[c * SEQ : (c + 1) * SEQ, :] = total * factor
+
+
+def unpack(recv):
     steps = SEQ // AT_ONCE
     return pl.pallas_call(
         unpack_kernel,
         grid=(steps,),
         out_shape=(jax.ShapeDtypeStruct((1, TOK, HEADS * HEAD), jnp.bfloat16),) * 4,
-        in_specs=[pl.BlockSpec(memory_space=pltpu.VMEM)]
-        + [pl.BlockSpec(memory_space=pl.ANY)] * len(before),
-        out_specs=(pl.BlockSpec((1, TOK, AT_ONCE * HEAD), lambda i: (0, 0, chunk * steps + i)),) * 4,
-        input_output_aliases={i + 1: i for i in range(len(before))},
+        in_specs=[pl.BlockSpec(memory_space=pltpu.VMEM)],
+        out_specs=(pl.BlockSpec((1, TOK, AT_ONCE * HEAD), lambda i: (0, 0, i)),) * 4,
+        cost_estimate=pl.CostEstimate(flops=0, bytes_accessed=8 << 20, transcendentals=0),
+        name="unpack0",
+    )(recv)
+
+
+def last_unpack(factor, recv, before):
+    steps = SEQ // AT_ONCE
+    gain = jax.ShapeDtypeStruct((HEADS, HEAD), jnp.float32)
+    return pl.pallas_call(
+        functools.partial(last_unpack_kernel, factor),
+        grid=(steps,),
+        out_shape=(jax.ShapeDtypeStruct((1, TOK, HEADS * HEAD), jnp.bfloat16),) * 4 + (gain, gain),
+        in_specs=[pl.BlockSpec(memory_space=pltpu.VMEM)] + [pl.BlockSpec(memory_space=pl.ANY)] * 4,
+        out_specs=(pl.BlockSpec((1, TOK, AT_ONCE * HEAD), lambda i: (0, 0, steps + i)),) * 4
+        + (pl.BlockSpec((HEADS, HEAD), lambda i: (0, 0)),) * 2,
+        input_output_aliases={i + 1: i for i in range(4)},
         compiler_params=pltpu.CompilerParams(vmem_limit_bytes=24 << 20),
         cost_estimate=pl.CostEstimate(flops=0, bytes_accessed=8 << 20, transcendentals=0),
-        name=f"unpack{chunk}",
+        name="unpack1",
     )(recv, *before)
+
+
+def attach_kernel(part_ref, _, send_ref, rows_ref, sem):
+    part = part_ref[...]
+    high = part.astype(jnp.bfloat16)
+    rest = part - high.astype(jnp.float32)
+    middle = rest.astype(jnp.bfloat16)
+    low = (rest - middle.astype(jnp.float32)).astype(jnp.bfloat16)
+    blank = jnp.zeros((EXTRA - 12, HEAD), jnp.bfloat16)
+    rows = jnp.concatenate([high, middle, low, blank], axis=0)
+    rows_ref[...] = jnp.broadcast_to(rows[None], (SEQ, EXTRA, HEAD))
+    copy = pltpu.make_async_copy(rows_ref, send_ref.at[:, pl.ds(4 * TOK, EXTRA), :], sem)
+    copy.start()
+    copy.wait()
+
+
+def attach(part, send):
+    return pl.pallas_call(
+        attach_kernel,
+        out_shape=pltpu.HBM(send.shape, send.dtype),
+        in_specs=[pl.BlockSpec(memory_space=pltpu.VMEM), pl.BlockSpec(memory_space=pltpu.HBM)],
+        out_specs=pl.BlockSpec(memory_space=pltpu.HBM),
+        input_output_aliases={1: 0},
+        scratch_shapes=[pltpu.VMEM((SEQ, EXTRA, HEAD), jnp.bfloat16), pltpu.SemaphoreType.DMA],
+        cost_estimate=pl.CostEstimate(flops=0, bytes_accessed=1 << 17, transcendentals=0),
+        name="attach",
+    )(part, send)
 
 
 def dot(a, b, ca, cb):
@@ -82,7 +141,22 @@
 
 
 def attend_kernel(
-    ids_ref, gains_ref, recv_ref, back_ref, gain_ref, kv_ref, qg_ref, sum_ref, prod_a, prod_b, mix_a, mix_b, *, group
+    ids_ref,
+    gains_ref,
+    recv_ref,
+    sent_ref,
+    gain_ref,
+    back_ref,
+    kv_ref,
+    qg_ref,
+    sum_ref,
+    prod_a,
+    prod_b,
+    mix_a,
+    mix_b,
+    sems,
+    *,
+    group,
 ):
     query_gain = gains_ref[0:1, :]
     key_gain = gains_ref[1:2, :]
@@ -168,6 +242,14 @@
     query_total = spread(units - 2, 0, query_total)
     query_total = spread(units - 1, 1, query_total)
 
+    def leave(half):
+        rows = pl.ds(half * 2 * TOK, 2 * TOK)
+        return pltpu.make_async_copy(
+            back_ref.at[:, rows, :], sent_ref.at[:, rows, :], sems.at[half]
+        )
+
+    leave(0).start()
+
     def finish(s, total):
         rows = pl.ds(pl.multiple_of(s * TOK, TOK), TOK)
         x = recv_ref[s, TOK : 2 * TOK, :].astype(jnp.float32)
@@ -178,15 +260,18 @@
         return total + gain_term.reshape(TOK // 8, 8, HEAD).sum(0)
 
     key_total = lax.fori_loop(0, SEQ, finish, jnp.zeros((8, HEAD), jnp.float32), unroll=4)
+    leave(1).start()
     gain_ref[0:1, :] = jnp.sum(query_total, axis=0, keepdims=True)
     gain_ref[1:2, :] = jnp.sum(key_total, axis=0, keepdims=True)
-
-
-def attend(chunk, ids, gains, recv, group=2):
+    leave(0).wait()
+    leave(1).wait()
+
+
+def attend(chunk, ids, gains, recv, extra=0, group=2):
     return pl.pallas_call(
         functools.partial(attend_kernel, group=group),
         out_shape=(
-            jax.ShapeDtypeStruct((SEQ, 4 * TOK, HEAD), jnp.bfloat16),
+            pltpu.HBM((SEQ, 4 * TOK + extra, HEAD), jnp.bfloat16),
             jax.ShapeDtypeStruct((2, HEAD), jnp.float32),
         ),
         in_specs=[
@@ -195,10 +280,11 @@
             pl.BlockSpec(memory_space=pltpu.VMEM),
         ],
         out_specs=(
-            pl.BlockSpec(memory_space=pltpu.VMEM),
+            pl.BlockSpec(memory_space=pltpu.HBM),
             pl.BlockSpec(memory_space=pltpu.VMEM),
         ),
         scratch_shapes=[
+            pltpu.VMEM((SEQ, 4 * TOK, HEAD), jnp.bfloat16),
             pltpu.VMEM((TOKENS, 2 * HEAD), jnp.bfloat16),
             pltpu.VMEM((NB, 2 * BLOCK, 2 * HEAD), jnp.bfloat16),
             pltpu.VMEM((TOKENS, 2 * HEAD), jnp.float32),
@@ -206,6 +292,7 @@
             pltpu.VMEM((group, 2 * BLOCK, SLOTS * BLOCK), jnp.float32),
             pltpu.VMEM((group, 2 * BLOCK, SLOTS * BLOCK), jnp.bfloat16),
             pltpu.VMEM((group, 2 * BLOCK, SLOTS * BLOCK), jnp.bfloat16),
+            pltpu.SemaphoreType.DMA((2,)),
         ],
         compiler_params=pltpu.CompilerParams(vmem_limit_bytes=32 << 20),
         cost_estimate=pl.CostEstimate(
@@ -221,10 +308,11 @@
     return lax.all_to_all(x, axis, split_axis=0, concat_axis=0, tiled=True)
 
 
-def summed(x, axis, steps):
-    size = lax.axis_size(axis)
-    for step in steps:
+def summed(x, axis):
+    size, step = lax.axis_size(axis), 1
+    while step < size:
         x = x + lax.ppermute(x, axis, [(i, i ^ step) for i in range(size)])
+        step *= 2
     return x
 
 
@@ -242,19 +330,12 @@
     back0, gain0 = attend(0, block_ids, gains[0], in0)
     back0, in1 = lax.optimization_barrier((back0, in1))
     out0 = swap(back0, "seq")
-    back1, gain1 = attend(1, block_ids, gains[1], in1)
-    part = summed(jnp.concatenate([gain0, gain1], axis=0), "dp", (1, 2, 4))
-    back1, part, out0 = lax.optimization_barrier((back1, part, out0))
+    back1, gain1 = attend(1, block_ids, gains[1], in1, EXTRA)
+    part = summed(jnp.concatenate([gain0, gain1], axis=0), "dp")
+    back1 = attach(part, back1)
     out1 = swap(back1, "seq")
-    done = unpack(0, out0, ())
-    done = unpack(1, out1, tuple(done))
-    part = summed(part, "dp", (8,))
-    mine = lax.broadcasted_iota(jnp.int32, (SEQ, 1, 1), 0) == s
-    every = summed(jnp.where(mine, part[None], 0.0), "seq", (1, 2, 4, 8))
     factor = (TOKENS * lax.axis_size("dp")) ** -0.5
-    every = jnp.transpose(every.reshape(SEQ, CHUNKS, 2, HEAD), (2, 1, 0, 3)) * factor
-    every = every.reshape(2, HEADS, HEAD)
-    return (*done, every[0], every[1])
+    return tuple(last_unpack(factor, out1, unpack(out0)))
 
 
 def solution(mesh):

time: 153 us -> 148 us (0.967)
  Pallas kernels: 30.7 us -> 35.7 us
  local copies, waits for them, and re-layouts: 6.24 us -> 1.38 us
  starting transfers between devices: 30.3 us -> 25.6 us
  waiting for transfers between devices: 84.5 us -> 82.8 us
    ppermute x8 -> x4, waiting for transfers between devices: 35.7 us -> 14.2 us  [summed(): x = x + lax.ppermute(x, axis, [(i, i ^ step) for i in range(size)])]
    all_to_all x4, waiting for transfers between devices: 48.8 us -> 68.6 us  [swap(): return lax.all_to_all(x, axis, split_axis=0, concat_axis=0, tiled=True)]
    ppermute x8 -> x4, starting transfers between devices: 10.3 us -> 2.67 us  [summed(): x = x + lax.ppermute(x, axis, [(i, i ^ step) for i in range(size)])]
    unnamed x15 -> x9, local copies, waits for them, and re-layouts: 5.63 us -> 1.38 us
    pallas_call x0 -> x2, Pallas kernels: none -> 2.94 us  [the longest x1 1.61 us: last_unpack(): pl.pallas_call(functools.partial(last_unpack_kernel, factor), grid=(steps...]
    all_to_all x4, starting transfers between devices: 20 us -> 22.9 us  [swap(): return lax.all_to_all(x, axis, split_axis=0, concat_axis=0, tiled=True)]
    pallas_call x2, Pallas kernels: 22 us -> 24.1 us  [attend(): pl.pallas_call(functools.partial(attend_kernel, group=group), out_shape=(...]
    pallas_call x2 -> x1, Pallas kernels: 3.19 us -> 3.21 us  [unpack(): pl.pallas_call(unpack_kernel, grid=(steps,), out_shape=(jax.ShapeDtypeStr...]
  transfers between devices with their start and end apart: 12 -> 8, of which waited for: 10 -> 7; matrix products, arithmetic and copies ran while one was open for 1% -> 0% of each run, Pallas kernels for 17% -> 21%
where the time goes in v3:
time: 148 us; the launch traced here: 147 us
  waiting for transfers between devices  82.8 us (56%)
  Pallas kernels  35.7 us (24%)
  starting transfers between devices  25.6 us (17%)
    all_to_all x4, waiting for transfers between devices, swap(): return lax.all_to_all(x, axis, split_axis=0, concat_axis=0, tiled=True)  68.6 us
    pallas_call x2, Pallas kernels, attend(): pl.pallas_call(functools.partial(attend_kernel, group=group), out_shape=(...  24.1 us
    all_to_all x4, starting transfers between devices, swap(): return lax.all_to_all(x, axis, split_axis=0, concat_axis=0, tiled=True)  22.9 us
    ppermute x4, waiting for transfers between devices, summed(): x = x + lax.ppermute(x, axis, [(i, i ^ step) for i in range(size)])  14.2 us
    pallas_call x2, Pallas kernels, pack(): pl.pallas_call(pack_kernel, grid=(steps,), out_shape=jax.ShapeDtypeStruct...  5.45 us
    pallas_call x1, Pallas kernels, unpack(): pl.pallas_call(unpack_kernel, grid=(steps,), out_shape=(jax.ShapeDtypeStr...  3.21 us
  transfers between devices with their start and end apart: 8, of which 7 were waited for; matrix products, arithmetic and copies ran while one was open for 0% of the time, Pallas kernels for 21%

profile of v3, /device:TPU:128, one launch (start us, length us, event | category | flops | bytes accessed | tf_op | source)
XLA Modules:
  0.0 146.9 jit_solution(14634139206655551133)
XLA Ops:
  0.6 2.7 %pack0.1 = bf16[16,512,128]{2,1,0:T(8,128)(2,1)} custom-call(bf16[1,128,4096]{2,1,0:T(8,128)(2,1)} %q_ref.3, bf16[1,128,4096]{2,1,0:T(8,128)(2,1)} %k_ref.3, bf16[1,128,4096]{2,1,0:T(8,128)(2,1)} %v_ref.3, bf16[1,128,4096]{2,1,0:T(8,128)(2,1)} %g_ref.3), custom_call_target="tpu_custom_call" | custom-call | bytes 8388608 | tf_op jit(solution)/shard_map/pack0/pallas_call | solution.py:34
  3.3 7.0 %all-to-all-start = ((bf16[16,512,128]{2,1,0:T(8,128)(2,1)}), bf16[16,512,128]{2,1,0:T(8,128)(2,1)S(1)}, u32[]{:S(2)}, u32[]{:S(2)}) async-start(bf16[16,512,128]{2,1,0:T(8,128)(2,1)} %pack0.1), calls=%async_computation | async-start | bytes 4194304 | tf_op jit(solution)/shard_map/all_to_all | solution.py:308
  10.4 0.0 copy-start.3
  10.4 0.0 copy-start.1
  10.4 0.0 copy-start.2
  10.4 2.7 %pack1.1 = bf16[16,512,128]{2,1,0:T(8,128)(2,1)} custom-call(bf16[1,128,4096]{2,1,0:T(8,128)(2,1)} %q_ref.3, bf16[1,128,4096]{2,1,0:T(8,128)(2,1)} %k_ref.3, bf16[1,128,4096]{2,1,0:T(8,128)(2,1)} %v_ref.3, bf16[1,128,4096]{2,1,0:T(8,128)(2,1)} %g_ref.3), custom_call_target="tpu_custom_call" | custom-call | bytes 8388608 | tf_op jit(solution)/shard_map/pack1/pallas_call | solution.py:34
  13.2 0.0 copy-done.3
  13.2 0.1 copy.18.ids_ref
  13.2 0.0 copy-done.1
  13.2 0.0 copy-done.2
  13.3 27.5 %all-to-all-done.recv_ref = bf16[16,512,128]{2,1,0:T(8,128)(2,1)S(1)} async-done(((bf16[16,512,128]{2,1,0:T(8,128)(2,1)}), bf16[16,512,128]{2,1,0:T(8,128)(2,1)S(1)}, u32[]{:S(2)}, u32[]{:S(2)}) %all-to-all-start) | async-done | bytes 2097184 | tf_op jit(solution)/shard_map/all_to_all | solution.py:308
  40.8 4.4 %all-to-all-start.1 = ((bf16[16,512,128]{2,1,0:T(8,128)(2,1)}), bf16[16,512,128]{2,1,0:T(8,128)(2,1)}, u32[]{:S(2)}, u32[]{:S(2)}) async-start(bf16[16,512,128]{2,1,0:T(8,128)(2,1)} %pack1.1), calls=%async_computation.1 | async-start | bytes 4194304 | tf_op jit(solution)/shard_map/all_to_all | solution.py:308
  45.2 11.6 %attend0.1 = (bf16[16,512,128]{2,1,0:T(8,128)(2,1)}, f32[2,128]{1,0:T(2,128)S(1)}) custom-call(s32[32,8]{1,0:T(8,128)S(1)} %copy.18.ids_ref, f32[2,128]{1,0:T(2,128)S(1)} %bitcast.5, bf16[16,512,128]{2,1,0:T(8,128)(2,1)S(1)} %all-to-all-done.recv_ref), custom_call_target="tpu_custom_call" | custom-call | flops 24999999488 | bytes 4194304 | tf_op jit(solution)/shard_map/attend0/pallas_call | solution.py:271
  56.9 16.0 %all-to-all-done.1.recv_ref = bf16[16,512,128]{2,1,0:T(8,128)(2,1)} async-done(((bf16[16,512,128]{2,1,0:T(8,128)(2,1)}), bf16[16,512,128]{2,1,0:T(8,128)(2,1)}, u32[]{:S(2)}, u32[]{:S(2)}) %all-to-all-start.1) | async-done | bytes 2097184 | tf_op jit(solution)/shard_map/all_to_all | solution.py:308
  72.9 4.2 %all-to-all-start.3 = ((bf16[16,512,128]{2,1,0:T(8,128)(2,1)}), bf16[16,512,128]{2,1,0:T(8,128)(2,1)S(1)}, u32[]{:S(2)}, u32[]{:S(2)}) async-start(bf16[16,512,128]{2,1,0:T(8,128)(2,1)} %get-tuple-element.25), calls=%async_computation.3 | async-start | bytes 4194304 | tf_op jit(solution)/shard_map/all_to_all | solution.py:308
  77.1 12.5 %attend1.1 = (bf16[16,528,128]{2,1,0:T(8,128)(2,1)}, f32[2,128]{1,0:T(2,128)S(1)}) custom-call(s32[32,8]{1,0:T(8,128)S(1)} %copy.18.ids_ref, f32[2,128]{1,0:T(2,128)S(1)} %bitcast.4, bf16[16,512,128]{2,1,0:T(8,128)(2,1)} %all-to-all-done.1.recv_ref), custom_call_target="tpu_custom_call" | custom-call | flops 24999999488 | bytes 4194304 | tf_op jit(solution)/shard_map/attend1/pallas_call | solution.py:271
  89.6 0.1 collective-permute-start
  89.7 1.1 collective-permute-done
  90.9 1.1 collective-permute-start.1
  92.0 2.6 %collective-permute-done.1 = f32[4,128]{1,0:T(4,128)S(1)} collective-permute-done((f32[4,128]{1,0:T(4,128)S(1)}, f32[4,128]{1,0:T(4,128)S(1)}, u32[]{:S(2)}, u32[]{:S(2)}) %collective-permute-start.1) | collective-permute-done | bytes 2080 | tf_op jit(solution)/shard_map/ppermute | solution.py:314
  94.6 1.5 %collective-permute-start.2 = (f32[4,128]{1,0:T(4,128)S(1)}, f32[4,128]{1,0:T(4,128)S(1)}, u32[]{:S(2)}, u32[]{:S(2)}) collective-permute-start(f32[4,128]{1,0:T(4,128)S(1)} %add.24), channel_id=1, source_target_pairs={{0,64},{16,80},{32,96},{48,112},{64,0},{80,16},{96,32},{112,48},{1... | collective-permute-start | bytes 6152 | tf_op jit(solution)/shard_map/ppermute | solution.py:314
  96.0 3.0 %collective-permute-done.2 = f32[4,128]{1,0:T(4,128)S(1)} collective-permute-done((f32[4,128]{1,0:T(4,128)S(1)}, f32[4,128]{1,0:T(4,128)S(1)}, u32[]{:S(2)}, u32[]{:S(2)}) %collective-permute-start.2) | collective-permute-done | bytes 2080 | tf_op jit(solution)/shard_map/ppermute | solution.py:314
  99.0 0.0 collective-permute-start.3
  99.0 7.5 %collective-permute-done.3 = f32[4,128]{1,0:T(4,128)S(1)} collective-permute-done((f32[4,128]{1,0:T(4,128)S(1)}, f32[4,128]{1,0:T(4,128)S(1)}, u32[]{:S(2)}, u32[]{:S(2)}) %collective-permute-start.3) | collective-permute-done | bytes 2080 | tf_op jit(solution)/shard_map/ppermute | solution.py:314
  106.5 0.6 add.26.part_ref
  107.1 1.3 attach.1
  108.5 0.0 all-to-all-done.3.recv_ref
  108.5 1.3 copy-done
  109.8 7.2 %all-to-all-start.2 = ((bf16[16,528,128]{2,1,0:T(8,128)(2,1)}), bf16[16,528,128]{2,1,0:T(8,128)(2,1)S(1)}, u32[]{:S(2)}, u32[]{:S(2)}) async-start(bf16[16,528,128]{2,1,0:T(8,128)(2,1)} %attach.1), calls=%async_computation.2 | async-start | bytes 4325376 | tf_op jit(solution)/shard_map/all_to_all | solution.py:308
  117.0 3.2 %unpack0.1 = (bf16[1,128,4096]{2,1,0:T(8,128)(2,1)}, bf16[1,128,4096]{2,1,0:T(8,128)(2,1)}, bf16[1,128,4096]{2,1,0:T(8,128)(2,1)}, bf16[1,128,4096]{2,1,0:T(8,128)(2,1)}) custom-call(bf16[16,512,128]{2,1,0:T(8,128)(2,1)} %copy-done), custom_call_target="tpu_custom_call" | custom-call | bytes 8388608 | tf_op jit(solution)/shard_map/unpack0/pallas_call | solution.py:71
  120.2 25.1 %all-to-all-done.2.recv_ref = bf16[16,528,128]{2,1,0:T(8,128)(2,1)S(1)} async-done(((bf16[16,528,128]{2,1,0:T(8,128)(2,1)}), bf16[16,528,128]{2,1,0:T(8,128)(2,1)S(1)}, u32[]{:S(2)}, u32[]{:S(2)}) %all-to-all-start.2) | async-done | bytes 2162720 | tf_op jit(solution)/shard_map/all_to_all | solution.py:308
  145.3 1.6 %unpack1.1 = (bf16[1,128,4096]{2,1,0:T(8,128)(2,1)}, bf16[1,128,4096]{2,1,0:T(8,128)(2,1)}, bf16[1,128,4096]{2,1,0:T(8,128)(2,1)}, bf16[1,128,4096]{2,1,0:T(8,12...) custom-call(bf16[16,528,128]{2,1,0:T(8,128)(2,1)S(1)} %all-to-all-do, ...), custom_call_target="tpu_custom_call", output_to_operand_aliasing={{0}: (1, {}), {1}: (2, {}), {2}: (3, {}), {3}: (4, {})} | custom-call | bytes 8388608 | tf_op jit(solution)/shard_map/unpack1/pallas_call | solution.py:85
  (6 shorter events, 0.0 us)
Async XLA Ops:
  3.3 37.4 %all-to-all-start = ((bf16[16,512,128]{2,1,0:T(8,128)(2,1)}), bf16[16,512,128]{2,1,0:T(8,128)(2,1)S(1)}, u32[]{:S(2)}, u32[]{:S(2)}) async-start(bf16[16,512,128]{2,1,0:T(8,128)(2,1)} %pack0.1), calls=%async_computation | async-start | bytes 4194304 | tf_op jit(solution)/shard_map/all_to_all | solution.py:308
  10.4 2.8 %copy-start.3 = (s32[32,8]{0,1:T(8,128)S(1)}, s32[32,8]{0,1:T(8,128)}, u32[]{:S(2)}) copy-start(s32[32,8]{0,1:T(8,128)} %param.13) | copy-start | bytes 3076
  10.4 2.8 %copy-start.1 = (f32[32,128]{1,0:T(8,128)S(1)}, f32[32,128]{1,0:T(8,128)}, u32[]{:S(2)}) copy-start(f32[32,128]{1,0:T(8,128)} %param.11) | copy-start | bytes 49156
  10.4 2.8 %copy-start.2 = (f32[32,128]{1,0:T(8,128)S(1)}, f32[32,128]{1,0:T(8,128)}, u32[]{:S(2)}) copy-start(f32[32,128]{1,0:T(8,128)} %param.12) | copy-start | bytes 49156
  40.8 32.1 %all-to-all-start.1 = ((bf16[16,512,128]{2,1,0:T(8,128)(2,1)}), bf16[16,512,128]{2,1,0:T(8,128)(2,1)}, u32[]{:S(2)}, u32[]{:S(2)}) async-start(bf16[16,512,128]{2,1,0:T(8,128)(2,1)} %pack1.1), calls=%async_computation.1 | async-start | bytes 4194304 | tf_op jit(solution)/shard_map/all_to_all | solution.py:308
  72.9 35.6 %all-to-all-start.3 = ((bf16[16,512,128]{2,1,0:T(8,128)(2,1)}), bf16[16,512,128]{2,1,0:T(8,128)(2,1)S(1)}, u32[]{:S(2)}, u32[]{:S(2)}) async-start(bf16[16,512,128]{2,1,0:T(8,128)(2,1)} %get-tuple-element.25), calls=%async_computation.3 | async-start | bytes 4194304 | tf_op jit(solution)/shard_map/all_to_all | solution.py:308
  89.6 1.2 collective-permute-start
  90.9 3.7 %collective-permute-start.1 = (f32[4,128]{1,0:T(4,128)S(1)}, f32[4,128]{1,0:T(4,128)S(1)}, u32[]{:S(2)}, u32[]{:S(2)}) collective-permute-start(f32[4,128]{1,0:T(4,128)S(1)} %fusion.2), channel_id=1, source_target_pairs={{0,32},{16,48},{32,0},{48,16},{64,96},{80,112},{96,64},{112,80},{1... | collective-permute-start | bytes 6152 | tf_op jit(solution)/shard_map/ppermute | solution.py:314
  94.6 4.5 %collective-permute-start.2 = (f32[4,128]{1,0:T(4,128)S(1)}, f32[4,128]{1,0:T(4,128)S(1)}, u32[]{:S(2)}, u32[]{:S(2)}) collective-permute-start(f32[4,128]{1,0:T(4,128)S(1)} %add.24), channel_id=1, source_target_pairs={{0,64},{16,80},{32,96},{48,112},{64,0},{80,16},{96,32},{112,48},{1... | collective-permute-start | bytes 6152 | tf_op jit(solution)/shard_map/ppermute | solution.py:314
  99.0 7.5 %collective-permute-start.3 = (f32[4,128]{1,0:T(4,128)S(1)}, f32[4,128]{1,0:T(4,128)S(1)}, u32[]{:S(2)}, u32[]{:S(2)}) collective-permute-start(f32[4,128]{1,0:T(4,128)S(1)} %add.25), channel_id=1, source_target_pairs={{0,128},{16,144},{32,160},{48,176},{64,192},{80,208},{96,224},{112... | collective-permute-start | bytes 6152 | tf_op jit(solution)/shard_map/ppermute | solution.py:314
  108.5 1.3 copy-start
  109.8 35.5 %all-to-all-start.2 = ((bf16[16,528,128]{2,1,0:T(8,128)(2,1)}), bf16[16,528,128]{2,1,0:T(8,128)(2,1)S(1)}, u32[]{:S(2)}, u32[]{:S(2)}) async-start(bf16[16,528,128]{2,1,0:T(8,128)(2,1)} %attach.1), calls=%async_computation.2 | async-start | bytes 4325376 | tf_op jit(solution)/shard_map/all_to_all | solution.py:308

commit v4 on v3

--- a/solution.py
+++ b/solution.py
@@ -20,23 +20,51 @@
 SCALE = HEAD**-0.5
 LOG2E = 1.4426950408889634
 AT_ONCE = 8
+PACKED = 4
 EXTRA = 16
 
 
-def pack_kernel(q_ref, k_ref, v_ref, g_ref, send_ref):
-    for a, ref in enumerate((q_ref, k_ref, v_ref, g_ref)):
-        for n in range(AT_ONCE):
-            send_ref[n, a * TOK : (a + 1) * TOK, :] = ref[0, :, n * HEAD : (n + 1) * HEAD]
+def pack_kernel(chunk, q_ref, k_ref, v_ref, g_ref, send_ref, held_ref, in_sems, out_sems):
+    def fetch(part):
+        for n in range(part * PACKED, (part + 1) * PACKED):
+            columns = pl.ds((chunk * SEQ + n) * HEAD, HEAD)
+            for a, ref in enumerate((q_ref, k_ref, v_ref, g_ref)):
+                pltpu.make_async_copy(
+                    ref.at[0, :, columns],
+                    held_ref.at[n, pl.ds(a * TOK, TOK), :],
+                    in_sems.at[part],
+                ).start()
+
+    def whole(part):
+        return held_ref.at[pl.ds(part * PACKED, PACKED)]
+
+    def leave(part):
+        return pltpu.make_async_copy(
+            whole(part), send_ref.at[pl.ds(part * PACKED, PACKED)], out_sems.at[part]
+        )
+
+    parts = SEQ // PACKED
+    for part in range(parts):
+        fetch(part)
+    for part in range(parts):
+        pltpu.make_async_copy(whole(part), whole(part), in_sems.at[part]).wait()
+        leave(part).start()
+    for part in range(parts):
+        leave(part).wait()
 
 
 def pack(chunk, arrays):
-    steps = SEQ // AT_ONCE
-    return pl.pallas_call(
-        pack_kernel,
-        grid=(steps,),
-        out_shape=jax.ShapeDtypeStruct((SEQ, 4 * TOK, HEAD), jnp.bfloat16),
-        in_specs=[pl.BlockSpec((1, TOK, AT_ONCE * HEAD), lambda i: (0, 0, chunk * steps + i))] * 4,
-        out_specs=pl.BlockSpec((AT_ONCE, 4 * TOK, HEAD), lambda i: (i, 0, 0)),
+    parts = SEQ // PACKED
+    return pl.pallas_call(
+        functools.partial(pack_kernel, chunk),
+        out_shape=pltpu.HBM((SEQ, 4 * TOK, HEAD), jnp.bfloat16),
+        in_specs=[pl.BlockSpec(memory_space=pl.ANY)] * 4,
+        out_specs=pl.BlockSpec(memory_space=pl.ANY),
+        scratch_shapes=[
+            pltpu.VMEM((SEQ, 4 * TOK, HEAD), jnp.bfloat16),
+            pltpu.SemaphoreType.DMA((parts,)),
+            pltpu.SemaphoreType.DMA((parts,)),
+        ],
         cost_estimate=pl.CostEstimate(flops=0, bytes_accessed=8 << 20, transcendentals=0),
         name=f"pack{chunk}",
     )(*arrays)
@@ -96,8 +124,8 @@
     )(recv, *before)
 
 
-def attach_kernel(part_ref, _, send_ref, rows_ref, sem):
-    part = part_ref[...]
+def attach_kernel(part_ref, other_ref, _, send_ref, rows_ref, sem):
+    part = part_ref[...] + other_ref[...]
     high = part.astype(jnp.bfloat16)
     rest = part - high.astype(jnp.float32)
     middle = rest.astype(jnp.bfloat16)
@@ -110,17 +138,19 @@
     copy.wait()
 
 
-def attach(part, send):
+def attach(part, other, send):
     return pl.pallas_call(
         attach_kernel,
         out_shape=pltpu.HBM(send.shape, send.dtype),
-        in_specs=[pl.BlockSpec(memory_space=pltpu.VMEM), pl.BlockSpec(memory_space=pltpu.HBM)],
+        in_specs=[pl.BlockSpec(memory_space=pltpu.VMEM)] * 2
+        + [pl.BlockSpec(memory_space=pltpu.HBM)],
         out_specs=pl.BlockSpec(memory_space=pltpu.HBM),
-        input_output_aliases={1: 0},
+        input_output_aliases={2: 0},
         scratch_shapes=[pltpu.VMEM((SEQ, EXTRA, HEAD), jnp.bfloat16), pltpu.SemaphoreType.DMA],
+        compiler_params=pltpu.CompilerParams(vmem_limit_bytes=8 << 20),
         cost_estimate=pl.CostEstimate(flops=0, bytes_accessed=1 << 17, transcendentals=0),
         name="attach",
-    )(part, send)
+    )(part, other, send)
 
 
 def dot(a, b, ca, cb):
@@ -308,12 +338,8 @@
     return lax.all_to_all(x, axis, split_axis=0, concat_axis=0, tiled=True)
 
 
-def summed(x, axis):
-    size, step = lax.axis_size(axis), 1
-    while step < size:
-        x = x + lax.ppermute(x, axis, [(i, i ^ step) for i in range(size)])
-        step *= 2
-    return x
+def far(x, axis, step):
+    return lax.ppermute(x, axis, [(i, i ^ step) for i in range(lax.axis_size(axis))])
 
 
 def on_device(queries, keys, values, cotangent, query_gain, key_gain, block_ids):
@@ -331,8 +357,10 @@
     back0, in1 = lax.optimization_barrier((back0, in1))
     out0 = swap(back0, "seq")
     back1, gain1 = attend(1, block_ids, gains[1], in1, EXTRA)
-    part = summed(jnp.concatenate([gain0, gain1], axis=0), "dp")
-    back1 = attach(part, back1)
+    part = jnp.concatenate([gain0, gain1], axis=0)
+    for step in (1, 2, 4):
+        part = part + far(part, "dp", step)
+    back1 = attach(part, far(part, "dp", 8), back1)
     out1 = swap(back1, "seq")
     factor = (TOKENS * lax.axis_size("dp")) ** -0.5
     return tuple(last_unpack(factor, out1, unpack(out0)))

time: 148 us -> 147 us (level)
  no operation moved by 1% of the time
where the time goes in v4:
time: 147 us; the launch traced here: 145 us
  waiting for transfers between devices  83.1 us (57%)
  Pallas kernels  34.4 us (23%)
  starting transfers between devices  25.6 us (17%)
    all_to_all x4, waiting for transfers between devices, swap(): return lax.all_to_all(x, axis, split_axis=0, concat_axis=0, tiled=True)  68.9 us
    pallas_call x2, Pallas kernels, attend(): pl.pallas_call(functools.partial(attend_kernel, group=group), out_shape=(...  24.1 us
    all_to_all x4, starting transfers between devices, swap(): return lax.all_to_all(x, axis, split_axis=0, concat_axis=0, tiled=True)  22.9 us
    ppermute x4, waiting for transfers between devices, far(): lax.ppermute(x, axis, [(i, i ^ step) for i in range(lax.axis_size(axis))])  14.2 us
    pallas_call x2, Pallas kernels, pack(): pl.pallas_call(functools.partial(pack_kernel, chunk), out_shape=pltpu.HBM...  4.87 us
    pallas_call x1, Pallas kernels, unpack(): pl.pallas_call(unpack_kernel, grid=(steps,), out_shape=(jax.ShapeDtypeStr...  3.21 us
  transfers between devices with their start and end apart: 8, of which 7 were waited for; matrix products, arithmetic and copies ran while one was open for 0% of the time, Pallas kernels for 21%

profile of v4, /device:TPU:128, one launch (start us, length us, event | category | flops | bytes accessed | tf_op | source)
XLA Modules:
  0.0 145.4 jit_solution(18360473456849567718)
XLA Ops:
  0.6 2.4 %pack0.1 = bf16[16,512,128]{2,1,0:T(8,128)(2,1)} custom-call(bf16[1,128,4096]{2,1,0:T(8,128)(2,1)} %q_ref.3, bf16[1,128,4096]{2,1,0:T(8,128)(2,1)} %k_ref.3, bf16[1,128,4096]{2,1,0:T(8,128)(2,1)} %v_ref.3, bf16[1,128,4096]{2,1,0:T(8,128)(2,1)} %g_ref.3), custom_call_target="tpu_custom_call" | custom-call | bytes 8388608 | tf_op jit(solution)/shard_map/pack0/pallas_call | solution.py:58
  3.1 7.0 %all-to-all-start = ((bf16[16,512,128]{2,1,0:T(8,128)(2,1)}), bf16[16,512,128]{2,1,0:T(8,128)(2,1)S(1)}, u32[]{:S(2)}, u32[]{:S(2)}) async-start(bf16[16,512,128]{2,1,0:T(8,128)(2,1)} %pack0.1), calls=%async_computation | async-start | bytes 4194304 | tf_op jit(solution)/shard_map/all_to_all | solution.py:338
  10.1 0.0 copy-start.3
  10.1 0.0 copy-start.1
  10.1 0.0 copy-start.2
  10.2 2.4 %pack1.1 = bf16[16,512,128]{2,1,0:T(8,128)(2,1)} custom-call(bf16[1,128,4096]{2,1,0:T(8,128)(2,1)} %q_ref.3, bf16[1,128,4096]{2,1,0:T(8,128)(2,1)} %k_ref.3, bf16[1,128,4096]{2,1,0:T(8,128)(2,1)} %v_ref.3, bf16[1,128,4096]{2,1,0:T(8,128)(2,1)} %g_ref.3), custom_call_target="tpu_custom_call" | custom-call | bytes 8388608 | tf_op jit(solution)/shard_map/pack1/pallas_call | solution.py:58
  12.6 0.0 copy-done.3
  12.6 0.1 copy.18.ids_ref
  12.7 0.0 copy-done.1
  12.7 0.0 copy-done.2
  12.7 27.8 %all-to-all-done.recv_ref = bf16[16,512,128]{2,1,0:T(8,128)(2,1)S(1)} async-done(((bf16[16,512,128]{2,1,0:T(8,128)(2,1)}), bf16[16,512,128]{2,1,0:T(8,128)(2,1)S(1)}, u32[]{:S(2)}, u32[]{:S(2)}) %all-to-all-start) | async-done | bytes 2097184 | tf_op jit(solution)/shard_map/all_to_all | solution.py:338
  40.5 4.4 %all-to-all-start.1 = ((bf16[16,512,128]{2,1,0:T(8,128)(2,1)}), bf16[16,512,128]{2,1,0:T(8,128)(2,1)}, u32[]{:S(2)}, u32[]{:S(2)}) async-start(bf16[16,512,128]{2,1,0:T(8,128)(2,1)} %pack1.1), calls=%async_computation.1 | async-start | bytes 4194304 | tf_op jit(solution)/shard_map/all_to_all | solution.py:338
  45.0 11.6 %attend0.1 = (bf16[16,512,128]{2,1,0:T(8,128)(2,1)}, f32[2,128]{1,0:T(2,128)S(1)}) custom-call(s32[32,8]{1,0:T(8,128)S(1)} %copy.18.ids_ref, f32[2,128]{1,0:T(2,128)S(1)} %bitcast.5, bf16[16,512,128]{2,1,0:T(8,128)(2,1)S(1)} %all-to-all-done.recv_ref), custom_call_target="tpu_custom_call" | custom-call | flops 24999999488 | bytes 4194304 | tf_op jit(solution)/shard_map/attend0/pallas_call | solution.py:301
  56.6 16.0 %all-to-all-done.1.recv_ref = bf16[16,512,128]{2,1,0:T(8,128)(2,1)} async-done(((bf16[16,512,128]{2,1,0:T(8,128)(2,1)}), bf16[16,512,128]{2,1,0:T(8,128)(2,1)}, u32[]{:S(2)}, u32[]{:S(2)}) %all-to-all-start.1) | async-done | bytes 2097184 | tf_op jit(solution)/shard_map/all_to_all | solution.py:338
  72.6 4.2 %all-to-all-start.3 = ((bf16[16,512,128]{2,1,0:T(8,128)(2,1)}), bf16[16,512,128]{2,1,0:T(8,128)(2,1)S(1)}, u32[]{:S(2)}, u32[]{:S(2)}) async-start(bf16[16,512,128]{2,1,0:T(8,128)(2,1)} %get-tuple-element.25), calls=%async_computation.3 | async-start | bytes 4194304 | tf_op jit(solution)/shard_map/all_to_all | solution.py:338
  76.9 12.5 %attend1.1 = (bf16[16,528,128]{2,1,0:T(8,128)(2,1)}, f32[2,128]{1,0:T(2,128)S(1)}) custom-call(s32[32,8]{1,0:T(8,128)S(1)} %copy.18.ids_ref, f32[2,128]{1,0:T(2,128)S(1)} %bitcast.4, bf16[16,512,128]{2,1,0:T(8,128)(2,1)} %all-to-all-done.1.recv_ref), custom_call_target="tpu_custom_call" | custom-call | flops 24999999488 | bytes 4194304 | tf_op jit(solution)/shard_map/attend1/pallas_call | solution.py:301
  89.4 0.1 collective-permute-start
  89.5 1.1 collective-permute-done
  90.6 1.1 collective-permute-start.1
  91.7 2.6 %collective-permute-done.1 = f32[4,128]{1,0:T(4,128)S(1)} collective-permute-done((f32[4,128]{1,0:T(4,128)S(1)}, f32[4,128]{1,0:T(4,128)S(1)}, u32[]{:S(2)}, u32[]{:S(2)}) %collective-permute-start.1) | collective-permute-done | bytes 2080 | tf_op jit(solution)/shard_map/ppermute | solution.py:342
  94.3 1.5 %collective-permute-start.2 = (f32[4,128]{1,0:T(4,128)S(1)}, f32[4,128]{1,0:T(4,128)S(1)}, u32[]{:S(2)}, u32[]{:S(2)}) collective-permute-start(f32[4,128]{1,0:T(4,128)S(1)} %add.21), channel_id=1, source_target_pairs={{0,64},{16,80},{32,96},{48,112},{64,0},{80,16},{96,32},{112,48},{1... | collective-permute-start | bytes 6152 | tf_op jit(solution)/shard_map/ppermute | solution.py:342
  95.8 3.0 %collective-permute-done.2 = f32[4,128]{1,0:T(4,128)S(1)} collective-permute-done((f32[4,128]{1,0:T(4,128)S(1)}, f32[4,128]{1,0:T(4,128)S(1)}, u32[]{:S(2)}, u32[]{:S(2)}) %collective-permute-start.2) | collective-permute-done | bytes 2080 | tf_op jit(solution)/shard_map/ppermute | solution.py:342
  98.8 0.0 collective-permute-start.3
  98.8 7.5 %collective-permute-done.3.other_ref = f32[4,128]{1,0:T(4,128)S(1)} collective-permute-done((f32[4,128]{1,0:T(4,128)S(1)}, f32[4,128]{1,0:T(4,128)S(1)}, u32[]{:S(2)}, u32[]{:S(2)}) %collective-permute-start.3) | collective-permute-done | bytes 2080 | tf_op jit(solution)/shard_map/ppermute | solution.py:342
  106.3 0.7 attach.1
  106.9 0.0 all-to-all-done.3.recv_ref
  106.9 0.0 copy-start
  107.0 1.3 copy-done
  108.2 7.2 %all-to-all-start.2 = ((bf16[16,528,128]{2,1,0:T(8,128)(2,1)}), bf16[16,528,128]{2,1,0:T(8,128)(2,1)S(1)}, u32[]{:S(2)}, u32[]{:S(2)}) async-start(bf16[16,528,128]{2,1,0:T(8,128)(2,1)} %attach.1), calls=%async_computation.2 | async-start | bytes 4325376 | tf_op jit(solution)/shard_map/all_to_all | solution.py:338
  115.5 3.2 %unpack0.1 = (bf16[1,128,4096]{2,1,0:T(8,128)(2,1)}, bf16[1,128,4096]{2,1,0:T(8,128)(2,1)}, bf16[1,128,4096]{2,1,0:T(8,128)(2,1)}, bf16[1,128,4096]{2,1,0:T(8,128)(2,1)}) custom-call(bf16[16,512,128]{2,1,0:T(8,128)(2,1)} %copy-done), custom_call_target="tpu_custom_call" | custom-call | bytes 8388608 | tf_op jit(solution)/shard_map/unpack0/pallas_call | solution.py:99
  118.7 25.1 %all-to-all-done.2.recv_ref = bf16[16,528,128]{2,1,0:T(8,128)(2,1)S(1)} async-done(((bf16[16,528,128]{2,1,0:T(8,128)(2,1)}), bf16[16,528,128]{2,1,0:T(8,128)(2,1)S(1)}, u32[]{:S(2)}, u32[]{:S(2)}) %all-to-all-start.2) | async-done | bytes 2162720 | tf_op jit(solution)/shard_map/all_to_all | solution.py:338
  143.8 1.6 %unpack1.1 = (bf16[1,128,4096]{2,1,0:T(8,128)(2,1)}, bf16[1,128,4096]{2,1,0:T(8,128)(2,1)}, bf16[1,128,4096]{2,1,0:T(8,128)(2,1)}, bf16[1,128,4096]{2,1,0:T(8,12...) custom-call(bf16[16,528,128]{2,1,0:T(8,128)(2,1)S(1)} %all-to-all-do, ...), custom_call_target="tpu_custom_call", output_to_operand_aliasing={{0}: (1, {}), {1}: (2, {}), {2}: (3, {}), {3}: (4, {})} | custom-call | bytes 8388608 | tf_op jit(solution)/shard_map/unpack1/pallas_call | solution.py:113
  (5 shorter events, 0.0 us)
Async XLA Ops:
  3.1 37.4 %all-to-all-start = ((bf16[16,512,128]{2,1,0:T(8,128)(2,1)}), bf16[16,512,128]{2,1,0:T(8,128)(2,1)S(1)}, u32[]{:S(2)}, u32[]{:S(2)}) async-start(bf16[16,512,128]{2,1,0:T(8,128)(2,1)} %pack0.1), calls=%async_computation | async-start | bytes 4194304 | tf_op jit(solution)/shard_map/all_to_all | solution.py:338
  10.1 2.5 %copy-start.3 = (s32[32,8]{0,1:T(8,128)S(1)}, s32[32,8]{0,1:T(8,128)}, u32[]{:S(2)}) copy-start(s32[32,8]{0,1:T(8,128)} %param.13) | copy-start | bytes 3076
  10.1 2.6 %copy-start.1 = (f32[32,128]{1,0:T(8,128)S(1)}, f32[32,128]{1,0:T(8,128)}, u32[]{:S(2)}) copy-start(f32[32,128]{1,0:T(8,128)} %param.11) | copy-start | bytes 49156
  10.1 2.6 %copy-start.2 = (f32[32,128]{1,0:T(8,128)S(1)}, f32[32,128]{1,0:T(8,128)}, u32[]{:S(2)}) copy-start(f32[32,128]{1,0:T(8,128)} %param.12) | copy-start | bytes 49156
  40.5 32.1 %all-to-all-start.1 = ((bf16[16,512,128]{2,1,0:T(8,128)(2,1)}), bf16[16,512,128]{2,1,0:T(8,128)(2,1)}, u32[]{:S(2)}, u32[]{:S(2)}) async-start(bf16[16,512,128]{2,1,0:T(8,128)(2,1)} %pack1.1), calls=%async_computation.1 | async-start | bytes 4194304 | tf_op jit(solution)/shard_map/all_to_all | solution.py:338
  72.6 34.3 %all-to-all-start.3 = ((bf16[16,512,128]{2,1,0:T(8,128)(2,1)}), bf16[16,512,128]{2,1,0:T(8,128)(2,1)S(1)}, u32[]{:S(2)}, u32[]{:S(2)}) async-start(bf16[16,512,128]{2,1,0:T(8,128)(2,1)} %get-tuple-element.25), calls=%async_computation.3 | async-start | bytes 4194304 | tf_op jit(solution)/shard_map/all_to_all | solution.py:338
  89.4 1.2 collective-permute-start
  90.6 3.7 %collective-permute-start.1 = (f32[4,128]{1,0:T(4,128)S(1)}, f32[4,128]{1,0:T(4,128)S(1)}, u32[]{:S(2)}, u32[]{:S(2)}) collective-permute-start(f32[4,128]{1,0:T(4,128)S(1)} %fusion.2), channel_id=1, source_target_pairs={{0,32},{16,48},{32,0},{48,16},{64,96},{80,112},{96,64},{112,80},{1... | collective-permute-start | bytes 6152 | tf_op jit(solution)/shard_map/ppermute | solution.py:342
  94.3 4.5 %collective-permute-start.2 = (f32[4,128]{1,0:T(4,128)S(1)}, f32[4,128]{1,0:T(4,128)S(1)}, u32[]{:S(2)}, u32[]{:S(2)}) collective-permute-start(f32[4,128]{1,0:T(4,128)S(1)} %add.21), channel_id=1, source_target_pairs={{0,64},{16,80},{32,96},{48,112},{64,0},{80,16},{96,32},{112,48},{1... | collective-permute-start | bytes 6152 | tf_op jit(solution)/shard_map/ppermute | solution.py:342
  98.8 7.5 %collective-permute-start.3 = (f32[4,128]{1,0:T(4,128)S(1)}, f32[4,128]{1,0:T(4,128)S(1)}, u32[]{:S(2)}, u32[]{:S(2)}) collective-permute-start(f32[4,128]{1,0:T(4,128)S(1)} %add.22.part_ref), channel_id=1, source_target_pairs={{0,128},{16,144},{32,160},{48,176},{64,192},{80,208},{96,224},{112... | collective-permute-start | bytes 6152 | tf_op jit(solution)/shard_map/ppermute | solution.py:342
  106.9 1.3 copy-start
  108.2 35.5 %all-to-all-start.2 = ((bf16[16,528,128]{2,1,0:T(8,128)(2,1)}), bf16[16,528,128]{2,1,0:T(8,128)(2,1)S(1)}, u32[]{:S(2)}, u32[]{:S(2)}) async-start(bf16[16,528,128]{2,1,0:T(8,128)(2,1)} %attach.1), calls=%async_computation.2 | async-start | bytes 4325376 | tf_op jit(solution)/shard_map/all_to_all | solution.py:338

commit v5 on v4

--- a/solution.py
+++ b/solution.py
@@ -21,7 +21,7 @@
 LOG2E = 1.4426950408889634
 AT_ONCE = 8
 PACKED = 4
-EXTRA = 16
+SIDE = 4
 
 
 def pack_kernel(chunk, q_ref, k_ref, v_ref, g_ref, send_ref, held_ref, in_sems, out_sems):
@@ -77,7 +77,7 @@
             ref[0, :, n * HEAD : (n + 1) * HEAD] = recv_ref[first + n, a * TOK : (a + 1) * TOK, :]
 
 
-def last_unpack_kernel(factor, recv_ref, *refs):
+def last_unpack_kernel(factor, recv_ref, gathered_ref, place_ref, *refs):
     outs, query_gain_ref, key_gain_ref = refs[4:8], refs[8], refs[9]
     first = pl.program_id(0) * AT_ONCE
     for a, ref in enumerate(outs):
@@ -86,12 +86,15 @@
 
     @pl.when(pl.program_id(0) == 0)
     def _():
-        terms = recv_ref[:, 4 * TOK :, :].astype(jnp.float32)
-        for c in range(CHUNKS):
-            for k, ref in enumerate((query_gain_ref, key_gain_ref)):
-                row = 2 * c + k
-                total = terms[:, row] + terms[:, 4 + row] + terms[:, 8 + row]
-                ref[c * SEQ : (c + 1) * SEQ, :] = total * factor
+        row, column = place_ref[0] // SIDE, place_ref[0] % SIDE
+        for x in range(SIDE):
+            for y in range(SIDE):
+                away = ((row - x + SIDE) % SIDE) * SIDE + (column - y + SIDE) % SIDE
+                total = gathered_ref[away] * factor
+                for c in range(CHUNKS):
+                    head = c * SEQ + x * SIDE + y
+                    query_gain_ref[head : head + 1, :] = total[2 * c : 2 * c + 1]
+                    key_gain_ref[head : head + 1, :] = total[2 * c + 1 : 2 * c + 2]
 
 
 def unpack(recv):
@@ -107,50 +110,26 @@
     )(recv)
 
 
-def last_unpack(factor, recv, before):
+def last_unpack(factor, recv, gathered, place, before):
     steps = SEQ // AT_ONCE
     gain = jax.ShapeDtypeStruct((HEADS, HEAD), jnp.float32)
     return pl.pallas_call(
         functools.partial(last_unpack_kernel, factor),
         grid=(steps,),
         out_shape=(jax.ShapeDtypeStruct((1, TOK, HEADS * HEAD), jnp.bfloat16),) * 4 + (gain, gain),
-        in_specs=[pl.BlockSpec(memory_space=pltpu.VMEM)] + [pl.BlockSpec(memory_space=pl.ANY)] * 4,
+        in_specs=[
+            pl.BlockSpec(memory_space=pltpu.VMEM),
+            pl.BlockSpec(memory_space=pltpu.VMEM),
+            pl.BlockSpec(memory_space=pltpu.SMEM),
+        ]
+        + [pl.BlockSpec(memory_space=pl.ANY)] * 4,
         out_specs=(pl.BlockSpec((1, TOK, AT_ONCE * HEAD), lambda i: (0, 0, steps + i)),) * 4
         + (pl.BlockSpec((HEADS, HEAD), lambda i: (0, 0)),) * 2,
-        input_output_aliases={i + 1: i for i in range(4)},
+        input_output_aliases={i + 3: i for i in range(4)},
         compiler_params=pltpu.CompilerParams(vmem_limit_bytes=24 << 20),
         cost_estimate=pl.CostEstimate(flops=0, bytes_accessed=8 << 20, transcendentals=0),
         name="unpack1",
-    )(recv, *before)
-
-
-def attach_kernel(part_ref, other_ref, _, send_ref, rows_ref, sem):
-    part = part_ref[...] + other_ref[...]
-    high = part.astype(jnp.bfloat16)
-    rest = part - high.astype(jnp.float32)
-    middle = rest.astype(jnp.bfloat16)
-    low = (rest - middle.astype(jnp.float32)).astype(jnp.bfloat16)
-    blank = jnp.zeros((EXTRA - 12, HEAD), jnp.bfloat16)
-    rows = jnp.concatenate([high, middle, low, blank], axis=0)
-    rows_ref[...] = jnp.broadcast_to(rows[None], (SEQ, EXTRA, HEAD))
-    copy = pltpu.make_async_copy(rows_ref, send_ref.at[:, pl.ds(4 * TOK, EXTRA), :], sem)
-    copy.start()
-    copy.wait()
-
-
-def attach(part, other, send):
-    return pl.pallas_call(
-        attach_kernel,
-        out_shape=pltpu.HBM(send.shape, send.dtype),
-        in_specs=[pl.BlockSpec(memory_space=pltpu.VMEM)] * 2
-        + [pl.BlockSpec(memory_space=pltpu.HBM)],
-        out_specs=pl.BlockSpec(memory_space=pltpu.HBM),
-        input_output_aliases={2: 0},
-        scratch_shapes=[pltpu.VMEM((SEQ, EXTRA, HEAD), jnp.bfloat16), pltpu.SemaphoreType.DMA],
-        compiler_params=pltpu.CompilerParams(vmem_limit_bytes=8 << 20),
-        cost_estimate=pl.CostEstimate(flops=0, bytes_accessed=1 << 17, transcendentals=0),
-        name="attach",
-    )(part, other, send)
+    )(recv, gathered, place, *before)
 
 
 def dot(a, b, ca, cb):
@@ -297,11 +276,11 @@
     leave(1).wait()
 
 
-def attend(chunk, ids, gains, recv, extra=0, group=2):
+def attend(chunk, ids, gains, recv, group=2):
     return pl.pallas_call(
         functools.partial(attend_kernel, group=group),
         out_shape=(
-            pltpu.HBM((SEQ, 4 * TOK + extra, HEAD), jnp.bfloat16),
+            pltpu.HBM((SEQ, 4 * TOK, HEAD), jnp.bfloat16),
             jax.ShapeDtypeStruct((2, HEAD), jnp.float32),
         ),
         in_specs=[
@@ -342,6 +321,17 @@
     return lax.ppermute(x, axis, [(i, i ^ step) for i in range(lax.axis_size(axis))])
 
 
+def ring_of(x, stride):
+    held = [x]
+    for k in range(1, SIDE):
+        turn = []
+        for i in range(SEQ):
+            at = i // stride % SIDE
+            turn.append((i, i + ((at + k) % SIDE - at) * stride))
+        held.append(lax.ppermute(x, "seq", turn))
+    return jnp.stack(held)
+
+
 def on_device(queries, keys, values, cotangent, query_gain, key_gain, block_ids):
     arrays = (queries, keys, values, cotangent)
     s = lax.axis_index("seq")
@@ -356,14 +346,15 @@
     back0, gain0 = attend(0, block_ids, gains[0], in0)
     back0, in1 = lax.optimization_barrier((back0, in1))
     out0 = swap(back0, "seq")
-    back1, gain1 = attend(1, block_ids, gains[1], in1, EXTRA)
-    part = jnp.concatenate([gain0, gain1], axis=0)
-    for step in (1, 2, 4):
+    back1, gain1 = attend(1, block_ids, gains[1], in1)
+    part = ring_of(jnp.concatenate([gain0, gain1], axis=0), 1)
+    part, back1, out0 = lax.optimization_barrier((part, back1, out0))
+    out1 = swap(back1, "seq")
+    for step in (1, 2, 4, 8):
         part = part + far(part, "dp", step)
-    back1 = attach(part, far(part, "dp", 8), back1)
-    out1 = swap(back1, "seq")
+    part = ring_of(part, SIDE).reshape(SEQ, 2 * CHUNKS, HEAD)
     factor = (TOKENS * lax.axis_size("dp")) ** -0.5
-    return tuple(last_unpack(factor, out1, unpack(out0)))
+    return tuple(last_unpack(factor, out1, part, s.reshape(1), unpack(out0)))
 
 
 def solution(mesh):

time: 147 us -> 140 us (0.952)
  waiting for transfers between devices: 83.1 us -> 69.5 us
  starting transfers between devices: 25.6 us -> 34.1 us
    all_to_all x4, waiting for transfers between devices: 68.9 us -> 52.4 us  [swap(): return lax.all_to_all(x, axis, split_axis=0, concat_axis=0, tiled=True)]
    ppermute x0 -> x6, starting transfers between devices: none -> 11.5 us  [ring_of(): held.append(lax.ppermute(x, 'seq', turn))]
    all_to_all x4, starting transfers between devices: 22.9 us -> 20 us  [swap(): return lax.all_to_all(x, axis, split_axis=0, concat_axis=0, tiled=True)]
    ppermute x0 -> x6, waiting for transfers between devices: none -> 2.69 us  [ring_of(): held.append(lax.ppermute(x, 'seq', turn))]
  transfers between devices with their start and end apart: 8 -> 14, of which waited for: 7 -> 12; matrix products, arithmetic and copies ran while one was open for 0% -> 0% of each run, Pallas kernels for 21% -> 21%
where the time goes in v5:
time: 140 us
  waiting for transfers between devices  69.5 us (50%)
  starting transfers between devices  34.1 us (24%)
  Pallas kernels  33.8 us (24%)
    all_to_all x4, waiting for transfers between devices, swap(): return lax.all_to_all(x, axis, split_axis=0, concat_axis=0, tiled=True)  52.4 us
    pallas_call x2, Pallas kernels, attend(): pl.pallas_call(functools.partial(attend_kernel, group=group), out_shape=(...  24.1 us
    all_to_all x4, starting transfers between devices, swap(): return lax.all_to_all(x, axis, split_axis=0, concat_axis=0, tiled=True)  20 us
    ppermute x4, waiting for transfers between devices, far(): lax.ppermute(x, axis, [(i, i ^ step) for i in range(lax.axis_size(axis))])  14.4 us
    ppermute x6, starting transfers between devices, ring_of(): held.append(lax.ppermute(x, 'seq', turn))  11.5 us
    pallas_call x2, Pallas kernels, pack(): pl.pallas_call(functools.partial(pack_kernel, chunk), out_shape=pltpu.HBM...  4.85 us
    pallas_call x1, Pallas kernels, unpack(): pl.pallas_call(unpack_kernel, grid=(steps,), out_shape=(jax.ShapeDtypeStr...  3.17 us
  transfers between devices with their start and end apart: 14, of which 12 were waited for; matrix products, arithmetic and copies ran while one was open for 0% of the time, Pallas kernels for 21%

profile of v5, /device:TPU:128, one launch (start us, length us, event | category | flops | bytes accessed | tf_op | source)
XLA Modules:
  0.0 139.6 jit_solution(10908445190176307228)
XLA Ops:
  0.6 2.4 %pack0.1 = bf16[16,512,128]{2,1,0:T(8,128)(2,1)} custom-call(bf16[1,128,4096]{2,1,0:T(8,128)(2,1)} %q_ref.3, bf16[1,128,4096]{2,1,0:T(8,128)(2,1)} %k_ref.3, bf16[1,128,4096]{2,1,0:T(8,128)(2,1)} %v_ref.3, bf16[1,128,4096]{2,1,0:T(8,128)(2,1)} %g_ref.3), custom_call_target="tpu_custom_call" | custom-call | bytes 8388608 | tf_op jit(solution)/shard_map/pack0/pallas_call | solution.py:58
  3.0 7.0 %all-to-all-start = ((bf16[16,512,128]{2,1,0:T(8,128)(2,1)}), bf16[16,512,128]{2,1,0:T(8,128)(2,1)S(1)}, u32[]{:S(2)}, u32[]{:S(2)}) async-start(bf16[16,512,128]{2,1,0:T(8,128)(2,1)} %pack0.1), calls=%async_computation | async-start | bytes 4194304 | tf_op jit(solution)/shard_map/all_to_all | solution.py:317
  10.1 2.4 %pack1.1 = bf16[16,512,128]{2,1,0:T(8,128)(2,1)} custom-call(bf16[1,128,4096]{2,1,0:T(8,128)(2,1)} %q_ref.3, bf16[1,128,4096]{2,1,0:T(8,128)(2,1)} %k_ref.3, bf16[1,128,4096]{2,1,0:T(8,128)(2,1)} %v_ref.3, bf16[1,128,4096]{2,1,0:T(8,128)(2,1)} %g_ref.3), custom_call_target="tpu_custom_call" | custom-call | bytes 8388608 | tf_op jit(solution)/shard_map/pack1/pallas_call | solution.py:58
  12.6 0.1 copy.17.ids_ref
  12.7 27.8 %all-to-all-done.recv_ref = bf16[16,512,128]{2,1,0:T(8,128)(2,1)S(1)} async-done(((bf16[16,512,128]{2,1,0:T(8,128)(2,1)}), bf16[16,512,128]{2,1,0:T(8,128)(2,1)S(1)}, u32[]{:S(2)}, u32[]{:S(2)}) %all-to-all-start) | async-done | bytes 2097184 | tf_op jit(solution)/shard_map/all_to_all | solution.py:317
  40.5 4.4 %all-to-all-start.1 = ((bf16[16,512,128]{2,1,0:T(8,128)(2,1)}), bf16[16,512,128]{2,1,0:T(8,128)(2,1)}, u32[]{:S(2)}, u32[]{:S(2)}) async-start(bf16[16,512,128]{2,1,0:T(8,128)(2,1)} %pack1.1), calls=%async_computation.1 | async-start | bytes 4194304 | tf_op jit(solution)/shard_map/all_to_all | solution.py:317
  44.9 11.7 %attend0.1 = (bf16[16,512,128]{2,1,0:T(8,128)(2,1)}, f32[2,128]{1,0:T(2,128)S(1)}) custom-call(s32[32,8]{1,0:T(8,128)S(1)} %copy.17.ids_ref, f32[2,128]{1,0:T(2,128)S(1)} %bitcast.17, bf16[16,512,128]{2,1,0:T(8,128)(2,1)S(1)} %all-to-all-done.recv_ref), custom_call_target="tpu_custom_call" | custom-call | flops 24999999488 | bytes 4194304 | tf_op jit(solution)/shard_map/attend0/pallas_call | solution.py:280
  56.6 16.0 %all-to-all-done.1.recv_ref = bf16[16,512,128]{2,1,0:T(8,128)(2,1)} async-done(((bf16[16,512,128]{2,1,0:T(8,128)(2,1)}), bf16[16,512,128]{2,1,0:T(8,128)(2,1)}, u32[]{:S(2)}, u32[]{:S(2)}) %all-to-all-start.1) | async-done | bytes 2097184 | tf_op jit(solution)/shard_map/all_to_all | solution.py:317
  72.6 4.2 %all-to-all-start.2 = ((bf16[16,512,128]{2,1,0:T(8,128)(2,1)}), bf16[16,512,128]{2,1,0:T(8,128)(2,1)S(1)}, u32[]{:S(2)}, u32[]{:S(2)}) async-start(bf16[16,512,128]{2,1,0:T(8,128)(2,1)} %get-tuple-element.28), calls=%async_computation.2 | async-start | bytes 4194304 | tf_op jit(solution)/shard_map/all_to_all | solution.py:317
  76.8 12.5 %attend1.1 = (bf16[16,512,128]{2,1,0:T(8,128)(2,1)}, f32[2,128]{1,0:T(2,128)S(1)}) custom-call(s32[32,8]{1,0:T(8,128)S(1)} %copy.17.ids_ref, f32[2,128]{1,0:T(2,128)S(1)} %bitcast.16, bf16[16,512,128]{2,1,0:T(8,128)(2,1)} %all-to-all-done.1.recv_ref), custom_call_target="tpu_custom_call" | custom-call | flops 24999999488 | bytes 4194304 | tf_op jit(solution)/shard_map/attend1/pallas_call | solution.py:280
  89.3 3.5 %collective-permute-start.1 = (f32[4,128]{1,0:T(4,128)S(1)}, f32[4,128]{1,0:T(4,128)S(1)}, u32[]{:S(2)}, u32[]{:S(2)}) collective-permute-start(f32[4,128]{1,0:T(4,128)S(1)} %get-tuple-element.39), channel_id=1, source_target_pairs={{0,2},{1,3},{2,0},{3,1},{4,6},{5,7},{6,4},{7,5},{8,10},{9,11},{10,... | collective-permute-start | bytes 6152 | tf_op jit(solution)/shard_map/ppermute | solution.py:331
  92.8 0.6 collective-permute-start
  93.4 2.7 %collective-permute-start.2 = (f32[4,128]{1,0:T(4,128)S(1)}, f32[4,128]{1,0:T(4,128)S(1)}, u32[]{:S(2)}, u32[]{:S(2)}) collective-permute-start(f32[4,128]{1,0:T(4,128)S(1)} %get-tuple-element.39), channel_id=1, source_target_pairs={{0,3},{1,0},{2,1},{3,2},{4,7},{5,4},{6,5},{7,6},{8,11},{9,8},{10,9... | collective-permute-start | bytes 6152 | tf_op jit(solution)/shard_map/ppermute | solution.py:331
  96.1 1.6 %collective-permute-done = f32[4,128]{1,0:T(4,128)S(1)} collective-permute-done((f32[4,128]{1,0:T(4,128)S(1)}, f32[4,128]{1,0:T(4,128)S(1)}, u32[]{:S(2)}, u32[]{:S(2)}) %collective-permute-start) | collective-permute-done | bytes 2080 | tf_op jit(solution)/shard_map/ppermute | solution.py:331
  97.6 0.1 collective-permute-done.2
  97.8 6.7 %all-to-all-done.2.recv_ref = bf16[16,512,128]{2,1,0:T(8,128)(2,1)S(1)} async-done(((bf16[16,512,128]{2,1,0:T(8,128)(2,1)}), bf16[16,512,128]{2,1,0:T(8,128)(2,1)S(1)}, u32[]{:S(2)}, u32[]{:S(2)}) %all-to-all-start.2) | async-done | bytes 2097184 | tf_op jit(solution)/shard_map/all_to_all | solution.py:317
  104.5 1.3 copy-done
  105.8 4.3 %all-to-all-start.3 = ((bf16[16,512,128]{2,1,0:T(8,128)(2,1)}), bf16[16,512,128]{2,1,0:T(8,128)(2,1)S(1)}, u32[]{:S(2)}, u32[]{:S(2)}) async-start(bf16[16,512,128]{2,1,0:T(8,128)(2,1)} %get-tuple-element.29), calls=%async_computation.3 | async-start | bytes 4194304 | tf_op jit(solution)/shard_map/all_to_all | solution.py:317
  110.1 0.1 collective-permute-start.3
  110.2 1.2 collective-permute-done.3
  111.4 1.0 collective-permute-start.4
  112.4 2.6 %collective-permute-done.4 = f32[4,4,128]{2,1,0:T(4,128)S(1)} collective-permute-done((f32[4,4,128]{2,1,0:T(4,128)S(1)}, f32[4,4,128]{2,1,0:T(4,128)S(1)}, u32[]{:S(2)}, u32[]{:S(2)}) %collective-permute-start.4) | collective-permute-done | bytes 8224 | tf_op jit(solution)/shard_map/ppermute | solution.py:321
  115.1 1.5 %collective-permute-start.5 = (f32[4,4,128]{2,1,0:T(4,128)S(1)}, f32[4,4,128]{2,1,0:T(4,128)S(1)}, u32[]{:S(2)}, u32[]{:S(2)}) collective-permute-start(f32[4,4,128]{2,1,0:T(4,128)S(1)} %add.24), channel_id=1, source_target_pairs={{0,64},{16,80},{32,96},{48,112},{64,0},{80,16},{96,32},{112,48},{1... | collective-permute-start | bytes 24584 | tf_op jit(solution)/shard_map/ppermute | solution.py:321
  116.5 3.1 %collective-permute-done.5 = f32[4,4,128]{2,1,0:T(4,128)S(1)} collective-permute-done((f32[4,4,128]{2,1,0:T(4,128)S(1)}, f32[4,4,128]{2,1,0:T(4,128)S(1)}, u32[]{:S(2)}, u32[]{:S(2)}) %collective-permute-start.5) | collective-permute-done | bytes 8224 | tf_op jit(solution)/shard_map/ppermute | solution.py:321
  119.6 7.6 %collective-permute-done.6 = f32[4,4,128]{2,1,0:T(4,128)S(1)} collective-permute-done((f32[4,4,128]{2,1,0:T(4,128)S(1)}, f32[4,4,128]{2,1,0:T(4,128)S(1)}, u32[]{:S(2)}, u32[]{:S(2)}) %collective-permute-start.6) | collective-permute-done | bytes 8224 | tf_op jit(solution)/shard_map/ppermute | solution.py:321
  127.2 3.1 %collective-permute-start.9 = (f32[4,4,128]{2,1,0:T(4,128)S(1)}, f32[4,4,128]{2,1,0:T(4,128)S(1)}, u32[]{:S(2)}, u32[]{:S(2)}) collective-permute-start(f32[4,4,128]{2,1,0:T(4,128)S(1)} %add.26), channel_id=1, source_target_pairs={{0,12},{1,13},{2,14},{3,15},{4,0},{5,1},{6,2},{7,3},{8,4},{9,5},{1... | collective-permute-start | bytes 24584 | tf_op jit(solution)/shard_map/ppermute | solution.py:331
  130.2 0.9 collective-permute-start.8
  131.1 0.9 collective-permute-start.7
  131.9 3.2 %unpack0.1 = (bf16[1,128,4096]{2,1,0:T(8,128)(2,1)}, bf16[1,128,4096]{2,1,0:T(8,128)(2,1)}, bf16[1,128,4096]{2,1,0:T(8,128)(2,1)}, bf16[1,128,4096]{2,1,0:T(8,128)(2,1)}) custom-call(bf16[16,512,128]{2,1,0:T(8,128)(2,1)} %copy-done), custom_call_target="tpu_custom_call" | custom-call | bytes 8388608 | tf_op jit(solution)/shard_map/unpack0/pallas_call | solution.py:102
  135.1 0.9 collective-permute-done.8
  136.1 1.9 %all-to-all-done.3.recv_ref = bf16[16,512,128]{2,1,0:T(8,128)(2,1)S(1)} async-done(((bf16[16,512,128]{2,1,0:T(8,128)(2,1)}), bf16[16,512,128]{2,1,0:T(8,128)(2,1)S(1)}, u32[]{:S(2)}, u32[]{:S(2)}) %all-to-all-start.3) | async-done | bytes 2097184 | tf_op jit(solution)/shard_map/all_to_all | solution.py:317
  138.0 1.6 %unpack1.1 = (bf16[1,128,4096]{2,1,0:T(8,128)(2,1)}, bf16[1,128,4096]{2,1,0:T(8,128)(2,1)}, bf16[1,128,4096]{2,1,0:T(8,128)(2,1)}, bf16[1,128,4096]{2,1,0:T(8,12...) custom-call(bf16[16,512,128]{2,1,0:T(8,128)(2,1)S(1)} %all-to-all-do, ...), custom_call_target="tpu_custom_call", output_to_operand_aliasing={{0}: (3, {}), {1}: (4, {}), {2}: (5, {}), {3}: (6, {})} | custom-call | bytes 8388608 | tf_op jit(solution)/shard_map/unpack1/pallas_call | solution.py:116
  (19 shorter events, 0.1 us)
Async XLA Ops:
  3.0 37.4 %all-to-all-start = ((bf16[16,512,128]{2,1,0:T(8,128)(2,1)}), bf16[16,512,128]{2,1,0:T(8,128)(2,1)S(1)}, u32[]{:S(2)}, u32[]{:S(2)}) async-start(bf16[16,512,128]{2,1,0:T(8,128)(2,1)} %pack0.1), calls=%async_computation | async-start | bytes 4194304 | tf_op jit(solution)/shard_map/all_to_all | solution.py:317
  10.1 2.5 %copy-start.3 = (s32[32,8]{0,1:T(8,128)S(1)}, s32[32,8]{0,1:T(8,128)}, u32[]{:S(2)}) copy-start(s32[32,8]{0,1:T(8,128)} %param.13) | copy-start | bytes 3076
  10.1 2.6 %copy-start.1 = (f32[32,128]{1,0:T(8,128)S(1)}, f32[32,128]{1,0:T(8,128)}, u32[]{:S(2)}) copy-start(f32[32,128]{1,0:T(8,128)} %param.11) | copy-start | bytes 49156
  10.1 2.6 %copy-start.2 = (f32[32,128]{1,0:T(8,128)S(1)}, f32[32,128]{1,0:T(8,128)}, u32[]{:S(2)}) copy-start(f32[32,128]{1,0:T(8,128)} %param.12) | copy-start | bytes 49156
  40.5 32.1 %all-to-all-start.1 = ((bf16[16,512,128]{2,1,0:T(8,128)(2,1)}), bf16[16,512,128]{2,1,0:T(8,128)(2,1)}, u32[]{:S(2)}, u32[]{:S(2)}) async-start(bf16[16,512,128]{2,1,0:T(8,128)(2,1)} %pack1.1), calls=%async_computation.1 | async-start | bytes 4194304 | tf_op jit(solution)/shard_map/all_to_all | solution.py:317
  72.6 31.9 %all-to-all-start.2 = ((bf16[16,512,128]{2,1,0:T(8,128)(2,1)}), bf16[16,512,128]{2,1,0:T(8,128)(2,1)S(1)}, u32[]{:S(2)}, u32[]{:S(2)}) async-start(bf16[16,512,128]{2,1,0:T(8,128)(2,1)} %get-tuple-element.28), calls=%async_computation.2 | async-start | bytes 4194304 | tf_op jit(solution)/shard_map/all_to_all | solution.py:317
  89.3 6.8 %collective-permute-start.1 = (f32[4,128]{1,0:T(4,128)S(1)}, f32[4,128]{1,0:T(4,128)S(1)}, u32[]{:S(2)}, u32[]{:S(2)}) collective-permute-start(f32[4,128]{1,0:T(4,128)S(1)} %get-tuple-element.39), channel_id=1, source_target_pairs={{0,2},{1,3},{2,0},{3,1},{4,6},{5,7},{6,4},{7,5},{8,10},{9,11},{10,... | collective-permute-start | bytes 6152 | tf_op jit(solution)/shard_map/ppermute | solution.py:331
  92.8 4.8 %collective-permute-start = (f32[4,128]{1,0:T(4,128)S(1)}, f32[4,128]{1,0:T(4,128)S(1)}, u32[]{:S(2)}, u32[]{:S(2)}) collective-permute-start(f32[4,128]{1,0:T(4,128)S(1)} %get-tuple-element.39), channel_id=1, source_target_pairs={{0,1},{1,2},{2,3},{3,0},{4,5},{5,6},{6,7},{7,4},{8,9},{9,10},{10,1... | collective-permute-start | bytes 6152 | tf_op jit(solution)/shard_map/ppermute | solution.py:331
  93.4 4.4 %collective-permute-start.2 = (f32[4,128]{1,0:T(4,128)S(1)}, f32[4,128]{1,0:T(4,128)S(1)}, u32[]{:S(2)}, u32[]{:S(2)}) collective-permute-start(f32[4,128]{1,0:T(4,128)S(1)} %get-tuple-element.39), channel_id=1, source_target_pairs={{0,3},{1,0},{2,1},{3,2},{4,7},{5,4},{6,5},{7,6},{8,11},{9,8},{10,9... | collective-permute-start | bytes 6152 | tf_op jit(solution)/shard_map/ppermute | solution.py:331
  104.5 1.3 copy-start
  105.8 32.2 %all-to-all-start.3 = ((bf16[16,512,128]{2,1,0:T(8,128)(2,1)}), bf16[16,512,128]{2,1,0:T(8,128)(2,1)S(1)}, u32[]{:S(2)}, u32[]{:S(2)}) async-start(bf16[16,512,128]{2,1,0:T(8,128)(2,1)} %get-tuple-element.29), calls=%async_computation.3 | async-start | bytes 4194304 | tf_op jit(solution)/shard_map/all_to_all | solution.py:317
  110.1 1.3 collective-permute-start.3
  111.4 3.7 %collective-permute-start.4 = (f32[4,4,128]{2,1,0:T(4,128)S(1)}, f32[4,4,128]{2,1,0:T(4,128)S(1)}, u32[]{:S(2)}, u32[]{:S(2)}) collective-permute-start(f32[4,4,128]{2,1,0:T(4,128)S(1)} %add.23), channel_id=1, source_target_pairs={{0,32},{16,48},{32,0},{48,16},{64,96},{80,112},{96,64},{112,80},{1... | collective-permute-start | bytes 24584 | tf_op jit(solution)/shard_map/ppermute | solution.py:321
  115.1 4.5 %collective-permute-start.5 = (f32[4,4,128]{2,1,0:T(4,128)S(1)}, f32[4,4,128]{2,1,0:T(4,128)S(1)}, u32[]{:S(2)}, u32[]{:S(2)}) collective-permute-start(f32[4,4,128]{2,1,0:T(4,128)S(1)} %add.24), channel_id=1, source_target_pairs={{0,64},{16,80},{32,96},{48,112},{64,0},{80,16},{96,32},{112,48},{1... | collective-permute-start | bytes 24584 | tf_op jit(solution)/shard_map/ppermute | solution.py:321
  119.6 7.6 %collective-permute-start.6 = (f32[4,4,128]{2,1,0:T(4,128)S(1)}, f32[4,4,128]{2,1,0:T(4,128)S(1)}, u32[]{:S(2)}, u32[]{:S(2)}) collective-permute-start(f32[4,4,128]{2,1,0:T(4,128)S(1)} %add.25), channel_id=1, source_target_pairs={{0,128},{16,144},{32,160},{48,176},{64,192},{80,208},{96,224},{112... | collective-permute-start | bytes 24584 | tf_op jit(solution)/shard_map/ppermute | solution.py:321
  127.2 7.9 %collective-permute-start.9 = (f32[4,4,128]{2,1,0:T(4,128)S(1)}, f32[4,4,128]{2,1,0:T(4,128)S(1)}, u32[]{:S(2)}, u32[]{:S(2)}) collective-permute-start(f32[4,4,128]{2,1,0:T(4,128)S(1)} %add.26), channel_id=1, source_target_pairs={{0,12},{1,13},{2,14},{3,15},{4,0},{5,1},{6,2},{7,3},{8,4},{9,5},{1... | collective-permute-start | bytes 24584 | tf_op jit(solution)/shard_map/ppermute | solution.py:331
  130.2 5.8 %collective-permute-start.8 = (f32[4,4,128]{2,1,0:T(4,128)S(1)}, f32[4,4,128]{2,1,0:T(4,128)S(1)}, u32[]{:S(2)}, u32[]{:S(2)}) collective-permute-start(f32[4,4,128]{2,1,0:T(4,128)S(1)} %add.26), channel_id=1, source_target_pairs={{0,8},{1,9},{2,10},{3,11},{4,12},{5,13},{6,14},{7,15},{8,0},{9,1},... | collective-permute-start | bytes 24584 | tf_op jit(solution)/shard_map/ppermute | solution.py:331
  131.1 5.0 %collective-permute-start.7 = (f32[4,4,128]{2,1,0:T(4,128)S(1)}, f32[4,4,128]{2,1,0:T(4,128)S(1)}, u32[]{:S(2)}, u32[]{:S(2)}) collective-permute-start(f32[4,4,128]{2,1,0:T(4,128)S(1)} %add.26), channel_id=1, source_target_pairs={{0,4},{1,5},{2,6},{3,7},{4,8},{5,9},{6,10},{7,11},{8,12},{9,13},{1... | collective-permute-start | bytes 24584 | tf_op jit(solution)/shard_map/ppermute | solution.py:331

commit v6 on v5

--- a/solution.py
+++ b/solution.py
@@ -71,10 +71,9 @@
 
 
 def unpack_kernel(recv_ref, *refs):
-    first = pl.program_id(0) * AT_ONCE
     for a, ref in enumerate(refs):
         for n in range(AT_ONCE):
-            ref[0, :, n * HEAD : (n + 1) * HEAD] = recv_ref[first + n, a * TOK : (a + 1) * TOK, :]
+            ref[0, :, n * HEAD : (n + 1) * HEAD] = recv_ref[n, a * TOK : (a + 1) * TOK, :]
 
 
 def last_unpack_kernel(factor, recv_ref, gathered_ref, place_ref, *refs):
@@ -103,7 +102,7 @@
         unpack_kernel,
         grid=(steps,),
         out_shape=(jax.ShapeDtypeStruct((1, TOK, HEADS * HEAD), jnp.bfloat16),) * 4,
-        in_specs=[pl.BlockSpec(memory_space=pltpu.VMEM)],
+        in_specs=[pl.BlockSpec((AT_ONCE, 4 * TOK, HEAD), lambda i: (i, 0, 0))],
         out_specs=(pl.BlockSpec((1, TOK, AT_ONCE * HEAD), lambda i: (0, 0, i)),) * 4,
         cost_estimate=pl.CostEstimate(flops=0, bytes_accessed=8 << 20, transcendentals=0),
         name="unpack0",
@@ -303,7 +302,7 @@
             pltpu.VMEM((group, 2 * BLOCK, SLOTS * BLOCK), jnp.bfloat16),
             pltpu.SemaphoreType.DMA((2,)),
         ],
-        compiler_params=pltpu.CompilerParams(vmem_limit_bytes=32 << 20),
+        compiler_params=pltpu.CompilerParams(vmem_limit_bytes=(64 if chunk == 0 else 125) << 19),
         cost_estimate=pl.CostEstimate(
             flops=25_000_000_000,
             bytes_accessed=4 << 20,

time: 140 us -> 139 us (level)
    all_to_all x4, waiting for transfers between devices: 52.4 us -> 47.6 us  [swap(): return lax.all_to_all(x, axis, split_axis=0, concat_axis=0, tiled=True)]
    ppermute x6, waiting for transfers between devices: 2.69 us -> 6.3 us  [ring_of(): held.append(lax.ppermute(x, 'seq', turn))]
  transfers between devices with their start and end apart: 14 -> 14, of which waited for: 12 -> 11; matrix products, arithmetic and copies ran while one was open for 0% -> 1% of each run, Pallas kernels for 21% -> 22%
where the time goes in v6:
time: 139 us
  waiting for transfers between devices  68.3 us (49%)
  starting transfers between devices  34.1 us (25%)
  Pallas kernels  34 us (24%)
    all_to_all x4, waiting for transfers between devices, swap(): return lax.all_to_all(x, axis, split_axis=0, concat_axis=0, tiled=True)  47.6 us
    pallas_call x2, Pallas kernels, attend(): pl.pallas_call(functools.partial(attend_kernel, group=group), out_shape=(...  24.7 us
    all_to_all x4, starting transfers between devices, swap(): return lax.all_to_all(x, axis, split_axis=0, concat_axis=0, tiled=True)  20.3 us
    ppermute x4, waiting for transfers between devices, far(): lax.ppermute(x, axis, [(i, i ^ step) for i in range(lax.axis_size(axis))])  14.4 us
    ppermute x6, starting transfers between devices, ring_of(): held.append(lax.ppermute(x, 'seq', turn))  11.2 us
    ppermute x6, waiting for transfers between devices, ring_of(): held.append(lax.ppermute(x, 'seq', turn))  6.3 us
    pallas_call x2, Pallas kernels, pack(): pl.pallas_call(functools.partial(pack_kernel, chunk), out_shape=pltpu.HBM...  4.85 us
    pallas_call x1, Pallas kernels, unpack(): pl.pallas_call(unpack_kernel, grid=(steps,), out_shape=(jax.ShapeDtypeStr...  2.81 us
  transfers between devices with their start and end apart: 14, of which 11 were waited for; matrix products, arithmetic and copies ran while one was open for 1% of the time, Pallas kernels for 22%

profile of v6, /device:TPU:128, one launch (start us, length us, event | category | flops | bytes accessed | tf_op | source)
XLA Modules:
  0.0 138.6 jit_solution(3055112880486986327)
XLA Ops:
  0.6 2.4 %pack0.1 = bf16[16,512,128]{2,1,0:T(8,128)(2,1)} custom-call(bf16[1,128,4096]{2,1,0:T(8,128)(2,1)} %q_ref.3, bf16[1,128,4096]{2,1,0:T(8,128)(2,1)} %k_ref.3, bf16[1,128,4096]{2,1,0:T(8,128)(2,1)} %v_ref.3, bf16[1,128,4096]{2,1,0:T(8,128)(2,1)} %g_ref.3), custom_call_target="tpu_custom_call" | custom-call | bytes 8388608 | tf_op jit(solution)/shard_map/pack0/pallas_call | solution.py:58
  3.1 7.0 %all-to-all-start = ((bf16[16,512,128]{2,1,0:T(8,128)(2,1)}), bf16[16,512,128]{2,1,0:T(8,128)(2,1)S(1)}, u32[]{:S(2)}, u32[]{:S(2)}) async-start(bf16[16,512,128]{2,1,0:T(8,128)(2,1)} %pack0.1), calls=%async_computation | async-start | bytes 4194304 | tf_op jit(solution)/shard_map/all_to_all | solution.py:316
  10.2 2.4 %pack1.1 = bf16[16,512,128]{2,1,0:T(8,128)(2,1)} custom-call(bf16[1,128,4096]{2,1,0:T(8,128)(2,1)} %q_ref.3, bf16[1,128,4096]{2,1,0:T(8,128)(2,1)} %k_ref.3, bf16[1,128,4096]{2,1,0:T(8,128)(2,1)} %v_ref.3, bf16[1,128,4096]{2,1,0:T(8,128)(2,1)} %g_ref.3), custom_call_target="tpu_custom_call" | custom-call | bytes 8388608 | tf_op jit(solution)/shard_map/pack1/pallas_call | solution.py:58
  12.6 0.1 copy.17.ids_ref
  12.7 0.6 fusion.1
  13.3 27.2 %all-to-all-done.recv_ref = bf16[16,512,128]{2,1,0:T(8,128)(2,1)S(1)} async-done(((bf16[16,512,128]{2,1,0:T(8,128)(2,1)}), bf16[16,512,128]{2,1,0:T(8,128)(2,1)S(1)}, u32[]{:S(2)}, u32[]{:S(2)}) %all-to-all-start) | async-done | bytes 2097184 | tf_op jit(solution)/shard_map/all_to_all | solution.py:316
  40.5 4.4 %all-to-all-start.1 = ((bf16[16,512,128]{2,1,0:T(8,128)(2,1)}), bf16[16,512,128]{2,1,0:T(8,128)(2,1)}, u32[]{:S(2)}, u32[]{:S(2)}) async-start(bf16[16,512,128]{2,1,0:T(8,128)(2,1)} %pack1.1), calls=%async_computation.1 | async-start | bytes 4194304 | tf_op jit(solution)/shard_map/all_to_all | solution.py:316
  45.0 11.7 %attend0.1 = (bf16[16,512,128]{2,1,0:T(8,128)(2,1)}, f32[2,128]{1,0:T(2,128)S(1)}) custom-call(s32[32,8]{1,0:T(8,128)S(1)} %copy.17.ids_ref, f32[2,128]{1,0:T(2,128)S(1)} %bitcast.16, bf16[16,512,128]{2,1,0:T(8,128)(2,1)S(1)} %all-to-all-done.recv_ref), custom_call_target="tpu_custom_call" | custom-call | flops 24999999488 | bytes 4194304 | tf_op jit(solution)/shard_map/attend0/pallas_call | solution.py:279
  56.6 16.0 %all-to-all-done.1.recv_ref = bf16[16,512,128]{2,1,0:T(8,128)(2,1)} async-done(((bf16[16,512,128]{2,1,0:T(8,128)(2,1)}), bf16[16,512,128]{2,1,0:T(8,128)(2,1)}, u32[]{:S(2)}, u32[]{:S(2)}) %all-to-all-start.1) | async-done | bytes 2097184 | tf_op jit(solution)/shard_map/all_to_all | solution.py:316
  72.6 4.4 %all-to-all-start.2 = ((bf16[16,512,128]{2,1,0:T(8,128)(2,1)}), bf16[16,512,128]{2,1,0:T(8,128)(2,1)}, u32[]{:S(2)}, u32[]{:S(2)}) async-start(bf16[16,512,128]{2,1,0:T(8,128)(2,1)} %get-tuple-element.28), calls=%async_computation.2 | async-start | bytes 4194304 | tf_op jit(solution)/shard_map/all_to_all | solution.py:316
  77.1 13.0 %attend1.1 = (bf16[16,512,128]{2,1,0:T(8,128)(2,1)}, f32[2,128]{1,0:T(2,128)}) custom-call(s32[32,8]{1,0:T(8,128)} %copy-done, f32[2,128]{1,0:T(2,128)} %bitcast.26, bf16[16,512,128]{2,1,0:T(8,128)(2,1)} %all-to-all-done.1.recv_ref), custom_call_target="tpu_custom_call" | custom-call | flops 24999999488 | bytes 4194304 | tf_op jit(solution)/shard_map/attend1/pallas_call | solution.py:279
  90.1 0.7 fusion.2
  90.8 3.2 %collective-permute-start.1 = (f32[4,128]{1,0:T(4,128)S(1)}, f32[4,128]{1,0:T(4,128)S(1)}, u32[]{:S(2)}, u32[]{:S(2)}) collective-permute-start(f32[4,128]{1,0:T(4,128)S(1)} %get-tuple-element.39), channel_id=1, source_target_pairs={{0,2},{1,3},{2,0},{3,1},{4,6},{5,7},{6,4},{7,5},{8,10},{9,11},{10,... | collective-permute-start | bytes 6152 | tf_op jit(solution)/shard_map/ppermute | solution.py:330
  94.1 0.6 collective-permute-start
  94.6 2.7 %collective-permute-start.2 = (f32[4,128]{1,0:T(4,128)S(1)}, f32[4,128]{1,0:T(4,128)S(1)}, u32[]{:S(2)}, u32[]{:S(2)}) collective-permute-start(f32[4,128]{1,0:T(4,128)S(1)} %get-tuple-element.39), channel_id=1, source_target_pairs={{0,3},{1,0},{2,1},{3,2},{4,7},{5,4},{6,5},{7,6},{8,11},{9,8},{10,9... | collective-permute-start | bytes 6152 | tf_op jit(solution)/shard_map/ppermute | solution.py:330
  97.3 4.8 %collective-permute-done = f32[4,128]{1,0:T(4,128)S(1)} collective-permute-done((f32[4,128]{1,0:T(4,128)S(1)}, f32[4,128]{1,0:T(4,128)S(1)}, u32[]{:S(2)}, u32[]{:S(2)}) %collective-permute-start) | collective-permute-done | bytes 2080 | tf_op jit(solution)/shard_map/ppermute | solution.py:330
  102.1 2.6 %all-to-all-done.2.recv_ref = bf16[16,512,128]{2,1,0:T(8,128)(2,1)} async-done(((bf16[16,512,128]{2,1,0:T(8,128)(2,1)}), bf16[16,512,128]{2,1,0:T(8,128)(2,1)}, u32[]{:S(2)}, u32[]{:S(2)}) %all-to-all-start.2) | async-done | bytes 2097184 | tf_op jit(solution)/shard_map/all_to_all | solution.py:316
  104.7 4.3 %all-to-all-start.3 = ((bf16[16,512,128]{2,1,0:T(8,128)(2,1)}), bf16[16,512,128]{2,1,0:T(8,128)(2,1)S(1)}, u32[]{:S(2)}, u32[]{:S(2)}) async-start(bf16[16,512,128]{2,1,0:T(8,128)(2,1)} %get-tuple-element.29), calls=%async_computation.3 | async-start | bytes 4194304 | tf_op jit(solution)/shard_map/all_to_all | solution.py:316
  109.1 0.1 collective-permute-start.3
  109.2 1.2 collective-permute-done.3
  110.3 1.0 collective-permute-start.4
  111.3 2.6 %collective-permute-done.4 = f32[4,4,128]{2,1,0:T(4,128)S(1)} collective-permute-done((f32[4,4,128]{2,1,0:T(4,128)S(1)}, f32[4,4,128]{2,1,0:T(4,128)S(1)}, u32[]{:S(2)}, u32[]{:S(2)}) %collective-permute-start.4) | collective-permute-done | bytes 8224 | tf_op jit(solution)/shard_map/ppermute | solution.py:320
  114.0 1.5 %collective-permute-start.5 = (f32[4,4,128]{2,1,0:T(4,128)S(1)}, f32[4,4,128]{2,1,0:T(4,128)S(1)}, u32[]{:S(2)}, u32[]{:S(2)}) collective-permute-start(f32[4,4,128]{2,1,0:T(4,128)S(1)} %add.24), channel_id=1, source_target_pairs={{0,64},{16,80},{32,96},{48,112},{64,0},{80,16},{96,32},{112,48},{1... | collective-permute-start | bytes 24584 | tf_op jit(solution)/shard_map/ppermute | solution.py:320
  115.4 3.1 %collective-permute-done.5 = f32[4,4,128]{2,1,0:T(4,128)S(1)} collective-permute-done((f32[4,4,128]{2,1,0:T(4,128)S(1)}, f32[4,4,128]{2,1,0:T(4,128)S(1)}, u32[]{:S(2)}, u32[]{:S(2)}) %collective-permute-start.5) | collective-permute-done | bytes 8224 | tf_op jit(solution)/shard_map/ppermute | solution.py:320
  118.5 7.6 %collective-permute-done.6 = f32[4,4,128]{2,1,0:T(4,128)S(1)} collective-permute-done((f32[4,4,128]{2,1,0:T(4,128)S(1)}, f32[4,4,128]{2,1,0:T(4,128)S(1)}, u32[]{:S(2)}, u32[]{:S(2)}) %collective-permute-start.6) | collective-permute-done | bytes 8224 | tf_op jit(solution)/shard_map/ppermute | solution.py:320
  126.1 3.1 %collective-permute-start.9 = (f32[4,4,128]{2,1,0:T(4,128)S(1)}, f32[4,4,128]{2,1,0:T(4,128)S(1)}, u32[]{:S(2)}, u32[]{:S(2)}) collective-permute-start(f32[4,4,128]{2,1,0:T(4,128)S(1)} %add.26), channel_id=1, source_target_pairs={{0,12},{1,13},{2,14},{3,15},{4,0},{5,1},{6,2},{7,3},{8,4},{9,5},{1... | collective-permute-start | bytes 24584 | tf_op jit(solution)/shard_map/ppermute | solution.py:330
  129.1 0.9 collective-permute-start.8
  130.0 0.9 collective-permute-start.7
  130.9 2.8 %unpack0.1 = (bf16[1,128,4096]{2,1,0:T(8,128)(2,1)}, bf16[1,128,4096]{2,1,0:T(8,128)(2,1)}, bf16[1,128,4096]{2,1,0:T(8,128)(2,1)}, bf16[1,128,4096]{2,1,0:T(8,128)(2,1)}) custom-call(bf16[16,512,128]{2,1,0:T(8,128)(2,1)} %all-to-all-done.2.recv_ref), custom_call_target="tpu_custom_call" | custom-call | bytes 8388608 | tf_op jit(solution)/shard_map/unpack0/pallas_call | solution.py:101
  133.7 1.4 %collective-permute-done.8 = f32[4,4,128]{2,1,0:T(4,128)S(1)} collective-permute-done((f32[4,4,128]{2,1,0:T(4,128)S(1)}, f32[4,4,128]{2,1,0:T(4,128)S(1)}, u32[]{:S(2)}, u32[]{:S(2)}) %collective-permute-start.8) | collective-permute-done | bytes 8224 | tf_op jit(solution)/shard_map/ppermute | solution.py:330
  135.2 1.8 %all-to-all-done.3.recv_ref = bf16[16,512,128]{2,1,0:T(8,128)(2,1)S(1)} async-done(((bf16[16,512,128]{2,1,0:T(8,128)(2,1)}), bf16[16,512,128]{2,1,0:T(8,128)(2,1)S(1)}, u32[]{:S(2)}, u32[]{:S(2)}) %all-to-all-start.3) | async-done | bytes 2097184 | tf_op jit(solution)/shard_map/all_to_all | solution.py:316
  136.9 1.6 %unpack1.1 = (bf16[1,128,4096]{2,1,0:T(8,128)(2,1)}, bf16[1,128,4096]{2,1,0:T(8,128)(2,1)}, bf16[1,128,4096]{2,1,0:T(8,128)(2,1)}, bf16[1,128,4096]{2,1,0:T(8,12...) custom-call(bf16[16,512,128]{2,1,0:T(8,128)(2,1)S(1)} %all-to-all-do, ...), custom_call_target="tpu_custom_call", output_to_operand_aliasing={{0}: (3, {}), {1}: (4, {}), {2}: (5, {}), {3}: (6, {})} | custom-call | bytes 8388608 | tf_op jit(solution)/shard_map/unpack1/pallas_call | solution.py:115
  (19 shorter events, 0.1 us)
Async XLA Ops:
  3.1 37.4 %all-to-all-start = ((bf16[16,512,128]{2,1,0:T(8,128)(2,1)}), bf16[16,512,128]{2,1,0:T(8,128)(2,1)S(1)}, u32[]{:S(2)}, u32[]{:S(2)}) async-start(bf16[16,512,128]{2,1,0:T(8,128)(2,1)} %pack0.1), calls=%async_computation | async-start | bytes 4194304 | tf_op jit(solution)/shard_map/all_to_all | solution.py:316
  10.1 2.5 %copy-start.3 = (s32[32,8]{0,1:T(8,128)S(1)}, s32[32,8]{0,1:T(8,128)}, u32[]{:S(2)}) copy-start(s32[32,8]{0,1:T(8,128)} %param.13) | copy-start | bytes 3076
  10.1 2.5 %copy-start.1 = (f32[32,128]{1,0:T(8,128)S(1)}, f32[32,128]{1,0:T(8,128)}, u32[]{:S(2)}) copy-start(f32[32,128]{1,0:T(8,128)} %param.11) | copy-start | bytes 49156
  10.2 2.5 %copy-start.2 = (f32[32,128]{1,0:T(8,128)S(1)}, f32[32,128]{1,0:T(8,128)}, u32[]{:S(2)}) copy-start(f32[32,128]{1,0:T(8,128)} %param.12) | copy-start | bytes 49156
  12.7 32.3 %copy-start = (s32[32,8]{1,0:T(8,128)}, s32[32,8]{1,0:T(8,128)S(1)}, u32[]{:S(2)}) copy-start(s32[32,8]{1,0:T(8,128)S(1)} %copy.17.ids_ref) | copy-start | bytes 3076
  40.5 32.1 %all-to-all-start.1 = ((bf16[16,512,128]{2,1,0:T(8,128)(2,1)}), bf16[16,512,128]{2,1,0:T(8,128)(2,1)}, u32[]{:S(2)}, u32[]{:S(2)}) async-start(bf16[16,512,128]{2,1,0:T(8,128)(2,1)} %pack1.1), calls=%async_computation.1 | async-start | bytes 4194304 | tf_op jit(solution)/shard_map/all_to_all | solution.py:316
  72.6 32.1 %all-to-all-start.2 = ((bf16[16,512,128]{2,1,0:T(8,128)(2,1)}), bf16[16,512,128]{2,1,0:T(8,128)(2,1)}, u32[]{:S(2)}, u32[]{:S(2)}) async-start(bf16[16,512,128]{2,1,0:T(8,128)(2,1)} %get-tuple-element.28), calls=%async_computation.2 | async-start | bytes 4194304 | tf_op jit(solution)/shard_map/all_to_all | solution.py:316
  90.8 6.5 %collective-permute-start.1 = (f32[4,128]{1,0:T(4,128)S(1)}, f32[4,128]{1,0:T(4,128)S(1)}, u32[]{:S(2)}, u32[]{:S(2)}) collective-permute-start(f32[4,128]{1,0:T(4,128)S(1)} %get-tuple-element.39), channel_id=1, source_target_pairs={{0,2},{1,3},{2,0},{3,1},{4,6},{5,7},{6,4},{7,5},{8,10},{9,11},{10,... | collective-permute-start | bytes 6152 | tf_op jit(solution)/shard_map/ppermute | solution.py:330
  94.1 8.0 %collective-permute-start = (f32[4,128]{1,0:T(4,128)S(1)}, f32[4,128]{1,0:T(4,128)S(1)}, u32[]{:S(2)}, u32[]{:S(2)}) collective-permute-start(f32[4,128]{1,0:T(4,128)S(1)} %get-tuple-element.39), channel_id=1, source_target_pairs={{0,1},{1,2},{2,3},{3,0},{4,5},{5,6},{6,7},{7,4},{8,9},{9,10},{10,1... | collective-permute-start | bytes 6152 | tf_op jit(solution)/shard_map/ppermute | solution.py:330
  94.6 7.5 %collective-permute-start.2 = (f32[4,128]{1,0:T(4,128)S(1)}, f32[4,128]{1,0:T(4,128)S(1)}, u32[]{:S(2)}, u32[]{:S(2)}) collective-permute-start(f32[4,128]{1,0:T(4,128)S(1)} %get-tuple-element.39), channel_id=1, source_target_pairs={{0,3},{1,0},{2,1},{3,2},{4,7},{5,4},{6,5},{7,6},{8,11},{9,8},{10,9... | collective-permute-start | bytes 6152 | tf_op jit(solution)/shard_map/ppermute | solution.py:330
  104.7 32.2 %all-to-all-start.3 = ((bf16[16,512,128]{2,1,0:T(8,128)(2,1)}), bf16[16,512,128]{2,1,0:T(8,128)(2,1)S(1)}, u32[]{:S(2)}, u32[]{:S(2)}) async-start(bf16[16,512,128]{2,1,0:T(8,128)(2,1)} %get-tuple-element.29), calls=%async_computation.3 | async-start | bytes 4194304 | tf_op jit(solution)/shard_map/all_to_all | solution.py:316
  109.1 1.3 collective-permute-start.3
  110.3 3.7 %collective-permute-start.4 = (f32[4,4,128]{2,1,0:T(4,128)S(1)}, f32[4,4,128]{2,1,0:T(4,128)S(1)}, u32[]{:S(2)}, u32[]{:S(2)}) collective-permute-start(f32[4,4,128]{2,1,0:T(4,128)S(1)} %add.23), channel_id=1, source_target_pairs={{0,32},{16,48},{32,0},{48,16},{64,96},{80,112},{96,64},{112,80},{1... | collective-permute-start | bytes 24584 | tf_op jit(solution)/shard_map/ppermute | solution.py:320
  114.0 4.5 %collective-permute-start.5 = (f32[4,4,128]{2,1,0:T(4,128)S(1)}, f32[4,4,128]{2,1,0:T(4,128)S(1)}, u32[]{:S(2)}, u32[]{:S(2)}) collective-permute-start(f32[4,4,128]{2,1,0:T(4,128)S(1)} %add.24), channel_id=1, source_target_pairs={{0,64},{16,80},{32,96},{48,112},{64,0},{80,16},{96,32},{112,48},{1... | collective-permute-start | bytes 24584 | tf_op jit(solution)/shard_map/ppermute | solution.py:320
  118.5 7.6 %collective-permute-start.6 = (f32[4,4,128]{2,1,0:T(4,128)S(1)}, f32[4,4,128]{2,1,0:T(4,128)S(1)}, u32[]{:S(2)}, u32[]{:S(2)}) collective-permute-start(f32[4,4,128]{2,1,0:T(4,128)S(1)} %add.25), channel_id=1, source_target_pairs={{0,128},{16,144},{32,160},{48,176},{64,192},{80,208},{96,224},{112... | collective-permute-start | bytes 24584 | tf_op jit(solution)/shard_map/ppermute | solution.py:320
  126.1 7.6 %collective-permute-start.9 = (f32[4,4,128]{2,1,0:T(4,128)S(1)}, f32[4,4,128]{2,1,0:T(4,128)S(1)}, u32[]{:S(2)}, u32[]{:S(2)}) collective-permute-start(f32[4,4,128]{2,1,0:T(4,128)S(1)} %add.26), channel_id=1, source_target_pairs={{0,12},{1,13},{2,14},{3,15},{4,0},{5,1},{6,2},{7,3},{8,4},{9,5},{1... | collective-permute-start | bytes 24584 | tf_op jit(solution)/shard_map/ppermute | solution.py:330
  129.1 6.0 %collective-permute-start.8 = (f32[4,4,128]{2,1,0:T(4,128)S(1)}, f32[4,4,128]{2,1,0:T(4,128)S(1)}, u32[]{:S(2)}, u32[]{:S(2)}) collective-permute-start(f32[4,4,128]{2,1,0:T(4,128)S(1)} %add.26), channel_id=1, source_target_pairs={{0,8},{1,9},{2,10},{3,11},{4,12},{5,13},{6,14},{7,15},{8,0},{9,1},... | collective-permute-start | bytes 24584 | tf_op jit(solution)/shard_map/ppermute | solution.py:330
  130.0 5.2 %collective-permute-start.7 = (f32[4,4,128]{2,1,0:T(4,128)S(1)}, f32[4,4,128]{2,1,0:T(4,128)S(1)}, u32[]{:S(2)}, u32[]{:S(2)}) collective-permute-start(f32[4,4,128]{2,1,0:T(4,128)S(1)} %add.26), channel_id=1, source_target_pairs={{0,4},{1,5},{2,6},{3,7},{4,8},{5,9},{6,10},{7,11},{8,12},{9,13},{1... | collective-permute-start | bytes 24584 | tf_op jit(solution)/shard_map/ppermute | solution.py:330

commit v7 on v6

--- a/solution.py
+++ b/solution.py
@@ -349,11 +349,13 @@
     part = ring_of(jnp.concatenate([gain0, gain1], axis=0), 1)
     part, back1, out0 = lax.optimization_barrier((part, back1, out0))
     out1 = swap(back1, "seq")
-    for step in (1, 2, 4, 8):
+    for step in (1, 2, 4):
         part = part + far(part, "dp", step)
-    part = ring_of(part, SIDE).reshape(SEQ, 2 * CHUNKS, HEAD)
+    part, out0 = lax.optimization_barrier((part, out0))
+    done, other = lax.optimization_barrier((tuple(unpack(out0)), far(part, "dp", 14)))
+    part = ring_of(part + other, SIDE).reshape(SEQ, 2 * CHUNKS, HEAD)
     factor = (TOKENS * lax.axis_size("dp")) ** -0.5
-    return tuple(last_unpack(factor, out1, part, s.reshape(1), unpack(out0)))
+    return tuple(last_unpack(factor, out1, part, s.reshape(1), done))
 
 
 def solution(mesh):

time: 139 us -> 139 us (level)
    ppermute x4, waiting for transfers between devices: 14.4 us -> 8.81 us  [far(): lax.ppermute(x, axis, [(i, i ^ step) for i in range(lax.axis_size(axis))])]
    ppermute x6, waiting for transfers between devices: 6.3 us -> 11.7 us  [ring_of(): held.append(lax.ppermute(x, 'seq', turn))]
where the time goes in v7:
time: 139 us
  waiting for transfers between devices  68.2 us (49%)
  starting transfers between devices  34.2 us (25%)
  Pallas kernels  34 us (24%)
    all_to_all x4, waiting for transfers between devices, swap(): return lax.all_to_all(x, axis, split_axis=0, concat_axis=0, tiled=True)  47.7 us
    pallas_call x2, Pallas kernels, attend(): pl.pallas_call(functools.partial(attend_kernel, group=group), out_shape=(...  24.7 us
    all_to_all x4, starting transfers between devices, swap(): return lax.all_to_all(x, axis, split_axis=0, concat_axis=0, tiled=True)  20.3 us
    ppermute x6, waiting for transfers between devices, ring_of(): held.append(lax.ppermute(x, 'seq', turn))  11.7 us
    ppermute x6, starting transfers between devices, ring_of(): held.append(lax.ppermute(x, 'seq', turn))  11.2 us
    ppermute x4, waiting for transfers between devices, far(): lax.ppermute(x, axis, [(i, i ^ step) for i in range(lax.axis_size(axis))])  8.81 us
    pallas_call x2, Pallas kernels, pack(): pl.pallas_call(functools.partial(pack_kernel, chunk), out_shape=pltpu.HBM...  4.85 us
    pallas_call x1, Pallas kernels, unpack(): pl.pallas_call(unpack_kernel, grid=(steps,), out_shape=(jax.ShapeDtypeStr...  2.81 us
  transfers between devices with their start and end apart: 14, of which 11 were waited for; matrix products, arithmetic and copies ran while one was open for 1% of the time, Pallas kernels for 22%

profile of v7, /device:TPU:128, one launch (start us, length us, event | category | flops | bytes accessed | tf_op | source)
XLA Modules:
  0.0 138.6 jit_solution(8936337443024479880)
XLA Ops:
  0.6 2.4 %pack0.1 = bf16[16,512,128]{2,1,0:T(8,128)(2,1)} custom-call(bf16[1,128,4096]{2,1,0:T(8,128)(2,1)} %q_ref.3, bf16[1,128,4096]{2,1,0:T(8,128)(2,1)} %k_ref.3, bf16[1,128,4096]{2,1,0:T(8,128)(2,1)} %v_ref.3, bf16[1,128,4096]{2,1,0:T(8,128)(2,1)} %g_ref.3), custom_call_target="tpu_custom_call" | custom-call | bytes 8388608 | tf_op jit(solution)/shard_map/pack0/pallas_call | solution.py:58
  3.1 7.0 %all-to-all-start = ((bf16[16,512,128]{2,1,0:T(8,128)(2,1)}), bf16[16,512,128]{2,1,0:T(8,128)(2,1)S(1)}, u32[]{:S(2)}, u32[]{:S(2)}) async-start(bf16[16,512,128]{2,1,0:T(8,128)(2,1)} %pack0.1), calls=%async_computation | async-start | bytes 4194304 | tf_op jit(solution)/shard_map/all_to_all | solution.py:316
  10.2 2.4 %pack1.1 = bf16[16,512,128]{2,1,0:T(8,128)(2,1)} custom-call(bf16[1,128,4096]{2,1,0:T(8,128)(2,1)} %q_ref.3, bf16[1,128,4096]{2,1,0:T(8,128)(2,1)} %k_ref.3, bf16[1,128,4096]{2,1,0:T(8,128)(2,1)} %v_ref.3, bf16[1,128,4096]{2,1,0:T(8,128)(2,1)} %g_ref.3), custom_call_target="tpu_custom_call" | custom-call | bytes 8388608 | tf_op jit(solution)/shard_map/pack1/pallas_call | solution.py:58
  12.7 0.6 fusion.1
  13.3 27.2 %all-to-all-done.recv_ref = bf16[16,512,128]{2,1,0:T(8,128)(2,1)S(1)} async-done(((bf16[16,512,128]{2,1,0:T(8,128)(2,1)}), bf16[16,512,128]{2,1,0:T(8,128)(2,1)S(1)}, u32[]{:S(2)}, u32[]{:S(2)}) %all-to-all-start) | async-done | bytes 2097184 | tf_op jit(solution)/shard_map/all_to_all | solution.py:316
  40.5 4.4 %all-to-all-start.1 = ((bf16[16,512,128]{2,1,0:T(8,128)(2,1)}), bf16[16,512,128]{2,1,0:T(8,128)(2,1)}, u32[]{:S(2)}, u32[]{:S(2)}) async-start(bf16[16,512,128]{2,1,0:T(8,128)(2,1)} %pack1.1), calls=%async_computation.1 | async-start | bytes 4194304 | tf_op jit(solution)/shard_map/all_to_all | solution.py:316
  45.0 11.7 %attend0.1 = (bf16[16,512,128]{2,1,0:T(8,128)(2,1)}, f32[2,128]{1,0:T(2,128)S(1)}) custom-call(s32[32,8]{1,0:T(8,128)S(1)} %copy.17.ids_ref, f32[2,128]{1,0:T(2,128)S(1)} %bitcast.16, bf16[16,512,128]{2,1,0:T(8,128)(2,1)S(1)} %all-to-all-done.recv_ref), custom_call_target="tpu_custom_call" | custom-call | flops 24999999488 | bytes 4194304 | tf_op jit(solution)/shard_map/attend0/pallas_call | solution.py:279
  56.6 16.0 %all-to-all-done.1.recv_ref = bf16[16,512,128]{2,1,0:T(8,128)(2,1)} async-done(((bf16[16,512,128]{2,1,0:T(8,128)(2,1)}), bf16[16,512,128]{2,1,0:T(8,128)(2,1)}, u32[]{:S(2)}, u32[]{:S(2)}) %all-to-all-start.1) | async-done | bytes 2097184 | tf_op jit(solution)/shard_map/all_to_all | solution.py:316
  72.6 4.4 %all-to-all-start.2 = ((bf16[16,512,128]{2,1,0:T(8,128)(2,1)}), bf16[16,512,128]{2,1,0:T(8,128)(2,1)}, u32[]{:S(2)}, u32[]{:S(2)}) async-start(bf16[16,512,128]{2,1,0:T(8,128)(2,1)} %get-tuple-element.35), calls=%async_computation.2 | async-start | bytes 4194304 | tf_op jit(solution)/shard_map/all_to_all | solution.py:316
  77.1 13.0 %attend1.1 = (bf16[16,512,128]{2,1,0:T(8,128)(2,1)}, f32[2,128]{1,0:T(2,128)}) custom-call(s32[32,8]{1,0:T(8,128)} %copy-done, f32[2,128]{1,0:T(2,128)} %bitcast.26, bf16[16,512,128]{2,1,0:T(8,128)(2,1)} %all-to-all-done.1.recv_ref), custom_call_target="tpu_custom_call" | custom-call | flops 24999999488 | bytes 4194304 | tf_op jit(solution)/shard_map/attend1/pallas_call | solution.py:279
  90.1 0.7 fusion.2
  90.8 3.2 %collective-permute-start.1 = (f32[4,128]{1,0:T(4,128)S(1)}, f32[4,128]{1,0:T(4,128)S(1)}, u32[]{:S(2)}, u32[]{:S(2)}) collective-permute-start(f32[4,128]{1,0:T(4,128)S(1)} %get-tuple-element.53), channel_id=1, source_target_pairs={{0,2},{1,3},{2,0},{3,1},{4,6},{5,7},{6,4},{7,5},{8,10},{9,11},{10,... | collective-permute-start | bytes 6152 | tf_op jit(solution)/shard_map/ppermute | solution.py:330
  94.1 0.6 collective-permute-start
  94.6 2.7 %collective-permute-start.2 = (f32[4,128]{1,0:T(4,128)S(1)}, f32[4,128]{1,0:T(4,128)S(1)}, u32[]{:S(2)}, u32[]{:S(2)}) collective-permute-start(f32[4,128]{1,0:T(4,128)S(1)} %get-tuple-element.53), channel_id=1, source_target_pairs={{0,3},{1,0},{2,1},{3,2},{4,7},{5,4},{6,5},{7,6},{8,11},{9,8},{10,9... | collective-permute-start | bytes 6152 | tf_op jit(solution)/shard_map/ppermute | solution.py:330
  97.3 4.8 %collective-permute-done = f32[4,128]{1,0:T(4,128)S(1)} collective-permute-done((f32[4,128]{1,0:T(4,128)S(1)}, f32[4,128]{1,0:T(4,128)S(1)}, u32[]{:S(2)}, u32[]{:S(2)}) %collective-permute-start) | collective-permute-done | bytes 2080 | tf_op jit(solution)/shard_map/ppermute | solution.py:330
  102.1 2.6 %all-to-all-done.2.recv_ref = bf16[16,512,128]{2,1,0:T(8,128)(2,1)} async-done(((bf16[16,512,128]{2,1,0:T(8,128)(2,1)}), bf16[16,512,128]{2,1,0:T(8,128)(2,1)}, u32[]{:S(2)}, u32[]{:S(2)}) %all-to-all-start.2) | async-done | bytes 2097184 | tf_op jit(solution)/shard_map/all_to_all | solution.py:316
  104.7 4.3 %all-to-all-start.3 = ((bf16[16,512,128]{2,1,0:T(8,128)(2,1)}), bf16[16,512,128]{2,1,0:T(8,128)(2,1)S(1)}, u32[]{:S(2)}, u32[]{:S(2)}) async-start(bf16[16,512,128]{2,1,0:T(8,128)(2,1)} %get-tuple-element.36), calls=%async_computation.3 | async-start | bytes 4194304 | tf_op jit(solution)/shard_map/all_to_all | solution.py:316
  109.2 1.2 collective-permute-done.3
  110.3 1.0 collective-permute-start.4
  111.3 2.6 %collective-permute-done.4 = f32[4,4,128]{2,1,0:T(4,128)S(1)} collective-permute-done((f32[4,4,128]{2,1,0:T(4,128)S(1)}, f32[4,4,128]{2,1,0:T(4,128)S(1)}, u32[]{:S(2)}, u32[]{:S(2)}) %collective-permute-start.4) | collective-permute-done | bytes 8224 | tf_op jit(solution)/shard_map/ppermute | solution.py:320
  114.0 1.5 %collective-permute-start.5 = (f32[4,4,128]{2,1,0:T(4,128)S(1)}, f32[4,4,128]{2,1,0:T(4,128)S(1)}, u32[]{:S(2)}, u32[]{:S(2)}) collective-permute-start(f32[4,4,128]{2,1,0:T(4,128)S(1)} %add.24), channel_id=1, source_target_pairs={{0,64},{16,80},{32,96},{48,112},{64,0},{80,16},{96,32},{112,48},{1... | collective-permute-start | bytes 24584 | tf_op jit(solution)/shard_map/ppermute | solution.py:320
  115.4 3.1 %collective-permute-done.5 = f32[4,4,128]{2,1,0:T(4,128)S(1)} collective-permute-done((f32[4,4,128]{2,1,0:T(4,128)S(1)}, f32[4,4,128]{2,1,0:T(4,128)S(1)}, u32[]{:S(2)}, u32[]{:S(2)}) %collective-permute-start.5) | collective-permute-done | bytes 8224 | tf_op jit(solution)/shard_map/ppermute | solution.py:320
  118.5 0.1 collective-permute-start.6
  118.6 2.8 %unpack0.1 = (bf16[1,128,4096]{2,1,0:T(8,128)(2,1)}, bf16[1,128,4096]{2,1,0:T(8,128)(2,1)}, bf16[1,128,4096]{2,1,0:T(8,128)(2,1)}, bf16[1,128,4096]{2,1,0:T(8,128)(2,1)}) custom-call(bf16[16,512,128]{2,1,0:T(8,128)(2,1)} %all-to-all-done.2.recv_ref), custom_call_target="tpu_custom_call" | custom-call | bytes 8388608 | tf_op jit(solution)/shard_map/unpack0/pallas_call | solution.py:101
  121.4 1.9 %collective-permute-done.6 = f32[4,4,128]{2,1,0:T(4,128)S(1)} collective-permute-done((f32[4,4,128]{2,1,0:T(4,128)S(1)}, f32[4,4,128]{2,1,0:T(4,128)S(1)}, u32[]{:S(2)}, u32[]{:S(2)}) %collective-permute-start.6) | collective-permute-done | bytes 8224 | tf_op jit(solution)/shard_map/ppermute | solution.py:320
  123.4 3.1 %collective-permute-start.9 = (f32[4,4,128]{2,1,0:T(4,128)S(1)}, f32[4,4,128]{2,1,0:T(4,128)S(1)}, u32[]{:S(2)}, u32[]{:S(2)}) collective-permute-start(f32[4,4,128]{2,1,0:T(4,128)S(1)} %add.26), channel_id=1, source_target_pairs={{0,12},{1,13},{2,14},{3,15},{4,0},{5,1},{6,2},{7,3},{8,4},{9,5},{1... | collective-permute-start | bytes 24584 | tf_op jit(solution)/shard_map/ppermute | solution.py:330
  126.5 0.9 collective-permute-start.8
  127.3 0.9 collective-permute-start.7
  128.2 5.2 %collective-permute-done.9 = f32[4,4,128]{2,1,0:T(4,128)S(1)} collective-permute-done((f32[4,4,128]{2,1,0:T(4,128)S(1)}, f32[4,4,128]{2,1,0:T(4,128)S(1)}, u32[]{:S(2)}, u32[]{:S(2)}) %collective-permute-start.9) | collective-permute-done | bytes 8224 | tf_op jit(solution)/shard_map/ppermute | solution.py:330
  133.4 1.7 %collective-permute-done.8 = f32[4,4,128]{2,1,0:T(4,128)S(1)} collective-permute-done((f32[4,4,128]{2,1,0:T(4,128)S(1)}, f32[4,4,128]{2,1,0:T(4,128)S(1)}, u32[]{:S(2)}, u32[]{:S(2)}) %collective-permute-start.8) | collective-permute-done | bytes 8224 | tf_op jit(solution)/shard_map/ppermute | solution.py:330
  135.1 1.9 %all-to-all-done.3.recv_ref = bf16[16,512,128]{2,1,0:T(8,128)(2,1)S(1)} async-done(((bf16[16,512,128]{2,1,0:T(8,128)(2,1)}), bf16[16,512,128]{2,1,0:T(8,128)(2,1)S(1)}, u32[]{:S(2)}, u32[]{:S(2)}) %all-to-all-start.3) | async-done | bytes 2097184 | tf_op jit(solution)/shard_map/all_to_all | solution.py:316
  137.0 1.6 %unpack1.1 = (bf16[1,128,4096]{2,1,0:T(8,128)(2,1)}, bf16[1,128,4096]{2,1,0:T(8,128)(2,1)}, bf16[1,128,4096]{2,1,0:T(8,128)(2,1)}, bf16[1,128,4096]{2,1,0:T(8,12...) custom-call(bf16[16,512,128]{2,1,0:T(8,128)(2,1)S(1)} %all-to-all-do, ...), custom_call_target="tpu_custom_call", output_to_operand_aliasing={{0}: (3, {}), {1}: (4, {}), {2}: (5, {}), {3}: (6, {})} | custom-call | bytes 8388608 | tf_op jit(solution)/shard_map/unpack1/pallas_call | solution.py:115
  (19 shorter events, 0.2 us)
Async XLA Ops:
  3.1 37.4 %all-to-all-start = ((bf16[16,512,128]{2,1,0:T(8,128)(2,1)}), bf16[16,512,128]{2,1,0:T(8,128)(2,1)S(1)}, u32[]{:S(2)}, u32[]{:S(2)}) async-start(bf16[16,512,128]{2,1,0:T(8,128)(2,1)} %pack0.1), calls=%async_computation | async-start | bytes 4194304 | tf_op jit(solution)/shard_map/all_to_all | solution.py:316
  10.1 2.5 %copy-start.3 = (s32[32,8]{0,1:T(8,128)S(1)}, s32[32,8]{0,1:T(8,128)}, u32[]{:S(2)}) copy-start(s32[32,8]{0,1:T(8,128)} %param.13) | copy-start | bytes 3076
  10.1 2.5 %copy-start.1 = (f32[32,128]{1,0:T(8,128)S(1)}, f32[32,128]{1,0:T(8,128)}, u32[]{:S(2)}) copy-start(f32[32,128]{1,0:T(8,128)} %param.11) | copy-start | bytes 49156
  10.2 2.5 %copy-start.2 = (f32[32,128]{1,0:T(8,128)S(1)}, f32[32,128]{1,0:T(8,128)}, u32[]{:S(2)}) copy-start(f32[32,128]{1,0:T(8,128)} %param.12) | copy-start | bytes 49156
  12.7 32.3 %copy-start = (s32[32,8]{1,0:T(8,128)}, s32[32,8]{1,0:T(8,128)S(1)}, u32[]{:S(2)}) copy-start(s32[32,8]{1,0:T(8,128)S(1)} %copy.17.ids_ref) | copy-start | bytes 3076
  40.5 32.1 %all-to-all-start.1 = ((bf16[16,512,128]{2,1,0:T(8,128)(2,1)}), bf16[16,512,128]{2,1,0:T(8,128)(2,1)}, u32[]{:S(2)}, u32[]{:S(2)}) async-start(bf16[16,512,128]{2,1,0:T(8,128)(2,1)} %pack1.1), calls=%async_computation.1 | async-start | bytes 4194304 | tf_op jit(solution)/shard_map/all_to_all | solution.py:316
  72.6 32.1 %all-to-all-start.2 = ((bf16[16,512,128]{2,1,0:T(8,128)(2,1)}), bf16[16,512,128]{2,1,0:T(8,128)(2,1)}, u32[]{:S(2)}, u32[]{:S(2)}) async-start(bf16[16,512,128]{2,1,0:T(8,128)(2,1)} %get-tuple-element.35), calls=%async_computation.2 | async-start | bytes 4194304 | tf_op jit(solution)/shard_map/all_to_all | solution.py:316
  90.8 6.5 %collective-permute-start.1 = (f32[4,128]{1,0:T(4,128)S(1)}, f32[4,128]{1,0:T(4,128)S(1)}, u32[]{:S(2)}, u32[]{:S(2)}) collective-permute-start(f32[4,128]{1,0:T(4,128)S(1)} %get-tuple-element.53), channel_id=1, source_target_pairs={{0,2},{1,3},{2,0},{3,1},{4,6},{5,7},{6,4},{7,5},{8,10},{9,11},{10,... | collective-permute-start | bytes 6152 | tf_op jit(solution)/shard_map/ppermute | solution.py:330
  94.1 8.0 %collective-permute-start = (f32[4,128]{1,0:T(4,128)S(1)}, f32[4,128]{1,0:T(4,128)S(1)}, u32[]{:S(2)}, u32[]{:S(2)}) collective-permute-start(f32[4,128]{1,0:T(4,128)S(1)} %get-tuple-element.53), channel_id=1, source_target_pairs={{0,1},{1,2},{2,3},{3,0},{4,5},{5,6},{6,7},{7,4},{8,9},{9,10},{10,1... | collective-permute-start | bytes 6152 | tf_op jit(solution)/shard_map/ppermute | solution.py:330
  94.6 7.5 %collective-permute-start.2 = (f32[4,128]{1,0:T(4,128)S(1)}, f32[4,128]{1,0:T(4,128)S(1)}, u32[]{:S(2)}, u32[]{:S(2)}) collective-permute-start(f32[4,128]{1,0:T(4,128)S(1)} %get-tuple-element.53), channel_id=1, source_target_pairs={{0,3},{1,0},{2,1},{3,2},{4,7},{5,4},{6,5},{7,6},{8,11},{9,8},{10,9... | collective-permute-start | bytes 6152 | tf_op jit(solution)/shard_map/ppermute | solution.py:330
  104.7 32.2 %all-to-all-start.3 = ((bf16[16,512,128]{2,1,0:T(8,128)(2,1)}), bf16[16,512,128]{2,1,0:T(8,128)(2,1)S(1)}, u32[]{:S(2)}, u32[]{:S(2)}) async-start(bf16[16,512,128]{2,1,0:T(8,128)(2,1)} %get-tuple-element.36), calls=%async_computation.3 | async-start | bytes 4194304 | tf_op jit(solution)/shard_map/all_to_all | solution.py:316
  109.1 1.3 collective-permute-start.3
  110.3 3.7 %collective-permute-start.4 = (f32[4,4,128]{2,1,0:T(4,128)S(1)}, f32[4,4,128]{2,1,0:T(4,128)S(1)}, u32[]{:S(2)}, u32[]{:S(2)}) collective-permute-start(f32[4,4,128]{2,1,0:T(4,128)S(1)} %add.23), channel_id=1, source_target_pairs={{0,32},{16,48},{32,0},{48,16},{64,96},{80,112},{96,64},{112,80},{1... | collective-permute-start | bytes 24584 | tf_op jit(solution)/shard_map/ppermute | solution.py:320
  114.0 4.5 %collective-permute-start.5 = (f32[4,4,128]{2,1,0:T(4,128)S(1)}, f32[4,4,128]{2,1,0:T(4,128)S(1)}, u32[]{:S(2)}, u32[]{:S(2)}) collective-permute-start(f32[4,4,128]{2,1,0:T(4,128)S(1)} %add.24), channel_id=1, source_target_pairs={{0,64},{16,80},{32,96},{48,112},{64,0},{80,16},{96,32},{112,48},{1... | collective-permute-start | bytes 24584 | tf_op jit(solution)/shard_map/ppermute | solution.py:320
  118.5 4.9 %collective-permute-start.6 = (f32[4,4,128]{2,1,0:T(4,128)S(1)}, f32[4,4,128]{2,1,0:T(4,128)S(1)}, u32[]{:S(2)}, u32[]{:S(2)}) collective-permute-start(f32[4,4,128]{2,1,0:T(4,128)S(1)} %add.25), channel_id=1, source_target_pairs={{0,224},{16,240},{32,192},{48,208},{64,160},{80,176},{96,128},{112... | collective-permute-start | bytes 24584 | tf_op jit(solution)/shard_map/ppermute | solution.py:320
  123.4 10.0 %collective-permute-start.9 = (f32[4,4,128]{2,1,0:T(4,128)S(1)}, f32[4,4,128]{2,1,0:T(4,128)S(1)}, u32[]{:S(2)}, u32[]{:S(2)}) collective-permute-start(f32[4,4,128]{2,1,0:T(4,128)S(1)} %add.26), channel_id=1, source_target_pairs={{0,12},{1,13},{2,14},{3,15},{4,0},{5,1},{6,2},{7,3},{8,4},{9,5},{1... | collective-permute-start | bytes 24584 | tf_op jit(solution)/shard_map/ppermute | solution.py:330
  126.5 8.6 %collective-permute-start.8 = (f32[4,4,128]{2,1,0:T(4,128)S(1)}, f32[4,4,128]{2,1,0:T(4,128)S(1)}, u32[]{:S(2)}, u32[]{:S(2)}) collective-permute-start(f32[4,4,128]{2,1,0:T(4,128)S(1)} %add.26), channel_id=1, source_target_pairs={{0,8},{1,9},{2,10},{3,11},{4,12},{5,13},{6,14},{7,15},{8,0},{9,1},... | collective-permute-start | bytes 24584 | tf_op jit(solution)/shard_map/ppermute | solution.py:330
  127.3 7.8 %collective-permute-start.7 = (f32[4,4,128]{2,1,0:T(4,128)S(1)}, f32[4,4,128]{2,1,0:T(4,128)S(1)}, u32[]{:S(2)}, u32[]{:S(2)}) collective-permute-start(f32[4,4,128]{2,1,0:T(4,128)S(1)} %add.26), channel_id=1, source_target_pairs={{0,4},{1,5},{2,6},{3,7},{4,8},{5,9},{6,10},{7,11},{8,12},{9,13},{1... | collective-permute-start | bytes 24584 | tf_op jit(solution)/shard_map/ppermute | solution.py:330

commit v8 on v7

--- a/solution.py
+++ b/solution.py
@@ -24,28 +24,26 @@
 SIDE = 4
 
 
-def pack_kernel(chunk, q_ref, k_ref, v_ref, g_ref, send_ref, held_ref, in_sems, out_sems):
-    def fetch(part):
+def pack_one(chunk, refs, send_ref, held_ref, in_sems, out_sems):
+    parts = SEQ // PACKED
+
+    def whole(part):
+        return held_ref.at[pl.ds(part * PACKED, PACKED)]
+
+    def leave(part):
+        return pltpu.make_async_copy(
+            whole(part), send_ref.at[pl.ds(part * PACKED, PACKED)], out_sems.at[part]
+        )
+
+    for part in range(parts):
         for n in range(part * PACKED, (part + 1) * PACKED):
             columns = pl.ds((chunk * SEQ + n) * HEAD, HEAD)
-            for a, ref in enumerate((q_ref, k_ref, v_ref, g_ref)):
+            for a, ref in enumerate(refs):
                 pltpu.make_async_copy(
                     ref.at[0, :, columns],
                     held_ref.at[n, pl.ds(a * TOK, TOK), :],
                     in_sems.at[part],
                 ).start()
-
-    def whole(part):
-        return held_ref.at[pl.ds(part * PACKED, PACKED)]
-
-    def leave(part):
-        return pltpu.make_async_copy(
-            whole(part), send_ref.at[pl.ds(part * PACKED, PACKED)], out_sems.at[part]
-        )
-
-    parts = SEQ // PACKED
-    for part in range(parts):
-        fetch(part)
     for part in range(parts):
         pltpu.make_async_copy(whole(part), whole(part), in_sems.at[part]).wait()
         leave(part).start()
@@ -53,21 +51,39 @@
         leave(part).wait()
 
 
-def pack(chunk, arrays):
+def pack_first_kernel(core_ref, q_ref, k_ref, v_ref, g_ref, first_ref, second_ref, *scratch):
+    refs = (q_ref, k_ref, v_ref, g_ref)
+
+    @pl.when(core_ref[0] == 1)
+    def _():
+        pack_one(1, refs, second_ref, *scratch)
+
+    pack_one(0, refs, first_ref, *scratch)
+
+
+def pack_second_kernel(core_ref, q_ref, k_ref, v_ref, g_ref, _, second_ref, *scratch):
+    @pl.when(core_ref[0] == 0)
+    def _():
+        pack_one(1, (q_ref, k_ref, v_ref, g_ref), second_ref, *scratch)
+
+
+def pack(kernel, outputs, core, *arrays):
     parts = SEQ // PACKED
+    some = pl.BlockSpec(memory_space=pl.ANY)
     return pl.pallas_call(
-        functools.partial(pack_kernel, chunk),
-        out_shape=pltpu.HBM((SEQ, 4 * TOK, HEAD), jnp.bfloat16),
-        in_specs=[pl.BlockSpec(memory_space=pl.ANY)] * 4,
-        out_specs=pl.BlockSpec(memory_space=pl.ANY),
+        kernel,
+        out_shape=(pltpu.HBM((SEQ, 4 * TOK, HEAD), jnp.bfloat16),) * outputs,
+        in_specs=[pl.BlockSpec(memory_space=pltpu.SMEM)] + [some] * len(arrays),
+        out_specs=(some,) * outputs,
+        input_output_aliases={5: 0} if len(arrays) == 5 else {},
         scratch_shapes=[
             pltpu.VMEM((SEQ, 4 * TOK, HEAD), jnp.bfloat16),
             pltpu.SemaphoreType.DMA((parts,)),
             pltpu.SemaphoreType.DMA((parts,)),
         ],
         cost_estimate=pl.CostEstimate(flops=0, bytes_accessed=8 << 20, transcendentals=0),
-        name=f"pack{chunk}",
-    )(*arrays)
+        name=f"pack{2 - outputs}",
+    )(core, *arrays)
 
 
 def unpack_kernel(recv_ref, *refs):
@@ -338,9 +354,11 @@
     gains = [
         lax.dynamic_index_in_dim(both, c * SEQ + s, 0, keepdims=False) for c in range(CHUNKS)
     ]
-    sent0 = pack(0, arrays)
+    core = (lax.axis_index("dp") % 2).reshape(1)
+    sent0, sent1 = pack(pack_first_kernel, 2, core, *arrays)
     in0 = swap(sent0, "seq")
-    sent1, in0 = lax.optimization_barrier((pack(1, arrays), in0))
+    (sent1,) = pack(pack_second_kernel, 1, core, *arrays, sent1)
+    sent1, in0 = lax.optimization_barrier((sent1, in0))
     in1 = swap(sent1, "seq")
     back0, gain0 = attend(0, block_ids, gains[0], in0)
     back0, in1 = lax.optimization_barrier((back0, in1))

time: 139 us -> 147 us (1.058)
  waiting for transfers between devices: 68.2 us -> 73.9 us
  starting transfers between devices: 34.2 us -> 36.5 us
    all_to_all x4, waiting for transfers between devices: 47.7 us -> 53.8 us  [swap(): return lax.all_to_all(x, axis, split_axis=0, concat_axis=0, tiled=True)]
    all_to_all x4, starting transfers between devices: 20.3 us -> 22.4 us  [swap(): return lax.all_to_all(x, axis, split_axis=0, concat_axis=0, tiled=True)]
  transfers between devices with their start and end apart: 14 -> 14, of which waited for: 11 -> 12; matrix products, arithmetic and copies ran while one was open for 1% -> 1% of each run, Pallas kernels for 22% -> 20%
where the time goes in v8:
time: 147 us
  waiting for transfers between devices  73.9 us (50%)
  starting transfers between devices  36.5 us (25%)
  Pallas kernels  34 us (23%)
    all_to_all x4, waiting for transfers between devices, swap(): return lax.all_to_all(x, axis, split_axis=0, concat_axis=0, tiled=True)  53.8 us
    pallas_call x2, Pallas kernels, attend(): pl.pallas_call(functools.partial(attend_kernel, group=group), out_shape=(...  24.7 us
    all_to_all x4, starting transfers between devices, swap(): return lax.all_to_all(x, axis, split_axis=0, concat_axis=0, tiled=True)  22.4 us
    ppermute x6, starting transfers between devices, ring_of(): held.append(lax.ppermute(x, 'seq', turn))  11.4 us
    ppermute x6, waiting for transfers between devices, ring_of(): held.append(lax.ppermute(x, 'seq', turn))  11.3 us
    ppermute x4, waiting for transfers between devices, far(): lax.ppermute(x, axis, [(i, i ^ step) for i in range(lax.axis_size(axis))])  8.81 us
    pallas_call x2, Pallas kernels, pack(): pl.pallas_call(kernel, out_shape=(pltpu.HBM((SEQ, 4 * TOK, HEAD), jnp.bfl...  4.92 us
  transfers between devices with their start and end apart: 14, of which 12 were waited for; matrix products, arithmetic and copies ran while one was open for 1% of the time, Pallas kernels for 20%

profile of v8, /device:TPU:128, one launch (start us, length us, event | category | flops | bytes accessed | tf_op | source)
XLA Modules:
  0.0 146.5 jit_solution(1346217761386661587)
XLA Ops:
  0.6 2.4 %pack0.1 = (bf16[16,512,128]{2,1,0:T(8,128)(2,1)}, bf16[16,512,128]{2,1,0:T(8,128)(2,1)}) custom-call(s32[1]{0:T(128)} %bitcast.3.core_ref, bf16[1,128,4096]{2,1,0:T(8,128)(2,1)} %q_ref.3, bf16[1,128,4096]{2,1,0:T(8,128)(2,1)} %k_ref.3, bf16[1,128,4096]{2,1,0:T(8,128)(2,1)} %v_ref.3, bf16[1,128,4096]{2,1,0:T(8,128)(2,1)} %g_ref.3), custom_call_target="tpu_custom_call" | custom-call | bytes 8388608 | tf_op jit(solution)/shard_map/pack0/pallas_call | solution.py:73
  3.1 7.0 %all-to-all-start = ((bf16[16,512,128]{2,1,0:T(8,128)(2,1)}), bf16[16,512,128]{2,1,0:T(8,128)(2,1)S(1)}, u32[]{:S(2)}, u32[]{:S(2)}) async-start(bf16[16,512,128]{2,1,0:T(8,128)(2,1)} %get-tuple-element.31), calls=%async_computation | async-start | bytes 4194304 | tf_op jit(solution)/shard_map/all_to_all | solution.py:332
  10.3 2.5 %pack1.1 = bf16[16,512,128]{2,1,0:T(8,128)(2,1)} custom-call(s32[1]{0:T(128)} %bitcast.3.core_ref, bf16[1,128,4096]{2,1,0:T(8,128)(2,1)} %q_ref.3, bf16[1,128,4096]{2,1,0:T(8,128)(2,1)} %k_ref.3, bf16[1,128,4096]{2,1,0:T(8,128)(2,1)} %v_ref.3, bf16[1,128,4096]{2,1,0:T(8,128)(2,1)} %g_ref.3, ...), custom_call_target="tpu_custom_call", output_to_operand_aliasing={{}: (5, {})} | custom-call | bytes 8388608 | tf_op jit(solution)/shard_map/pack1/pallas_call | solution.py:73
  12.8 0.6 fusion.1
  13.3 27.2 %all-to-all-done.recv_ref = bf16[16,512,128]{2,1,0:T(8,128)(2,1)S(1)} async-done(((bf16[16,512,128]{2,1,0:T(8,128)(2,1)}), bf16[16,512,128]{2,1,0:T(8,128)(2,1)S(1)}, u32[]{:S(2)}, u32[]{:S(2)}) %all-to-all-start) | async-done | bytes 2097184 | tf_op jit(solution)/shard_map/all_to_all | solution.py:332
  40.5 5.2 %all-to-all-start.1 = ((bf16[16,512,128]{2,1,0:T(8,128)(2,1)}), bf16[16,512,128]{2,1,0:T(8,128)(2,1)}, u32[]{:S(2)}, u32[]{:S(2)}) async-start(bf16[16,512,128]{2,1,0:T(8,128)(2,1)} %pack1.1), calls=%async_computation.1 | async-start | bytes 4194304 | tf_op jit(solution)/shard_map/all_to_all | solution.py:332
  45.8 11.7 %attend0.1 = (bf16[16,512,128]{2,1,0:T(8,128)(2,1)}, f32[2,128]{1,0:T(2,128)S(1)}) custom-call(s32[32,8]{1,0:T(8,128)S(1)} %copy.18.ids_ref, f32[2,128]{1,0:T(2,128)S(1)} %bitcast.17, bf16[16,512,128]{2,1,0:T(8,128)(2,1)S(1)} %all-to-all-done.recv_ref), custom_call_target="tpu_custom_call" | custom-call | flops 24999999488 | bytes 4194304 | tf_op jit(solution)/shard_map/attend0/pallas_call | solution.py:295
  57.4 19.1 %all-to-all-done.1.recv_ref = bf16[16,512,128]{2,1,0:T(8,128)(2,1)} async-done(((bf16[16,512,128]{2,1,0:T(8,128)(2,1)}), bf16[16,512,128]{2,1,0:T(8,128)(2,1)}, u32[]{:S(2)}, u32[]{:S(2)}) %all-to-all-start.1) | async-done | bytes 2097184 | tf_op jit(solution)/shard_map/all_to_all | solution.py:332
  76.5 6.4 %all-to-all-start.2 = ((bf16[16,512,128]{2,1,0:T(8,128)(2,1)}), bf16[16,512,128]{2,1,0:T(8,128)(2,1)}, u32[]{:S(2)}, u32[]{:S(2)}) async-start(bf16[16,512,128]{2,1,0:T(8,128)(2,1)} %get-tuple-element.39), calls=%async_computation.2 | async-start | bytes 4194304 | tf_op jit(solution)/shard_map/all_to_all | solution.py:332
  82.9 13.0 %attend1.1 = (bf16[16,512,128]{2,1,0:T(8,128)(2,1)}, f32[2,128]{1,0:T(2,128)}) custom-call(s32[32,8]{1,0:T(8,128)} %copy-done, f32[2,128]{1,0:T(2,128)} %bitcast.27, bf16[16,512,128]{2,1,0:T(8,128)(2,1)} %all-to-all-done.1.recv_ref), custom_call_target="tpu_custom_call" | custom-call | flops 24999999488 | bytes 4194304 | tf_op jit(solution)/shard_map/attend1/pallas_call | solution.py:295
  95.9 0.7 fusion.2
  96.6 3.4 %collective-permute-start.1 = (f32[4,128]{1,0:T(4,128)S(1)}, f32[4,128]{1,0:T(4,128)S(1)}, u32[]{:S(2)}, u32[]{:S(2)}) collective-permute-start(f32[4,128]{1,0:T(4,128)S(1)} %get-tuple-element.57), channel_id=1, source_target_pairs={{0,2},{1,3},{2,0},{3,1},{4,6},{5,7},{6,4},{7,5},{8,10},{9,11},{10,... | collective-permute-start | bytes 6152 | tf_op jit(solution)/shard_map/ppermute | solution.py:346
  100.0 0.6 collective-permute-start
  100.5 2.7 %collective-permute-start.2 = (f32[4,128]{1,0:T(4,128)S(1)}, f32[4,128]{1,0:T(4,128)S(1)}, u32[]{:S(2)}, u32[]{:S(2)}) collective-permute-start(f32[4,128]{1,0:T(4,128)S(1)} %get-tuple-element.57), channel_id=1, source_target_pairs={{0,3},{1,0},{2,1},{3,2},{4,7},{5,4},{6,5},{7,6},{8,11},{9,8},{10,9... | collective-permute-start | bytes 6152 | tf_op jit(solution)/shard_map/ppermute | solution.py:346
  103.2 4.6 %collective-permute-done = f32[4,128]{1,0:T(4,128)S(1)} collective-permute-done((f32[4,128]{1,0:T(4,128)S(1)}, f32[4,128]{1,0:T(4,128)S(1)}, u32[]{:S(2)}, u32[]{:S(2)}) %collective-permute-start) | collective-permute-done | bytes 2080 | tf_op jit(solution)/shard_map/ppermute | solution.py:346
  107.9 5.2 %all-to-all-done.2.recv_ref = bf16[16,512,128]{2,1,0:T(8,128)(2,1)} async-done(((bf16[16,512,128]{2,1,0:T(8,128)(2,1)}), bf16[16,512,128]{2,1,0:T(8,128)(2,1)}, u32[]{:S(2)}, u32[]{:S(2)}) %all-to-all-start.2) | async-done | bytes 2097184 | tf_op jit(solution)/shard_map/all_to_all | solution.py:332
  113.1 3.8 %all-to-all-start.3 = ((bf16[16,512,128]{2,1,0:T(8,128)(2,1)}), bf16[16,512,128]{2,1,0:T(8,128)(2,1)S(1)}, u32[]{:S(2)}, u32[]{:S(2)}) async-start(bf16[16,512,128]{2,1,0:T(8,128)(2,1)} %get-tuple-element.40), calls=%async_computation.3 | async-start | bytes 4194304 | tf_op jit(solution)/shard_map/all_to_all | solution.py:332
  116.9 1.2 collective-permute-done.3
  118.1 1.0 collective-permute-start.4
  119.1 2.6 %collective-permute-done.4 = f32[4,4,128]{2,1,0:T(4,128)S(1)} collective-permute-done((f32[4,4,128]{2,1,0:T(4,128)S(1)}, f32[4,4,128]{2,1,0:T(4,128)S(1)}, u32[]{:S(2)}, u32[]{:S(2)}) %collective-permute-start.4) | collective-permute-done | bytes 8224 | tf_op jit(solution)/shard_map/ppermute | solution.py:336
  121.8 1.5 %collective-permute-start.5 = (f32[4,4,128]{2,1,0:T(4,128)S(1)}, f32[4,4,128]{2,1,0:T(4,128)S(1)}, u32[]{:S(2)}, u32[]{:S(2)}) collective-permute-start(f32[4,4,128]{2,1,0:T(4,128)S(1)} %add.29), channel_id=1, source_target_pairs={{0,64},{16,80},{32,96},{48,112},{64,0},{80,16},{96,32},{112,48},{1... | collective-permute-start | bytes 24584 | tf_op jit(solution)/shard_map/ppermute | solution.py:336
  123.2 3.1 %collective-permute-done.5 = f32[4,4,128]{2,1,0:T(4,128)S(1)} collective-permute-done((f32[4,4,128]{2,1,0:T(4,128)S(1)}, f32[4,4,128]{2,1,0:T(4,128)S(1)}, u32[]{:S(2)}, u32[]{:S(2)}) %collective-permute-start.5) | collective-permute-done | bytes 8224 | tf_op jit(solution)/shard_map/ppermute | solution.py:336
  126.4 2.8 %unpack0.1 = (bf16[1,128,4096]{2,1,0:T(8,128)(2,1)}, bf16[1,128,4096]{2,1,0:T(8,128)(2,1)}, bf16[1,128,4096]{2,1,0:T(8,128)(2,1)}, bf16[1,128,4096]{2,1,0:T(8,128)(2,1)}) custom-call(bf16[16,512,128]{2,1,0:T(8,128)(2,1)} %all-to-all-done.2.recv_ref), custom_call_target="tpu_custom_call" | custom-call | bytes 8388608 | tf_op jit(solution)/shard_map/unpack0/pallas_call | solution.py:117
  129.2 1.9 %collective-permute-done.6 = f32[4,4,128]{2,1,0:T(4,128)S(1)} collective-permute-done((f32[4,4,128]{2,1,0:T(4,128)S(1)}, f32[4,4,128]{2,1,0:T(4,128)S(1)}, u32[]{:S(2)}, u32[]{:S(2)}) %collective-permute-start.6) | collective-permute-done | bytes 8224 | tf_op jit(solution)/shard_map/ppermute | solution.py:336
  131.2 3.1 %collective-permute-start.9 = (f32[4,4,128]{2,1,0:T(4,128)S(1)}, f32[4,4,128]{2,1,0:T(4,128)S(1)}, u32[]{:S(2)}, u32[]{:S(2)}) collective-permute-start(f32[4,4,128]{2,1,0:T(4,128)S(1)} %add.31), channel_id=1, source_target_pairs={{0,12},{1,13},{2,14},{3,15},{4,0},{5,1},{6,2},{7,3},{8,4},{9,5},{1... | collective-permute-start | bytes 24584 | tf_op jit(solution)/shard_map/ppermute | solution.py:346
  134.2 0.9 collective-permute-start.8
  135.1 0.9 collective-permute-start.7
  135.9 4.9 %collective-permute-done.9 = f32[4,4,128]{2,1,0:T(4,128)S(1)} collective-permute-done((f32[4,4,128]{2,1,0:T(4,128)S(1)}, f32[4,4,128]{2,1,0:T(4,128)S(1)}, u32[]{:S(2)}, u32[]{:S(2)}) %collective-permute-start.9) | collective-permute-done | bytes 8224 | tf_op jit(solution)/shard_map/ppermute | solution.py:346
  140.8 1.5 collective-permute-done.8
  142.3 0.3 collective-permute-done.7
  142.6 2.4 %all-to-all-done.3.recv_ref = bf16[16,512,128]{2,1,0:T(8,128)(2,1)S(1)} async-done(((bf16[16,512,128]{2,1,0:T(8,128)(2,1)}), bf16[16,512,128]{2,1,0:T(8,128)(2,1)S(1)}, u32[]{:S(2)}, u32[]{:S(2)}) %all-to-all-start.3) | async-done | bytes 2097184 | tf_op jit(solution)/shard_map/all_to_all | solution.py:332
  144.9 1.6 %unpack1.1 = (bf16[1,128,4096]{2,1,0:T(8,128)(2,1)}, bf16[1,128,4096]{2,1,0:T(8,128)(2,1)}, bf16[1,128,4096]{2,1,0:T(8,128)(2,1)}, bf16[1,128,4096]{2,1,0:T(8,12...) custom-call(bf16[16,512,128]{2,1,0:T(8,128)(2,1)S(1)} %all-to-all-do, ...), custom_call_target="tpu_custom_call", output_to_operand_aliasing={{0}: (3, {}), {1}: (4, {}), {2}: (5, {}), {3}: (6, {})} | custom-call | bytes 8388608 | tf_op jit(solution)/shard_map/unpack1/pallas_call | solution.py:131
  (19 shorter events, 0.3 us)
Async XLA Ops:
  3.1 7.1 %copy-start.3 = (s32[32,8]{0,1:T(8,128)S(1)}, s32[32,8]{0,1:T(8,128)}, u32[]{:S(2)}) copy-start(s32[32,8]{0,1:T(8,128)} %param.13) | copy-start | bytes 3076
  3.1 37.4 %all-to-all-start = ((bf16[16,512,128]{2,1,0:T(8,128)(2,1)}), bf16[16,512,128]{2,1,0:T(8,128)(2,1)S(1)}, u32[]{:S(2)}, u32[]{:S(2)}) async-start(bf16[16,512,128]{2,1,0:T(8,128)(2,1)} %get-tuple-element.31), calls=%async_computation | async-start | bytes 4194304 | tf_op jit(solution)/shard_map/all_to_all | solution.py:332
  10.2 35.5 %copy-start = (s32[32,8]{1,0:T(8,128)}, s32[32,8]{1,0:T(8,128)S(1)}, u32[]{:S(2)}) copy-start(s32[32,8]{1,0:T(8,128)S(1)} %copy.18.ids_ref) | copy-start | bytes 3076
  10.2 2.5 %copy-start.1 = (f32[32,128]{1,0:T(8,128)S(1)}, f32[32,128]{1,0:T(8,128)}, u32[]{:S(2)}) copy-start(f32[32,128]{1,0:T(8,128)} %param.11) | copy-start | bytes 49156
  10.3 2.5 %copy-start.2 = (f32[32,128]{1,0:T(8,128)S(1)}, f32[32,128]{1,0:T(8,128)}, u32[]{:S(2)}) copy-start(f32[32,128]{1,0:T(8,128)} %param.12) | copy-start | bytes 49156
  40.5 36.0 %all-to-all-start.1 = ((bf16[16,512,128]{2,1,0:T(8,128)(2,1)}), bf16[16,512,128]{2,1,0:T(8,128)(2,1)}, u32[]{:S(2)}, u32[]{:S(2)}) async-start(bf16[16,512,128]{2,1,0:T(8,128)(2,1)} %pack1.1), calls=%async_computation.1 | async-start | bytes 4194304 | tf_op jit(solution)/shard_map/all_to_all | solution.py:332
  76.5 36.6 %all-to-all-start.2 = ((bf16[16,512,128]{2,1,0:T(8,128)(2,1)}), bf16[16,512,128]{2,1,0:T(8,128)(2,1)}, u32[]{:S(2)}, u32[]{:S(2)}) async-start(bf16[16,512,128]{2,1,0:T(8,128)(2,1)} %get-tuple-element.39), calls=%async_computation.2 | async-start | bytes 4194304 | tf_op jit(solution)/shard_map/all_to_all | solution.py:332
  96.6 6.6 %collective-permute-start.1 = (f32[4,128]{1,0:T(4,128)S(1)}, f32[4,128]{1,0:T(4,128)S(1)}, u32[]{:S(2)}, u32[]{:S(2)}) collective-permute-start(f32[4,128]{1,0:T(4,128)S(1)} %get-tuple-element.57), channel_id=1, source_target_pairs={{0,2},{1,3},{2,0},{3,1},{4,6},{5,7},{6,4},{7,5},{8,10},{9,11},{10,... | collective-permute-start | bytes 6152 | tf_op jit(solution)/shard_map/ppermute | solution.py:346
  100.0 7.9 %collective-permute-start = (f32[4,128]{1,0:T(4,128)S(1)}, f32[4,128]{1,0:T(4,128)S(1)}, u32[]{:S(2)}, u32[]{:S(2)}) collective-permute-start(f32[4,128]{1,0:T(4,128)S(1)} %get-tuple-element.57), channel_id=1, source_target_pairs={{0,1},{1,2},{2,3},{3,0},{4,5},{5,6},{6,7},{7,4},{8,9},{9,10},{10,1... | collective-permute-start | bytes 6152 | tf_op jit(solution)/shard_map/ppermute | solution.py:346
  100.5 7.3 %collective-permute-start.2 = (f32[4,128]{1,0:T(4,128)S(1)}, f32[4,128]{1,0:T(4,128)S(1)}, u32[]{:S(2)}, u32[]{:S(2)}) collective-permute-start(f32[4,128]{1,0:T(4,128)S(1)} %get-tuple-element.57), channel_id=1, source_target_pairs={{0,3},{1,0},{2,1},{3,2},{4,7},{5,4},{6,5},{7,6},{8,11},{9,8},{10,9... | collective-permute-start | bytes 6152 | tf_op jit(solution)/shard_map/ppermute | solution.py:346
  113.1 31.8 %all-to-all-start.3 = ((bf16[16,512,128]{2,1,0:T(8,128)(2,1)}), bf16[16,512,128]{2,1,0:T(8,128)(2,1)S(1)}, u32[]{:S(2)}, u32[]{:S(2)}) async-start(bf16[16,512,128]{2,1,0:T(8,128)(2,1)} %get-tuple-element.40), calls=%async_computation.3 | async-start | bytes 4194304 | tf_op jit(solution)/shard_map/all_to_all | solution.py:332
  116.8 1.3 collective-permute-start.3
  118.1 3.7 %collective-permute-start.4 = (f32[4,4,128]{2,1,0:T(4,128)S(1)}, f32[4,4,128]{2,1,0:T(4,128)S(1)}, u32[]{:S(2)}, u32[]{:S(2)}) collective-permute-start(f32[4,4,128]{2,1,0:T(4,128)S(1)} %add.28), channel_id=1, source_target_pairs={{0,32},{16,48},{32,0},{48,16},{64,96},{80,112},{96,64},{112,80},{1... | collective-permute-start | bytes 24584 | tf_op jit(solution)/shard_map/ppermute | solution.py:336
  121.8 4.5 %collective-permute-start.5 = (f32[4,4,128]{2,1,0:T(4,128)S(1)}, f32[4,4,128]{2,1,0:T(4,128)S(1)}, u32[]{:S(2)}, u32[]{:S(2)}) collective-permute-start(f32[4,4,128]{2,1,0:T(4,128)S(1)} %add.29), channel_id=1, source_target_pairs={{0,64},{16,80},{32,96},{48,112},{64,0},{80,16},{96,32},{112,48},{1... | collective-permute-start | bytes 24584 | tf_op jit(solution)/shard_map/ppermute | solution.py:336
  126.3 4.9 %collective-permute-start.6 = (f32[4,4,128]{2,1,0:T(4,128)S(1)}, f32[4,4,128]{2,1,0:T(4,128)S(1)}, u32[]{:S(2)}, u32[]{:S(2)}) collective-permute-start(f32[4,4,128]{2,1,0:T(4,128)S(1)} %add.30), channel_id=1, source_target_pairs={{0,224},{16,240},{32,192},{48,208},{64,160},{80,176},{96,128},{112... | collective-permute-start | bytes 24584 | tf_op jit(solution)/shard_map/ppermute | solution.py:336
  131.2 9.6 %collective-permute-start.9 = (f32[4,4,128]{2,1,0:T(4,128)S(1)}, f32[4,4,128]{2,1,0:T(4,128)S(1)}, u32[]{:S(2)}, u32[]{:S(2)}) collective-permute-start(f32[4,4,128]{2,1,0:T(4,128)S(1)} %add.31), channel_id=1, source_target_pairs={{0,12},{1,13},{2,14},{3,15},{4,0},{5,1},{6,2},{7,3},{8,4},{9,5},{1... | collective-permute-start | bytes 24584 | tf_op jit(solution)/shard_map/ppermute | solution.py:346
  134.2 8.0 %collective-permute-start.8 = (f32[4,4,128]{2,1,0:T(4,128)S(1)}, f32[4,4,128]{2,1,0:T(4,128)S(1)}, u32[]{:S(2)}, u32[]{:S(2)}) collective-permute-start(f32[4,4,128]{2,1,0:T(4,128)S(1)} %add.31), channel_id=1, source_target_pairs={{0,8},{1,9},{2,10},{3,11},{4,12},{5,13},{6,14},{7,15},{8,0},{9,1},... | collective-permute-start | bytes 24584 | tf_op jit(solution)/shard_map/ppermute | solution.py:346
  135.1 7.5 %collective-permute-start.7 = (f32[4,4,128]{2,1,0:T(4,128)S(1)}, f32[4,4,128]{2,1,0:T(4,128)S(1)}, u32[]{:S(2)}, u32[]{:S(2)}) collective-permute-start(f32[4,4,128]{2,1,0:T(4,128)S(1)} %add.31), channel_id=1, source_target_pairs={{0,4},{1,5},{2,6},{3,7},{4,8},{5,9},{6,10},{7,11},{8,12},{9,13},{1... | collective-permute-start | bytes 24584 | tf_op jit(solution)/shard_map/ppermute | solution.py:346

commit v9 on v8

--- a/solution.py
+++ b/solution.py
@@ -354,7 +354,7 @@
     gains = [
         lax.dynamic_index_in_dim(both, c * SEQ + s, 0, keepdims=False) for c in range(CHUNKS)
     ]
-    core = (lax.axis_index("dp") % 2).reshape(1)
+    core = ((lax.axis_index("dp") + 1) % 2).reshape(1)
     sent0, sent1 = pack(pack_first_kernel, 2, core, *arrays)
     in0 = swap(sent0, "seq")
     (sent1,) = pack(pack_second_kernel, 1, core, *arrays, sent1)

time: 147 us -> 139 us (0.946)
  waiting for transfers between devices: 73.9 us -> 67.4 us
  starting transfers between devices: 36.5 us -> 34.3 us
    all_to_all x4, waiting for transfers between devices: 53.8 us -> 46.9 us  [swap(): return lax.all_to_all(x, axis, split_axis=0, concat_axis=0, tiled=True)]
    all_to_all x4, starting transfers between devices: 22.4 us -> 20.2 us  [swap(): return lax.all_to_all(x, axis, split_axis=0, concat_axis=0, tiled=True)]
  transfers between devices with their start and end apart: 14 -> 14, of which waited for: 12 -> 11; matrix products, arithmetic and copies ran while one was open for 1% -> 1% of each run, Pallas kernels for 20% -> 20%
where the time goes in v9:
time: 139 us; the launch traced here: 138 us
  waiting for transfers between devices  67.4 us (48%)
  starting transfers between devices  34.3 us (25%)
  Pallas kernels  34 us (24%)
    all_to_all x4, waiting for transfers between devices, swap(): return lax.all_to_all(x, axis, split_axis=0, concat_axis=0, tiled=True)  46.9 us
    pallas_call x2, Pallas kernels, attend(): pl.pallas_call(functools.partial(attend_kernel, group=group), out_shape=(...  24.7 us
    all_to_all x4, starting transfers between devices, swap(): return lax.all_to_all(x, axis, split_axis=0, concat_axis=0, tiled=True)  20.2 us
    ppermute x6, waiting for transfers between devices, ring_of(): held.append(lax.ppermute(x, 'seq', turn))  11.7 us
    ppermute x6, starting transfers between devices, ring_of(): held.append(lax.ppermute(x, 'seq', turn))  11.4 us
    ppermute x4, waiting for transfers between devices, far(): lax.ppermute(x, axis, [(i, i ^ step) for i in range(lax.axis_size(axis))])  8.81 us
    pallas_call x2, Pallas kernels, pack(): pl.pallas_call(kernel, out_shape=(pltpu.HBM((SEQ, 4 * TOK, HEAD), jnp.bfl...  4.9 us
    pallas_call x1, Pallas kernels, unpack(): pl.pallas_call(unpack_kernel, grid=(steps,), out_shape=(jax.ShapeDtypeStr...  2.81 us
  transfers between devices with their start and end apart: 14, of which 11 were waited for; matrix products, arithmetic and copies ran while one was open for 1% of the time, Pallas kernels for 20%

profile of v9, /device:TPU:128, one launch (start us, length us, event | category | flops | bytes accessed | tf_op | source)
XLA Modules:
  0.0 138.5 jit_solution(14079741558013322562)
XLA Ops:
  0.6 4.8 %pack0.1 = (bf16[16,512,128]{2,1,0:T(8,128)(2,1)}, bf16[16,512,128]{2,1,0:T(8,128)(2,1)}) custom-call(s32[1]{0:T(128)} %bitcast.3.core_ref, bf16[1,128,4096]{2,1,0:T(8,128)(2,1)} %q_ref.3, bf16[1,128,4096]{2,1,0:T(8,128)(2,1)} %k_ref.3, bf16[1,128,4096]{2,1,0:T(8,128)(2,1)} %v_ref.3, bf16[1,128,4096]{2,1,0:T(8,128)(2,1)} %g_ref.3), custom_call_target="tpu_custom_call" | custom-call | bytes 8388608 | tf_op jit(solution)/shard_map/pack0/pallas_call | solution.py:73
  5.5 7.0 %all-to-all-start = ((bf16[16,512,128]{2,1,0:T(8,128)(2,1)}), bf16[16,512,128]{2,1,0:T(8,128)(2,1)S(1)}, u32[]{:S(2)}, u32[]{:S(2)}) async-start(bf16[16,512,128]{2,1,0:T(8,128)(2,1)} %get-tuple-element.31), calls=%async_computation | async-start | bytes 4194304 | tf_op jit(solution)/shard_map/all_to_all | solution.py:332
  12.7 0.6 copy-done.1
  13.4 0.6 fusion.1
  13.9 26.3 %all-to-all-done.recv_ref = bf16[16,512,128]{2,1,0:T(8,128)(2,1)S(1)} async-done(((bf16[16,512,128]{2,1,0:T(8,128)(2,1)}), bf16[16,512,128]{2,1,0:T(8,128)(2,1)S(1)}, u32[]{:S(2)}, u32[]{:S(2)}) %all-to-all-start) | async-done | bytes 2097184 | tf_op jit(solution)/shard_map/all_to_all | solution.py:332
  40.2 4.4 %all-to-all-start.1 = ((bf16[16,512,128]{2,1,0:T(8,128)(2,1)}), bf16[16,512,128]{2,1,0:T(8,128)(2,1)}, u32[]{:S(2)}, u32[]{:S(2)}) async-start(bf16[16,512,128]{2,1,0:T(8,128)(2,1)} %pack1.1), calls=%async_computation.1 | async-start | bytes 4194304 | tf_op jit(solution)/shard_map/all_to_all | solution.py:332
  44.7 11.7 %attend0.1 = (bf16[16,512,128]{2,1,0:T(8,128)(2,1)}, f32[2,128]{1,0:T(2,128)S(1)}) custom-call(s32[32,8]{1,0:T(8,128)S(1)} %copy.18.ids_ref, f32[2,128]{1,0:T(2,128)S(1)} %bitcast.17, bf16[16,512,128]{2,1,0:T(8,128)(2,1)S(1)} %all-to-all-done.recv_ref), custom_call_target="tpu_custom_call" | custom-call | flops 24999999488 | bytes 4194304 | tf_op jit(solution)/shard_map/attend0/pallas_call | solution.py:295
  56.4 16.1 %all-to-all-done.1.recv_ref = bf16[16,512,128]{2,1,0:T(8,128)(2,1)} async-done(((bf16[16,512,128]{2,1,0:T(8,128)(2,1)}), bf16[16,512,128]{2,1,0:T(8,128)(2,1)}, u32[]{:S(2)}, u32[]{:S(2)}) %all-to-all-start.1) | async-done | bytes 2097184 | tf_op jit(solution)/shard_map/all_to_all | solution.py:332
  72.4 4.4 %all-to-all-start.2 = ((bf16[16,512,128]{2,1,0:T(8,128)(2,1)}), bf16[16,512,128]{2,1,0:T(8,128)(2,1)}, u32[]{:S(2)}, u32[]{:S(2)}) async-start(bf16[16,512,128]{2,1,0:T(8,128)(2,1)} %get-tuple-element.39), calls=%async_computation.2 | async-start | bytes 4194304 | tf_op jit(solution)/shard_map/all_to_all | solution.py:332
  76.9 13.0 %attend1.1 = (bf16[16,512,128]{2,1,0:T(8,128)(2,1)}, f32[2,128]{1,0:T(2,128)}) custom-call(s32[32,8]{1,0:T(8,128)} %copy-done, f32[2,128]{1,0:T(2,128)} %bitcast.27, bf16[16,512,128]{2,1,0:T(8,128)(2,1)} %all-to-all-done.1.recv_ref), custom_call_target="tpu_custom_call" | custom-call | flops 24999999488 | bytes 4194304 | tf_op jit(solution)/shard_map/attend1/pallas_call | solution.py:295
  89.9 0.7 fusion.2
  90.6 3.3 %collective-permute-start.1 = (f32[4,128]{1,0:T(4,128)S(1)}, f32[4,128]{1,0:T(4,128)S(1)}, u32[]{:S(2)}, u32[]{:S(2)}) collective-permute-start(f32[4,128]{1,0:T(4,128)S(1)} %get-tuple-element.57), channel_id=1, source_target_pairs={{0,2},{1,3},{2,0},{3,1},{4,6},{5,7},{6,4},{7,5},{8,10},{9,11},{10,... | collective-permute-start | bytes 6152 | tf_op jit(solution)/shard_map/ppermute | solution.py:346
  94.0 0.6 collective-permute-start
  94.5 2.7 %collective-permute-start.2 = (f32[4,128]{1,0:T(4,128)S(1)}, f32[4,128]{1,0:T(4,128)S(1)}, u32[]{:S(2)}, u32[]{:S(2)}) collective-permute-start(f32[4,128]{1,0:T(4,128)S(1)} %get-tuple-element.57), channel_id=1, source_target_pairs={{0,3},{1,0},{2,1},{3,2},{4,7},{5,4},{6,5},{7,6},{8,11},{9,8},{10,9... | collective-permute-start | bytes 6152 | tf_op jit(solution)/shard_map/ppermute | solution.py:346
  97.2 4.8 %collective-permute-done = f32[4,128]{1,0:T(4,128)S(1)} collective-permute-done((f32[4,128]{1,0:T(4,128)S(1)}, f32[4,128]{1,0:T(4,128)S(1)}, u32[]{:S(2)}, u32[]{:S(2)}) %collective-permute-start) | collective-permute-done | bytes 2080 | tf_op jit(solution)/shard_map/ppermute | solution.py:346
  102.0 2.6 %all-to-all-done.2.recv_ref = bf16[16,512,128]{2,1,0:T(8,128)(2,1)} async-done(((bf16[16,512,128]{2,1,0:T(8,128)(2,1)}), bf16[16,512,128]{2,1,0:T(8,128)(2,1)}, u32[]{:S(2)}, u32[]{:S(2)}) %all-to-all-start.2) | async-done | bytes 2097184 | tf_op jit(solution)/shard_map/all_to_all | solution.py:332
  104.6 4.3 %all-to-all-start.3 = ((bf16[16,512,128]{2,1,0:T(8,128)(2,1)}), bf16[16,512,128]{2,1,0:T(8,128)(2,1)S(1)}, u32[]{:S(2)}, u32[]{:S(2)}) async-start(bf16[16,512,128]{2,1,0:T(8,128)(2,1)} %get-tuple-element.40), calls=%async_computation.3 | async-start | bytes 4194304 | tf_op jit(solution)/shard_map/all_to_all | solution.py:332
  109.0 1.2 collective-permute-done.3
  110.2 1.0 collective-permute-start.4
  111.2 2.6 %collective-permute-done.4 = f32[4,4,128]{2,1,0:T(4,128)S(1)} collective-permute-done((f32[4,4,128]{2,1,0:T(4,128)S(1)}, f32[4,4,128]{2,1,0:T(4,128)S(1)}, u32[]{:S(2)}, u32[]{:S(2)}) %collective-permute-start.4) | collective-permute-done | bytes 8224 | tf_op jit(solution)/shard_map/ppermute | solution.py:336
  113.8 1.5 %collective-permute-start.5 = (f32[4,4,128]{2,1,0:T(4,128)S(1)}, f32[4,4,128]{2,1,0:T(4,128)S(1)}, u32[]{:S(2)}, u32[]{:S(2)}) collective-permute-start(f32[4,4,128]{2,1,0:T(4,128)S(1)} %add.33), channel_id=1, source_target_pairs={{0,64},{16,80},{32,96},{48,112},{64,0},{80,16},{96,32},{112,48},{1... | collective-permute-start | bytes 24584 | tf_op jit(solution)/shard_map/ppermute | solution.py:336
  115.3 3.1 %collective-permute-done.5 = f32[4,4,128]{2,1,0:T(4,128)S(1)} collective-permute-done((f32[4,4,128]{2,1,0:T(4,128)S(1)}, f32[4,4,128]{2,1,0:T(4,128)S(1)}, u32[]{:S(2)}, u32[]{:S(2)}) %collective-permute-start.5) | collective-permute-done | bytes 8224 | tf_op jit(solution)/shard_map/ppermute | solution.py:336
  118.4 0.1 collective-permute-start.6
  118.5 2.8 %unpack0.1 = (bf16[1,128,4096]{2,1,0:T(8,128)(2,1)}, bf16[1,128,4096]{2,1,0:T(8,128)(2,1)}, bf16[1,128,4096]{2,1,0:T(8,128)(2,1)}, bf16[1,128,4096]{2,1,0:T(8,128)(2,1)}) custom-call(bf16[16,512,128]{2,1,0:T(8,128)(2,1)} %all-to-all-done.2.recv_ref), custom_call_target="tpu_custom_call" | custom-call | bytes 8388608 | tf_op jit(solution)/shard_map/unpack0/pallas_call | solution.py:117
  121.3 1.9 %collective-permute-done.6 = f32[4,4,128]{2,1,0:T(4,128)S(1)} collective-permute-done((f32[4,4,128]{2,1,0:T(4,128)S(1)}, f32[4,4,128]{2,1,0:T(4,128)S(1)}, u32[]{:S(2)}, u32[]{:S(2)}) %collective-permute-start.6) | collective-permute-done | bytes 8224 | tf_op jit(solution)/shard_map/ppermute | solution.py:336
  123.3 3.1 %collective-permute-start.9 = (f32[4,4,128]{2,1,0:T(4,128)S(1)}, f32[4,4,128]{2,1,0:T(4,128)S(1)}, u32[]{:S(2)}, u32[]{:S(2)}) collective-permute-start(f32[4,4,128]{2,1,0:T(4,128)S(1)} %add.35), channel_id=1, source_target_pairs={{0,12},{1,13},{2,14},{3,15},{4,0},{5,1},{6,2},{7,3},{8,4},{9,5},{1... | collective-permute-start | bytes 24584 | tf_op jit(solution)/shard_map/ppermute | solution.py:346
  126.3 0.9 collective-permute-start.8
  127.2 0.9 collective-permute-start.7
  128.0 5.6 %collective-permute-done.9 = f32[4,4,128]{2,1,0:T(4,128)S(1)} collective-permute-done((f32[4,4,128]{2,1,0:T(4,128)S(1)}, f32[4,4,128]{2,1,0:T(4,128)S(1)}, u32[]{:S(2)}, u32[]{:S(2)}) %collective-permute-start.9) | collective-permute-done | bytes 8224 | tf_op jit(solution)/shard_map/ppermute | solution.py:346
  133.6 1.3 collective-permute-done.8
  135.0 1.9 %all-to-all-done.3.recv_ref = bf16[16,512,128]{2,1,0:T(8,128)(2,1)S(1)} async-done(((bf16[16,512,128]{2,1,0:T(8,128)(2,1)}), bf16[16,512,128]{2,1,0:T(8,128)(2,1)S(1)}, u32[]{:S(2)}, u32[]{:S(2)}) %all-to-all-start.3) | async-done | bytes 2097184 | tf_op jit(solution)/shard_map/all_to_all | solution.py:332
  136.9 1.6 %unpack1.1 = (bf16[1,128,4096]{2,1,0:T(8,128)(2,1)}, bf16[1,128,4096]{2,1,0:T(8,128)(2,1)}, bf16[1,128,4096]{2,1,0:T(8,128)(2,1)}, bf16[1,128,4096]{2,1,0:T(8,12...) custom-call(bf16[16,512,128]{2,1,0:T(8,128)(2,1)S(1)} %all-to-all-do, ...), custom_call_target="tpu_custom_call", output_to_operand_aliasing={{0}: (3, {}), {1}: (4, {}), {2}: (5, {}), {3}: (6, {})} | custom-call | bytes 8388608 | tf_op jit(solution)/shard_map/unpack1/pallas_call | solution.py:131
  (19 shorter events, 0.3 us)
Async XLA Ops:
  5.5 7.1 %copy-start.3 = (s32[32,8]{0,1:T(8,128)S(1)}, s32[32,8]{0,1:T(8,128)}, u32[]{:S(2)}) copy-start(s32[32,8]{0,1:T(8,128)} %param.13) | copy-start | bytes 3076
  5.5 34.8 %all-to-all-start = ((bf16[16,512,128]{2,1,0:T(8,128)(2,1)}), bf16[16,512,128]{2,1,0:T(8,128)(2,1)S(1)}, u32[]{:S(2)}, u32[]{:S(2)}) async-start(bf16[16,512,128]{2,1,0:T(8,128)(2,1)} %get-tuple-element.31), calls=%async_computation | async-start | bytes 4194304 | tf_op jit(solution)/shard_map/all_to_all | solution.py:332
  12.6 32.1 %copy-start = (s32[32,8]{1,0:T(8,128)}, s32[32,8]{1,0:T(8,128)S(1)}, u32[]{:S(2)}) copy-start(s32[32,8]{1,0:T(8,128)S(1)} %copy.18.ids_ref) | copy-start | bytes 3076
  12.6 0.7 copy-start.1
  12.6 0.7 copy-start.2
  40.2 32.2 %all-to-all-start.1 = ((bf16[16,512,128]{2,1,0:T(8,128)(2,1)}), bf16[16,512,128]{2,1,0:T(8,128)(2,1)}, u32[]{:S(2)}, u32[]{:S(2)}) async-start(bf16[16,512,128]{2,1,0:T(8,128)(2,1)} %pack1.1), calls=%async_computation.1 | async-start | bytes 4194304 | tf_op jit(solution)/shard_map/all_to_all | solution.py:332
  72.4 32.2 %all-to-all-start.2 = ((bf16[16,512,128]{2,1,0:T(8,128)(2,1)}), bf16[16,512,128]{2,1,0:T(8,128)(2,1)}, u32[]{:S(2)}, u32[]{:S(2)}) async-start(bf16[16,512,128]{2,1,0:T(8,128)(2,1)} %get-tuple-element.39), calls=%async_computation.2 | async-start | bytes 4194304 | tf_op jit(solution)/shard_map/all_to_all | solution.py:332
  90.6 6.6 %collective-permute-start.1 = (f32[4,128]{1,0:T(4,128)S(1)}, f32[4,128]{1,0:T(4,128)S(1)}, u32[]{:S(2)}, u32[]{:S(2)}) collective-permute-start(f32[4,128]{1,0:T(4,128)S(1)} %get-tuple-element.57), channel_id=1, source_target_pairs={{0,2},{1,3},{2,0},{3,1},{4,6},{5,7},{6,4},{7,5},{8,10},{9,11},{10,... | collective-permute-start | bytes 6152 | tf_op jit(solution)/shard_map/ppermute | solution.py:346
  94.0 8.0 %collective-permute-start = (f32[4,128]{1,0:T(4,128)S(1)}, f32[4,128]{1,0:T(4,128)S(1)}, u32[]{:S(2)}, u32[]{:S(2)}) collective-permute-start(f32[4,128]{1,0:T(4,128)S(1)} %get-tuple-element.57), channel_id=1, source_target_pairs={{0,1},{1,2},{2,3},{3,0},{4,5},{5,6},{6,7},{7,4},{8,9},{9,10},{10,1... | collective-permute-start | bytes 6152 | tf_op jit(solution)/shard_map/ppermute | solution.py:346
  94.5 7.5 %collective-permute-start.2 = (f32[4,128]{1,0:T(4,128)S(1)}, f32[4,128]{1,0:T(4,128)S(1)}, u32[]{:S(2)}, u32[]{:S(2)}) collective-permute-start(f32[4,128]{1,0:T(4,128)S(1)} %get-tuple-element.57), channel_id=1, source_target_pairs={{0,3},{1,0},{2,1},{3,2},{4,7},{5,4},{6,5},{7,6},{8,11},{9,8},{10,9... | collective-permute-start | bytes 6152 | tf_op jit(solution)/shard_map/ppermute | solution.py:346
  104.6 32.3 %all-to-all-start.3 = ((bf16[16,512,128]{2,1,0:T(8,128)(2,1)}), bf16[16,512,128]{2,1,0:T(8,128)(2,1)S(1)}, u32[]{:S(2)}, u32[]{:S(2)}) async-start(bf16[16,512,128]{2,1,0:T(8,128)(2,1)} %get-tuple-element.40), calls=%async_computation.3 | async-start | bytes 4194304 | tf_op jit(solution)/shard_map/all_to_all | solution.py:332
  108.9 1.3 collective-permute-start.3
  110.2 3.7 %collective-permute-start.4 = (f32[4,4,128]{2,1,0:T(4,128)S(1)}, f32[4,4,128]{2,1,0:T(4,128)S(1)}, u32[]{:S(2)}, u32[]{:S(2)}) collective-permute-start(f32[4,4,128]{2,1,0:T(4,128)S(1)} %add.32), channel_id=1, source_target_pairs={{0,32},{16,48},{32,0},{48,16},{64,96},{80,112},{96,64},{112,80},{1... | collective-permute-start | bytes 24584 | tf_op jit(solution)/shard_map/ppermute | solution.py:336
  113.8 4.5 %collective-permute-start.5 = (f32[4,4,128]{2,1,0:T(4,128)S(1)}, f32[4,4,128]{2,1,0:T(4,128)S(1)}, u32[]{:S(2)}, u32[]{:S(2)}) collective-permute-start(f32[4,4,128]{2,1,0:T(4,128)S(1)} %add.33), channel_id=1, source_target_pairs={{0,64},{16,80},{32,96},{48,112},{64,0},{80,16},{96,32},{112,48},{1... | collective-permute-start | bytes 24584 | tf_op jit(solution)/shard_map/ppermute | solution.py:336
  118.4 4.9 %collective-permute-start.6 = (f32[4,4,128]{2,1,0:T(4,128)S(1)}, f32[4,4,128]{2,1,0:T(4,128)S(1)}, u32[]{:S(2)}, u32[]{:S(2)}) collective-permute-start(f32[4,4,128]{2,1,0:T(4,128)S(1)} %add.34), channel_id=1, source_target_pairs={{0,224},{16,240},{32,192},{48,208},{64,160},{80,176},{96,128},{112... | collective-permute-start | bytes 24584 | tf_op jit(solution)/shard_map/ppermute | solution.py:336
  123.3 10.4 %collective-permute-start.9 = (f32[4,4,128]{2,1,0:T(4,128)S(1)}, f32[4,4,128]{2,1,0:T(4,128)S(1)}, u32[]{:S(2)}, u32[]{:S(2)}) collective-permute-start(f32[4,4,128]{2,1,0:T(4,128)S(1)} %add.35), channel_id=1, source_target_pairs={{0,12},{1,13},{2,14},{3,15},{4,0},{5,1},{6,2},{7,3},{8,4},{9,5},{1... | collective-permute-start | bytes 24584 | tf_op jit(solution)/shard_map/ppermute | solution.py:346
  126.3 8.6 %collective-permute-start.8 = (f32[4,4,128]{2,1,0:T(4,128)S(1)}, f32[4,4,128]{2,1,0:T(4,128)S(1)}, u32[]{:S(2)}, u32[]{:S(2)}) collective-permute-start(f32[4,4,128]{2,1,0:T(4,128)S(1)} %add.35), channel_id=1, source_target_pairs={{0,8},{1,9},{2,10},{3,11},{4,12},{5,13},{6,14},{7,15},{8,0},{9,1},... | collective-permute-start | bytes 24584 | tf_op jit(solution)/shard_map/ppermute | solution.py:346
  127.2 7.8 %collective-permute-start.7 = (f32[4,4,128]{2,1,0:T(4,128)S(1)}, f32[4,4,128]{2,1,0:T(4,128)S(1)}, u32[]{:S(2)}, u32[]{:S(2)}) collective-permute-start(f32[4,4,128]{2,1,0:T(4,128)S(1)} %add.35), channel_id=1, source_target_pairs={{0,4},{1,5},{2,6},{3,7},{4,8},{5,9},{6,10},{7,11},{8,12},{9,13},{1... | collective-permute-start | bytes 24584 | tf_op jit(solution)/shard_map/ppermute | solution.py:346
